TPU v7x, 256 devices: a whole 4x4x8 slice. The times are simulated.
256 devices in a mesh: batch: 32 (over z, y_hi, core), feat: 8 (over y_lo, x).
Axes of the slice: x: 4, y: 4 (y_hi: 2, y_lo: 2; y = y_hi * 2 + y_lo), z: 8, core: 2. Of those that a mesh axis runs over, the one named last changes fastest.
Arguments:
- view_a: bfloat16 [4096, 8192], P('batch', 'feat'), may hold values from -256 to 256
- view_b: bfloat16 [4096, 8192], P('batch', 'feat'), may hold values from -256 to 256
Outputs:
- grad_a: bfloat16 [4096, 8192], P('batch', 'feat')
- grad_b: bfloat16 [4096, 8192], P('batch', 'feat')
- loss: float32 [], replicated
All inputs are finite; a program needn't handle non-finite values.
Results may differ from a plain program's by a relative error of at most 0.006.
Values may be sent and summed in bfloat16 or wider, within the bound.
No kernel may reach another device: no remote copies, remote signals or barrier semaphores. Data moves between devices by JAX's collectives and lax.ppermute only.
A program may use at most 128 MiB of HBM per device.

v0:
```python
import jax
import jax.numpy as jnp
from jax import lax
from jax.sharding import PartitionSpec as P

WIDTH = 8192


redund_weight = 0.0051
eps_var = 1e-05


def standardize(values, total_sum, square_sum, count):
    mean_value = total_sum / count
    var_value = square_sum / count - mean_value * mean_value
    rstd = lax.rsqrt(var_value + eps_var)
    return (((values.astype(jnp.float32) - mean_value) * rstd).astype(jnp.bfloat16), rstd)


def outer_rows(left, right):
    return lax.dot_general(
        left, right, (((1,), (1,)), ((), ())), preferred_element_type=jnp.float32
    )


def column_moments(values):
    floats = values.astype(jnp.float32)
    return (jnp.sum(floats, 0), jnp.sum(floats * floats, 0))


def shards(view_a, view_b):
    row_count = view_a.shape[0]
    batch_total = row_count * lax.axis_size("batch")
    sum_a, square_a = column_moments(view_a)
    sum_b, square_b = column_moments(view_b)
    moment_sums = lax.psum((sum_a, square_a, sum_b, square_b), "batch")
    norm_a, rstd_a = standardize(view_a, moment_sums[0], moment_sums[1], batch_total)
    norm_b, rstd_b = standardize(view_b, moment_sums[2], moment_sums[3], batch_total)
    all_a, all_b = (
        lax.all_gather(norm_a, "batch", axis=0, tiled=True),
        lax.all_gather(norm_b, "batch", axis=0, tiled=True),
    )
    cross_sum = lax.psum(
        jnp.sum(norm_a.astype(jnp.float32) * norm_b.astype(jnp.float32), 0), "batch"
    )
    corr_diag = cross_sum / batch_total
    diag_part = jnp.sum((1.0 - corr_diag) ** 2) - redund_weight * jnp.sum(corr_diag * corr_diag)
    gram_part_a = outer_rows(norm_a, all_a)
    gram_part_b = outer_rows(norm_b, all_b)
    gram_a, gram_b, diag_loss = lax.psum((gram_part_a, gram_part_b, diag_part), "feat")
    frob_rows = jnp.sum(gram_a * gram_b)
    low_a = gram_a.astype(jnp.bfloat16)
    low_b = gram_b.astype(jnp.bfloat16)
    diag_grad = -2.0 * (1.0 - corr_diag) - 2.0 * redund_weight * corr_diag
    coupling = 2.0 * redund_weight / (batch_total * batch_total)
    norm_af = norm_a.astype(jnp.float32)
    norm_bf = norm_b.astype(jnp.float32)
    grad_norm_a = diag_grad * norm_bf / batch_total + coupling * jnp.dot(
        low_b, all_a, preferred_element_type=jnp.float32
    )
    grad_norm_b = diag_grad * norm_af / batch_total + coupling * jnp.dot(
        low_a, all_b, preferred_element_type=jnp.float32
    )
    back_sums = lax.psum(
        (
            jnp.sum(grad_norm_a, 0),
            jnp.sum(grad_norm_a * norm_af, 0),
            jnp.sum(grad_norm_b, 0),
            jnp.sum(grad_norm_b * norm_bf, 0),
            frob_rows,
        ),
        "batch",
    )
    scale = batch_total * batch_total / (redund_weight * WIDTH)
    grad_a = (
        scale
        * rstd_a
        * (grad_norm_a - back_sums[0] / batch_total - norm_af * (back_sums[1] / batch_total))
    ).astype(jnp.bfloat16)
    grad_b = (
        scale
        * rstd_b
        * (grad_norm_b - back_sums[2] / batch_total - norm_bf * (back_sums[3] / batch_total))
    ).astype(jnp.bfloat16)
    loss = diag_loss + redund_weight * back_sums[4] / (batch_total * batch_total)
    return (grad_a, grad_b, loss)


def solution(mesh):
    return jax.shard_map(
        shards,
        mesh=mesh,
        in_specs=(P("batch", "feat"), P("batch", "feat")),
        out_specs=(P("batch", "feat"), P("batch", "feat"), P()),
        check_vma=False,
    )
```

profile of v0, /device:TPU:1, one launch (start us, length us, event | category | flops | bytes accessed | tf_op | source)
XLA Modules:
  0.0 632.8 jit_solution(4704090494640249074)
XLA Ops:
  7.2 0.0 all-gather.5.cloned.1.call-start
  7.2 1.0 convert_reduce_fusion.1
  8.2 1.0 convert_reduce_fusion
  9.3 132.0 %all-reduce.1 = (f32[1024]{0:T(1024)S(1)}, f32[1024]{0:T(1024)S(1)}, f32[1024]{0:T(1024)S(1)}, f32[1024]{0:T(1024)S(1)}) all-reduce(f32[1024]{0:T(1024)S(1)} %get-tuple-element.10, f32[1024]{0:T(1024)S(1)} %get-tuple-element.9, f32[1024]{0:T(1024)S(1)} %get-tuple-element.8, ...), channel_id=1, replica_groups=mesh['batch'=32,'feat'=8] {'batch'}, use_global_device_ids=true, to_apply=%region_1.0 | all-reduce | flops 4096 | bytes 32768 | tf_op jit(solution)/shard_map/psum | solution.py:36
  141.3 2.0 fusion.15
  143.2 0.0 copy-start.2
  143.2 0.0 all-gather.5.cloned.1.call-update
  143.3 0.0 all-gather.3.cloned.1.call-start
  143.3 0.7 all-gather.3.cloned.1.call-update
  144.0 0.0 all-reduce.5.cloned.1.call-start
  144.1 101.2 %all-gather.5.cloned.1.call-done = bf16[4096,1024]{1,0:T(8,128)(2,1)} async-done(((bf16[128,1024]{1,0:T(8,128)(2,1)}), bf16[4096,1024]{1,0:T(8,128)(2,1)}) %all-gather.5.cloned.1.call-update) | async-done | bytes 8388624 | tf_op jit(solution)/shard_map/all_gather | solution.py:40
  245.3 7.7 %fusion.26 = f32[128,4096]{1,0:T(8,128)} fusion(bf16[128,1024]{1,0:T(8,128)(2,1)} %get-tuple-element.30, bf16[4096,1024]{1,0:T(8,128)(2,1)} %all-gather.5.cloned.1.call-done), kind=kOutput, calls=%fused_computation.53 | convolution fusion | flops 1073741824 | bytes 10747904 | tf_op jit(solution)/shard_map/dot_general | solution.py:21
  253.0 0.0 copy-start.1
  253.0 93.6 %all-gather.3.cloned.1.call-done = bf16[4096,1024]{1,0:T(8,128)(2,1)} async-done(((bf16[128,1024]{1,0:T(8,128)(2,1)}), bf16[4096,1024]{1,0:T(8,128)(2,1)}) %all-gather.3.cloned.1.call-update) | async-done | bytes 8388624 | tf_op jit(solution)/shard_map/all_gather | solution.py:41
  346.6 0.0 copy-done.2
  346.6 7.6 %fusion.25 = f32[128,4096]{1,0:T(8,128)} fusion(bf16[128,1024]{1,0:T(8,128)(2,1)S(1)} %copy-done.2, bf16[4096,1024]{1,0:T(8,128)(2,1)} %all-gather.3.cloned.1.call-done), kind=kOutput, calls=%fused_computation.52 | convolution fusion | flops 1073741824 | bytes 10747904 | tf_op jit(solution)/shard_map/dot_general | solution.py:21
  354.2 0.0 all-reduce.5.cloned.1.call-update
  354.2 111.4 %psum.95 = f32[1024]{0:T(1024)S(1)} all-reduce(f32[1024]{0:T(1024)S(1)} %get-tuple-element.28), channel_id=1, replica_groups=mesh['batch'=32,'feat'=8] {'batch'}, use_global_device_ids=true, to_apply=%region_9.0 | all-reduce | flops 1024 | bytes 8192 | tf_op jit(solution)/shard_map/psum | solution.py:43
  465.6 0.6 multiply_reduce_fusion.1
  467.5 15.3 %psum.102 = f32[]{:T(128)} all-reduce(f32[]{:T(128)S(6)} %sub.68), channel_id=1, replica_groups=mesh['batch'=32,'feat'=8] {'feat'}, use_global_device_ids=true, to_apply=%region_22.0 | all-reduce | flops 1 | bytes 8 | tf_op jit(solution)/shard_map/psum | solution.py:50
  482.8 0.0 all-reduce.5.cloned.1.call-done
  482.8 0.0 slice-start
  482.8 3.5 multiply_reduce_fusion
  486.3 0.0 copy-done.1
  486.3 0.0 slice-start.1
  486.3 0.0 copy-start
  486.3 5.6 fusion.21
  491.9 0.0 slice-done
  491.9 0.0 slice-done.1
  491.9 0.3 copy-done
  492.2 1.5 fusion.22
  493.7 128.5 %all-reduce = (f32[1024]{0:T(1024)S(1)}, f32[1024]{0:T(1024)S(1)}, f32[1024]{0:T(1024)S(1)}, f32[1024]{0:T(1024)S(1)}, f32[]{:T(128)}) all-reduce(f32[1024]{0:T(1024)S(1)} %get-tuple-element.6, f32[1024]{0:T(1024)S(1)} %get-tuple-element.5, f32[1024]{0:T(1024)S(1)} %get-tuple-element.4, ...), channel_id=1, replica_groups=mesh['batch'=32,'feat'=8] {'batch'}, use_global_device_ids=true, to_apply=%region_14.0 | all-reduce | flops 4097 | bytes 32776 | tf_op jit(solution)/shard_map/psum | solution.py:64
  623.5 0.8 fusion.20
  624.3 0.8 fusion.13
  (6 shorter events, 0.0 us)
Async XLA Ops:
  7.2 238.1 %all-gather.5.cloned.1.call-start = ((), (), s32[]{:S(2)}) async-start(), calls=%async_computation.1 | async-start | bytes 8650752 | tf_op jit(solution)/shard_map/all_gather | solution.py:40
  143.2 203.4 %copy-start.2 = (bf16[128,1024]{1,0:T(8,128)(2,1)S(1)}, bf16[128,1024]{1,0:T(8,128)(2,1)}, u32[]{:S(2)}) copy-start(bf16[128,1024]{1,0:T(8,128)(2,1)} %get-tuple-element.29) | copy-start | bytes 786436
  143.3 203.4 %all-gather.3.cloned.1.call-start = ((), (), s32[]{:S(2)}) async-start(), calls=%async_computation | async-start | bytes 8650752 | tf_op jit(solution)/shard_map/all_gather | solution.py:41
  144.0 338.8 %all-reduce.5.cloned.1.call-start = ((), (), s32[]{:S(2)}) async-start(), calls=%async_computation.2 | async-start | bytes 8388608 | tf_op jit(solution)/shard_map/psum | solution.py:50
  253.0 233.3 %copy-start.1 = (bf16[128,1024]{1,0:T(8,128)(2,1)S(1)}, bf16[128,1024]{1,0:T(8,128)(2,1)}, u32[]{:S(2)}) copy-start(bf16[128,1024]{1,0:T(8,128)(2,1)} %get-tuple-element.30) | copy-start | bytes 786436
  482.8 9.1 %slice-start = ((s8[8388608]{0:T(1024)(128)(4,1)}), s8[4194304]{0:T(1024)(128)(4,1)S(1)}, s32[]{:S(2)}) async-start(s8[8388608]{0:T(1024)(128)(4,1)} %bitcast.6), calls=%async_computation.3 | async-start | bytes 8388608
  486.3 5.6 slice-start.1
  486.3 5.9 copy-start
Sparse Core Ops, SparseCore 0:
  143.4 101.8 all-gather.4
  248.7 97.9 all-gather.2
  354.3 107.0 all-reduce.4
where the time goes:
time: 637 us; the launch traced here: 633 us
  blocking collectives  387 us (61%)
  waiting for transfers between devices  196 us (31%)
  matrix products  22.3 us (4%)
  between operations  17.5 us (3%)
  other arithmetic  9.82 us (2%)
    psum x1, blocking collectives, shards(): moment_sums = lax.psum((sum_a, square_a, sum_b, square_b), 'batch')  132 us
    psum x1, blocking collectives, shards(): lax.psum((jnp.sum(grad_norm_a, 0), jnp.sum(grad_norm_a * norm_af, 0), jnp...  128 us
    psum x1, blocking collectives, shards(): lax.psum(jnp.sum(norm_a.astype(jnp.float32) * norm_b.astype(jnp.float32),...  111 us
    all_gather x1, waiting for transfers between devices, shards(): lax.all_gather(norm_a, 'batch', axis=0, tiled=True)  101 us
    all_gather x1, waiting for transfers between devices, shards(): lax.all_gather(norm_b, 'batch', axis=0, tiled=True)  93.6 us
    psum x1, blocking collectives, shards(): lax.psum((gram_part_a, gram_part_b, diag_part), 'feat')  15.3 us
    dot_general x2, matrix products, outer_rows(): lax.dot_general(left, right, (((1,), (1,)), ((), ())), preferred_element_...  15.2 us
  transfers between devices with their start and end apart: 3, of which 2 were waited for; matrix products, arithmetic and copies ran while one was open for 1% of the time, Pallas kernels for 0%

commit v1 on v0

v1 whole, which is shorter than its diff:
```python
import jax
import jax.numpy as jnp
from jax import lax
from jax.sharding import Mesh, PartitionSpec as P

WIDTH = 8192

redund_weight = 0.0051
eps_var = 1e-05

ROWS = ("z", "yh", "c")
FEAT = ("yl", "x")
SWAP = [(0, 1), (1, 0)]


def batch_sum(values):
    values = values + lax.ppermute(values, "c", SWAP)
    chips = lax.axis_size("z") * lax.axis_size("yh")
    parts = lax.all_to_all(
        jnp.broadcast_to(values[None], (chips,) + values.shape), ("z", "yh"), 0, 0
    )
    return jnp.sum(parts, 0)


def shards(view_a, view_b):
    row_count, width = view_a.shape
    batch_total = row_count * lax.axis_size(ROWS)
    feats = lax.axis_size(FEAT)
    both = jnp.stack([view_a, view_b])
    gathered = lax.all_gather(both, ("z", "c"))
    other = lax.ppermute(both, "yh", SWAP)

    floats = both.astype(jnp.float32)
    moments = batch_sum(jnp.stack([jnp.sum(floats, 1), jnp.sum(floats * floats, 1)]))
    mean = moments[0] / batch_total
    rstd = lax.rsqrt(moments[1] / batch_total - mean * mean + eps_var)

    def standardize(values, view):
        return ((values.astype(jnp.float32) - mean[view]) * rstd[view]).astype(jnp.bfloat16)

    own = [standardize(both[v], v) for v in range(2)]
    cross_sum = batch_sum(
        jnp.sum(own[0].astype(jnp.float32) * own[1].astype(jnp.float32), 0)[None]
    )[0]
    corr_diag = cross_sum / batch_total
    diag_part = jnp.sum((1.0 - corr_diag) ** 2) - redund_weight * jnp.sum(corr_diag * corr_diag)
    diag_grad = -2.0 * (1.0 - corr_diag) - 2.0 * redund_weight * corr_diag

    rows = [jnp.concatenate([own[v], standardize(other[v], v)]) for v in range(2)]
    cols = [standardize(gathered[:, v], v).reshape(-1, width) for v in range(2)]
    panel = cols[0].shape[0]
    piece = 2 * row_count // feats
    grams = [
        lax.dot_general(
            rows[v], cols[v], (((1,), (1,)), ((), ())), preferred_element_type=jnp.float32
        )
        .astype(jnp.bfloat16)
        .reshape(feats, piece, panel)
        for v in range(2)
    ]
    pieces = lax.all_to_all(jnp.stack(grams, 1), FEAT, 0, 0)
    summed = jnp.sum(pieces.astype(jnp.float32), 0)
    frob = jnp.sum(summed[0] * summed[1])
    loss_part = (
        diag_part / lax.axis_size(ROWS) + redund_weight * frob / (batch_total * batch_total)
    )
    high = lax.reduce_precision(loss_part, 8, 7)
    middle = lax.reduce_precision(loss_part - high, 8, 7)
    low = lax.reduce_precision(loss_part - high - middle, 8, 7)
    lane = lax.broadcasted_iota(jnp.int32, (2, piece, 128), 2)
    extra = jnp.where(lane == 0, high, jnp.where(lane == 1, middle, jnp.where(lane == 2, low, 0.0)))
    sent = jnp.concatenate([summed, extra], 2).astype(jnp.bfloat16)
    full = lax.all_to_all(jnp.broadcast_to(sent[None], (feats,) + sent.shape), FEAT, 0, 0)
    low_gram = [full[:, v, :, :panel].reshape(2 * row_count, panel) for v in range(2)]
    loss_row = jnp.sum(full[:, 0, 0, panel : panel + 3].astype(jnp.float32))

    coupling = 2.0 * redund_weight / (batch_total * batch_total)
    products = [
        coupling * jnp.dot(low_gram[1 - v], cols[v], preferred_element_type=jnp.float32)
        for v in range(2)
    ]
    received = lax.ppermute(
        jnp.stack([p[row_count:] for p in products]).astype(jnp.bfloat16), "yh", SWAP
    )
    sums = []
    mine = []
    for v in range(2):
        product = products[v]
        mine.append(
            product[:row_count] + diag_grad * own[1 - v].astype(jnp.float32) / batch_total
        )
        theirs = product[row_count:]
        sums.append(jnp.sum(mine[v], 0) + jnp.sum(theirs, 0))
        sums.append(
            jnp.sum(mine[v] * own[v].astype(jnp.float32), 0)
            + jnp.sum(theirs * rows[v][row_count:].astype(jnp.float32), 0)
        )
    sums.append(jnp.full((width,), loss_row))
    back = batch_sum(jnp.stack(sums))
    scale = batch_total * batch_total / (redund_weight * WIDTH)
    grads = [
        (
            scale
            * rstd[v]
            * (
                mine[v]
                + received[v].astype(jnp.float32)
                - back[2 * v] / batch_total
                - own[v].astype(jnp.float32) * (back[2 * v + 1] / batch_total)
            )
        ).astype(jnp.bfloat16)
        for v in range(2)
    ]
    return grads[0], grads[1], back[4, 0]


def solution(mesh):
    fine = Mesh(mesh.devices.reshape(8, 2, 2, 2, 4), ROWS + FEAT)
    return jax.shard_map(
        shards,
        mesh=fine,
        in_specs=(P(ROWS, FEAT), P(ROWS, FEAT)),
        out_specs=(P(ROWS, FEAT), P(ROWS, FEAT), P()),
        check_vma=False,
    )
```

time: 637 us -> 221 us (0.35)
  blocking collectives: 387 us -> 0 us
  waiting for transfers between devices: 196 us -> 102 us
  starting transfers between devices: 0.12 us -> 47.7 us
  other arithmetic: 9.82 us -> 38.4 us
  matrix products: 22.3 us -> 5.23 us
  local copies, waits for them, and re-layouts: 0.32 us -> 8 us
    psum x4 -> x0, blocking collectives: 387 us -> none  [the longest x1 132 us: shards(): moment_sums = lax.psum((sum_a, square_a, sum_b, square_b), 'batch')]
    all_gather x2 -> x1, waiting for transfers between devices: 195 us -> 21.7 us  [shards(): gathered = lax.all_gather(both, ('z', 'c'))]
    all_to_all x0 -> x5, waiting for transfers between devices: none -> 74.4 us  [the longest x3 27.6 us: batch_sum(): lax.all_to_all(jnp.broadcast_to(values[None], (chips,) + values.shape), (...]
    all_to_all x0 -> x5, starting transfers between devices: none -> 36.1 us  [the longest x3 25.2 us: batch_sum(): lax.all_to_all(jnp.broadcast_to(values[None], (chips,) + values.shape), (...]
    convert_element_type x2 -> x6, other arithmetic: 1.62 us -> 27.9 us  [the longest x4 14.3 us: standardize(): ((values.astype(jnp.float32) - mean[view]) * rstd[view]).astype(jnp.bfloa...]
    dot_general x4, matrix products: 22.3 us -> 5.23 us  [the longest x2 2.69 us: shards(): lax.dot_general(rows[v], cols[v], (((1,), (1,)), ((), ())), preferred_ele...]
    ppermute x0 -> x5, starting transfers between devices: none -> 11.6 us  [the longest x3 5.82 us: batch_sum(): values = values + lax.ppermute(values, 'c', SWAP)]
  transfers between devices with their start and end apart: 3 -> 11, of which waited for: 2 -> 10; matrix products, arithmetic and copies ran while one was open for 1% -> 16% of each run, Pallas kernels for 0% -> 0%
where the time goes in v1:
time: 221 us
  waiting for transfers between devices  102 us (46%)
  starting transfers between devices  47.7 us (22%)
  other arithmetic  38.4 us (17%)
  between operations  19.1 us (9%)
  local copies, waits for them, and re-layouts  8 us (4%)
  matrix products  5.23 us (2%)
    all_to_all x3, waiting for transfers between devices, batch_sum(): lax.all_to_all(jnp.broadcast_to(values[None], (chips,) + values.shape), (...  27.6 us
    all_to_all x3, starting transfers between devices, batch_sum(): lax.all_to_all(jnp.broadcast_to(values[None], (chips,) + values.shape), (...  25.2 us
    all_to_all x1, waiting for transfers between devices, shards(): pieces = lax.all_to_all(jnp.stack(grams, 1), FEAT, 0, 0)  25.1 us
    all_gather x1, waiting for transfers between devices, shards(): gathered = lax.all_gather(both, ('z', 'c'))  21.7 us
    all_to_all x1, waiting for transfers between devices, shards(): lax.all_to_all(jnp.broadcast_to(sent[None], (feats,) + sent.shape), FEAT,...  21.7 us
    convert_element_type x4, other arithmetic, standardize(): ((values.astype(jnp.float32) - mean[view]) * rstd[view]).astype(jnp.bfloa...  14.3 us
    convert_element_type x1, other arithmetic, standardize(): values.astype(jnp.float32) - mean[view]  11.4 us
    all_to_all x1, starting transfers between devices, shards(): lax.all_to_all(jnp.broadcast_to(sent[None], (feats,) + sent.shape), FEAT,...  6.75 us
  transfers between devices with their start and end apart: 11, of which 10 were waited for; matrix products, arithmetic and copies ran while one was open for 16% of the time, Pallas kernels for 0%

profile of v1, /device:TPU:1, one launch (start us, length us, event | category | flops | bytes accessed | tf_op | source)
XLA Modules:
  0.0 220.6 jit_solution(6359280279307743537)
XLA Ops:
  7.2 0.0 all-gather.3.cloned.1.call-start
  7.2 1.9 pad_maximum_fusion.1
  9.1 0.0 all-gather.3.cloned.1.call-update
  9.2 1.2 convert_reduce_fusion.1
  10.4 3.3 %collective-permute-start = (f32[2,2,1024]{2,1,0:T(2,128)S(1)}, f32[2,2,1024]{2,1,0:T(2,128)S(1)}, u32[]{:S(2)}, u32[]{:S(2)}) collective-permute-start(f32[2,2,1024]{2,1,0:T(2,128)S(1)} %pad_maximum_fusion.4), channel_id=1, source_target_pairs={{0,8},{8,0},{1,9},{9,1},{2,10},{10,2},{3,11},{11,3},{4,12},{12,4},... | collective-permute-start | bytes 49160 | tf_op jit(solution)/shard_map/ppermute | solution.py:17
  13.7 0.8 collective-permute-done
  14.6 0.8 broadcast_in_dim.27
  15.4 9.2 %all-to-all-start = ((f32[16,2,2,1024]{3,2,1,0:T(2,128)}), f32[16,2,2,1024]{3,2,1,0:T(2,128)S(1)}, u32[]{:S(2)}, u32[]{:S(2)}) async-start(f32[16,2,2,1024]{3,2,1,0:T(2,128)} %broadcast_in_dim.27), calls=%async_computation | async-start | bytes 524288 | tf_op jit(solution)/shard_map/all_to_all | solution.py:19
  24.6 2.9 %collective-permute-start.1 = (bf16[2,128,1024]{2,1,0:T(8,128)(2,1)}, bf16[2,128,1024]{2,1,0:T(8,128)(2,1)S(1)}, u32[]{:S(2)}, u32[]{:S(2)}) collective-permute-start(bf16[2,128,1024]{2,1,0:T(8,128)(2,1)} %pad_maximum_fusion.1), channel_id=1, source_target_pairs={{0,16},{16,0},{1,17},{17,1},{2,18},{18,2},{3,19},{19,3},{4,20},{20... | collective-permute-start | bytes 1572872 | tf_op jit(solution)/shard_map/ppermute | solution.py:31
  27.4 13.8 %all-to-all-done = f32[16,2,2,1024]{3,2,1,0:T(2,128)S(1)} async-done(((f32[16,2,2,1024]{3,2,1,0:T(2,128)}), f32[16,2,2,1024]{3,2,1,0:T(2,128)S(1)}, u32[]{:S(2)}, u32[]{:S(2)}) %all-to-all-start) | async-done | bytes 262176 | tf_op jit(solution)/shard_map/all_to_all | solution.py:19
  41.2 0.1 reduce_sum.173
  41.3 0.6 collective-permute-done.1
  41.9 1.4 fusion.29
  43.3 1.5 collective-permute-start.2
  44.8 0.8 collective-permute-done.2
  45.6 0.7 broadcast_in_dim.30
  46.3 8.7 %all-to-all-start.2 = ((f32[16,1,1024]{2,1,0:T(1,128)}), f32[16,1,1024]{2,1,0:T(1,128)S(1)}, u32[]{:S(2)}, u32[]{:S(2)}) async-start(f32[16,1,1024]{2,1,0:T(1,128)} %broadcast_in_dim.30), calls=%async_computation.2 | async-start | bytes 131072 | tf_op jit(solution)/shard_map/all_to_all | solution.py:19
  55.1 21.7 %all-gather.3.cloned.1.call-done = bf16[32,128,1024]{2,1,0:T(8,128)(2,1)} async-done(((bf16[2,128,1024]{2,1,0:T(8,128)(2,1)}), bf16[32,128,1024]{2,1,0:T(8,128)(2,1)}) %all-gather.3.cloned.1.call-update) | async-done | bytes 8388624 | tf_op jit(solution)/shard_map/all_gather | solution.py:30
  76.8 11.4 %slice_convert_fusion.1 = (f32[16,1,128,1024]{3,2,1,0:T(8,128)}, f32[16,1,128,1024]{3,2,1,0:T(8,128)}) fusion(bf16[16,2,128,1024]{3,2,1,0:T(8,128)(2,1)} %bitcast.78), kind=kLoop, calls=%fused_computation.9 | loop fusion | flops 4194304 | bytes 25165824 | tf_op jit(solution)/shard_map/convert_element_type | solution.py:39
  88.2 0.0 copy-start
  88.2 4.9 %fusion.3 = bf16[2048,1024]{1,0:T(8,128)(2,1)S(1)} fusion(f32[16,1,128,1024]{3,2,1,0:T(8,128)} %get-tuple-element.24, f32[1024]{0:T(1024)S(1)} %bitcast.95, f32[1024]{0:T(1024)S(1)} %bitcast.104), kind=kLoop, calls=%fused_computation.5 | loop fusion | flops 6291456 | bytes 12591104 | tf_op jit(solution)/shard_map/convert_element_type | solution.py:39
  93.0 0.9 copy-done
  94.0 1.4 fusion.1
  95.3 1.3 convolution_convert_fusion.1
  96.7 1.3 convolution_convert_fusion
  98.0 1.6 pad_maximum_fusion
  99.6 0.0 all-to-all-done.2
  99.6 4.1 %all-to-all-start.1 = ((bf16[8,2,32,2048]{3,2,1,0:T(8,128)(2,1)}), bf16[8,2,32,2048]{3,2,1,0:T(8,128)(2,1)S(1)}, u32[]{:S(2)}, u32[]{:S(2)}) async-start(bf16[8,2,32,2048]{3,2,1,0:T(8,128)(2,1)} %pad_maximum_fusion), calls=%async_computation.1 | async-start | bytes 4194304 | tf_op jit(solution)/shard_map/all_to_all | solution.py:61
  103.8 0.1 reduce_sum.176
  103.8 0.6 multiply_reduce_fusion.2
  105.7 25.1 %all-to-all-done.1 = bf16[8,2,32,2048]{3,2,1,0:T(8,128)(2,1)S(1)} async-done(((bf16[8,2,32,2048]{3,2,1,0:T(8,128)(2,1)}), bf16[8,2,32,2048]{3,2,1,0:T(8,128)(2,1)S(1)}, u32[]{:S(2)}, u32[]{:S(2)}) %all-to-all-start.1) | async-done | bytes 2097184 | tf_op jit(solution)/shard_map/all_to_all | solution.py:61
  130.8 0.4 convert_reduce_fusion
  131.2 0.7 fusion.32
  135.4 0.6 compare_select_fusion
  136.0 1.3 select_convert_fusion
  137.4 1.6 broadcast_in_dim.60
  139.0 6.7 %all-to-all-start.3 = ((bf16[8,2,32,2176]{3,2,1,0:T(8,128)(2,1)}), bf16[8,2,32,2176]{3,2,1,0:T(8,128)(2,1)S(1)}, u32[]{:S(2)}, u32[]{:S(2)}) async-start(bf16[8,2,32,2176]{3,2,1,0:T(8,128)(2,1)} %broadcast_in_dim.60), calls=%async_computation.3 | async-start | bytes 4456448 | tf_op jit(solution)/shard_map/all_to_all | solution.py:73
  145.7 6.7 %multiply_convert_fusion.1 = (bf16[16,1,128,1024]{3,2,1,0:T(8,128)(2,1)}, bf16[16,1,128,1024]{3,2,1,0:T(8,128)(2,1)}) fusion(f32[1024]{0:T(1024)S(1)} %bitcast.96, f32[1024]{0:T(1024)S(1)} %bitcast.105, bf16[16,2,128,1024]{3,2,1,0:T(8,128)(2,1)} %bitcast.79, f32[1024]{0:T(1024)S(1)} %bitcast.99, f32[1024]{0:T(1024)S(1)} %bitcast.102), kind=kLoop, calls=%fused_computation.7 | loop fusion | flops 16777216 | bytes 16793600 | tf_op jit(solution)/shard_map/convert_element_type | solution.py:39
  152.5 21.7 %all-to-all-done.3 = bf16[8,2,32,2176]{3,2,1,0:T(8,128)(2,1)S(1)} async-done(((bf16[8,2,32,2176]{3,2,1,0:T(8,128)(2,1)}), bf16[8,2,32,2176]{3,2,1,0:T(8,128)(2,1)S(1)}, u32[]{:S(2)}, u32[]{:S(2)}) %all-to-all-start.3) | async-done | bytes 2228256 | tf_op jit(solution)/shard_map/all_to_all | solution.py:73
  174.2 0.1 copy.36
  174.3 0.0 copy-start.2
  174.3 0.6 convert_reduce_fusion.2
  174.9 0.3 fusion.41
  175.2 0.0 copy-start.1
  175.2 1.3 copy-done.2
  176.5 1.3 convolution_multiply_fusion.1
  177.7 0.2 copy-done.1
  178.0 1.3 convolution_multiply_fusion
  179.2 0.5 fusion.5
  179.8 0.7 stack_broadcast_in_dim.3
  180.5 0.9 collective-permute-start.4
  181.4 0.8 collective-permute-done.4
  182.3 0.9 broadcast_in_dim.61
  183.1 7.3 %all-to-all-start.4 = ((f32[16,5,1024]{2,1,0:T(8,128)}), f32[16,5,1024]{2,1,0:T(8,128)S(1)}, u32[]{:S(2)}, u32[]{:S(2)}) async-start(f32[16,5,1024]{2,1,0:T(8,128)} %broadcast_in_dim.61), calls=%async_computation.4 | async-start | bytes 1048576 | tf_op jit(solution)/shard_map/all_to_all | solution.py:19
  190.5 0.8 pad_maximum_fusion.2
  191.3 2.9 %collective-permute-start.3 = (bf16[2,128,1024]{2,1,0:T(8,128)(2,1)}, bf16[2,128,1024]{2,1,0:T(8,128)(2,1)}, u32[]{:S(2)}, u32[]{:S(2)}) collective-permute-start(bf16[2,128,1024]{2,1,0:T(8,128)(2,1)} %pad_maximum_fusion.2), channel_id=1, source_target_pairs={{0,16},{16,0},{1,17},{17,1},{2,18},{18,2},{3,19},{19,3},{4,20},{20... | collective-permute-start | bytes 1572872 | tf_op jit(solution)/shard_map/ppermute | solution.py:82
  194.2 13.8 %all-to-all-done.4 = f32[16,5,1024]{2,1,0:T(8,128)S(1)} async-done(((f32[16,5,1024]{2,1,0:T(8,128)}), f32[16,5,1024]{2,1,0:T(8,128)S(1)}, u32[]{:S(2)}, u32[]{:S(2)}) %all-to-all-start.4) | async-done | bytes 327712 | tf_op jit(solution)/shard_map/all_to_all | solution.py:19
  208.0 0.5 slice.145
  208.6 3.0 %collective-permute-done.3 = bf16[2,128,1024]{2,1,0:T(8,128)(2,1)} collective-permute-done((bf16[2,128,1024]{2,1,0:T(8,128)(2,1)}, bf16[2,128,1024]{2,1,0:T(8,128)(2,1)}, u32[]{:S(2)}, u32[]{:S(2)}) %collective-permute-start.3) | collective-permute-done | bytes 524320 | tf_op jit(solution)/shard_map/ppermute | solution.py:82
  211.6 2.2 fusion.17
  (19 shorter events, 0.3 us)
Async XLA Ops:
  7.2 69.6 %all-gather.3.cloned.1.call-start = ((), (), s32[]{:S(2)}) async-start(), calls=%async_computation.5 | async-start | bytes 8912896 | tf_op jit(solution)/shard_map/all_gather | solution.py:30
  10.4 4.2 %collective-permute-start = (f32[2,2,1024]{2,1,0:T(2,128)S(1)}, f32[2,2,1024]{2,1,0:T(2,128)S(1)}, u32[]{:S(2)}, u32[]{:S(2)}) collective-permute-start(f32[2,2,1024]{2,1,0:T(2,128)S(1)} %pad_maximum_fusion.4), channel_id=1, source_target_pairs={{0,8},{8,0},{1,9},{9,1},{2,10},{10,2},{3,11},{11,3},{4,12},{12,4},... | collective-permute-start | bytes 49160 | tf_op jit(solution)/shard_map/ppermute | solution.py:17
  15.4 25.8 %all-to-all-start = ((f32[16,2,2,1024]{3,2,1,0:T(2,128)}), f32[16,2,2,1024]{3,2,1,0:T(2,128)S(1)}, u32[]{:S(2)}, u32[]{:S(2)}) async-start(f32[16,2,2,1024]{3,2,1,0:T(2,128)} %broadcast_in_dim.27), calls=%async_computation | async-start | bytes 524288 | tf_op jit(solution)/shard_map/all_to_all | solution.py:19
  24.6 17.3 %collective-permute-start.1 = (bf16[2,128,1024]{2,1,0:T(8,128)(2,1)}, bf16[2,128,1024]{2,1,0:T(8,128)(2,1)S(1)}, u32[]{:S(2)}, u32[]{:S(2)}) collective-permute-start(bf16[2,128,1024]{2,1,0:T(8,128)(2,1)} %pad_maximum_fusion.1), channel_id=1, source_target_pairs={{0,16},{16,0},{1,17},{17,1},{2,18},{18,2},{3,19},{19,3},{4,20},{20... | collective-permute-start | bytes 1572872 | tf_op jit(solution)/shard_map/ppermute | solution.py:31
  43.3 2.4 %collective-permute-start.2 = (f32[1,1024]{1,0:T(1,128)S(1)}, f32[1,1024]{1,0:T(1,128)S(1)}, u32[]{:S(2)}, u32[]{:S(2)}) collective-permute-start(f32[1,1024]{1,0:T(1,128)S(1)} %bitcast.106), channel_id=1, source_target_pairs={{0,8},{8,0},{1,9},{9,1},{2,10},{10,2},{3,11},{11,3},{4,12},{12,4},... | collective-permute-start | bytes 12296 | tf_op jit(solution)/shard_map/ppermute | solution.py:17
  46.3 53.3 %all-to-all-start.2 = ((f32[16,1,1024]{2,1,0:T(1,128)}), f32[16,1,1024]{2,1,0:T(1,128)S(1)}, u32[]{:S(2)}, u32[]{:S(2)}) async-start(f32[16,1,1024]{2,1,0:T(1,128)} %broadcast_in_dim.30), calls=%async_computation.2 | async-start | bytes 131072 | tf_op jit(solution)/shard_map/all_to_all | solution.py:19
  88.2 5.8 %copy-start = (f32[16,1,128,1024]{3,2,1,0:T(8,128)S(1)}, f32[16,1,128,1024]{3,2,1,0:T(8,128)}, u32[]{:S(2)}) copy-start(f32[16,1,128,1024]{3,2,1,0:T(8,128)} %get-tuple-element.25) | copy-start | bytes 25165828
  99.6 31.2 %all-to-all-start.1 = ((bf16[8,2,32,2048]{3,2,1,0:T(8,128)(2,1)}), bf16[8,2,32,2048]{3,2,1,0:T(8,128)(2,1)S(1)}, u32[]{:S(2)}, u32[]{:S(2)}) async-start(bf16[8,2,32,2048]{3,2,1,0:T(8,128)(2,1)} %pad_maximum_fusion), calls=%async_computation.1 | async-start | bytes 4194304 | tf_op jit(solution)/shard_map/all_to_all | solution.py:61
  139.0 35.2 %all-to-all-start.3 = ((bf16[8,2,32,2176]{3,2,1,0:T(8,128)(2,1)}), bf16[8,2,32,2176]{3,2,1,0:T(8,128)(2,1)S(1)}, u32[]{:S(2)}, u32[]{:S(2)}) async-start(bf16[8,2,32,2176]{3,2,1,0:T(8,128)(2,1)} %broadcast_in_dim.60), calls=%async_computation.3 | async-start | bytes 4456448 | tf_op jit(solution)/shard_map/all_to_all | solution.py:73
  174.3 2.2 copy-start.2
  175.2 2.8 %copy-start.1 = (bf16[16,1,128,1024]{3,2,1,0:T(8,128)(2,1)S(1)}, bf16[16,1,128,1024]{3,2,1,0:T(8,128)(2,1)}, u32[]{:S(2)}) copy-start(bf16[16,1,128,1024]{3,2,1,0:T(8,128)(2,1)} %get-tuple-element.23) | copy-start | bytes 12582916
  180.5 1.8 collective-permute-start.4
  183.1 24.8 %all-to-all-start.4 = ((f32[16,5,1024]{2,1,0:T(8,128)}), f32[16,5,1024]{2,1,0:T(8,128)S(1)}, u32[]{:S(2)}, u32[]{:S(2)}) async-start(f32[16,5,1024]{2,1,0:T(8,128)} %broadcast_in_dim.61), calls=%async_computation.4 | async-start | bytes 1048576 | tf_op jit(solution)/shard_map/all_to_all | solution.py:19
  191.3 20.3 %collective-permute-start.3 = (bf16[2,128,1024]{2,1,0:T(8,128)(2,1)}, bf16[2,128,1024]{2,1,0:T(8,128)(2,1)}, u32[]{:S(2)}, u32[]{:S(2)}) collective-permute-start(bf16[2,128,1024]{2,1,0:T(8,128)(2,1)} %pad_maximum_fusion.2), channel_id=1, source_target_pairs={{0,16},{16,0},{1,17},{17,1},{2,18},{18,2},{3,19},{19,3},{4,20},{20... | collective-permute-start | bytes 1572872 | tf_op jit(solution)/shard_map/ppermute | solution.py:82
Sparse Core Ops, SparseCore 0:
  9.8 66.9 all-gather.2

commit v2 on v1

v2 whole, which is shorter than its diff:
```python
import jax
import jax.numpy as jnp
from jax import lax
from jax.experimental import pallas as pl
from jax.experimental.pallas import tpu as pltpu
from jax.sharding import Mesh, PartitionSpec as P

WIDTH = 8192

redund_weight = 0.0051
eps_var = 1e-05

ROWS = ("z", "yh", "c")
FEAT = ("yl", "x")
SWAP = [(0, 1), (1, 0)]
LIMIT = 48 * 1024 * 1024


def pair_sum(values):
    values = values + lax.ppermute(values, "c", SWAP)
    return values + lax.ppermute(values, "yh", SWAP)


def spread(values):
    count = lax.axis_size("z")
    return lax.all_to_all(jnp.broadcast_to(values[None], (count,) + values.shape), "z", 0, 0)


def batch_sum(values):
    return jnp.sum(spread(pair_sum(values)), 0)


def standardize(values, mean, rstd):
    return ((values.astype(jnp.float32) - mean) * rstd).astype(jnp.bfloat16)


def gram_kernel(mean, rstd, raw, own, other, cols, rows, parts):
    count = own.shape[1]

    @pl.when(pl.program_id(0) == 0)
    def _():
        for v in range(2):
            rows[v, :count] = standardize(own[v], mean[v : v + 1], rstd[v : v + 1])
            rows[v, count:] = standardize(other[v], mean[v : v + 1], rstd[v : v + 1])

    for v in range(2):
        for k in range(raw.shape[0]):
            cols[v, k * count : (k + 1) * count] = standardize(
                raw[k, v], mean[v : v + 1], rstd[v : v + 1]
            )
        gram = lax.dot_general(
            rows[v], cols[v], (((1,), (1,)), ((), ())), preferred_element_type=jnp.float32
        )
        feats, _, piece, width = parts.shape
        parts[:, v] = gram.astype(jnp.bfloat16).reshape(feats, piece, width)


def gram_parts(mean, rstd, gathered, own, other, feats):
    blocks, _, count, width = gathered.shape
    step = 2
    piece = 2 * count // feats
    whole = lambda shape: pl.BlockSpec(shape, lambda k: (0,) * len(shape))
    return pl.pallas_call(
        gram_kernel,
        grid=(blocks // step,),
        in_specs=[
            whole((2, width)),
            whole((2, width)),
            pl.BlockSpec((step, 2, count, width), lambda k: (k, 0, 0, 0)),
            whole((2, count, width)),
            whole((2, count, width)),
        ],
        out_specs=[
            pl.BlockSpec((2, step * count, width), lambda k: (0, k, 0)),
            whole((2, 2 * count, width)),
            pl.BlockSpec((feats, 2, piece, step * count), lambda k: (0, 0, 0, k)),
        ],
        out_shape=[
            jax.ShapeDtypeStruct((2, blocks * count, width), jnp.bfloat16),
            jax.ShapeDtypeStruct((2, 2 * count, width), jnp.bfloat16),
            jax.ShapeDtypeStruct((feats, 2, piece, blocks * count), jnp.bfloat16),
        ],
        compiler_params=pltpu.CompilerParams(vmem_limit_bytes=LIMIT),
        name="gram",
    )(mean, rstd, gathered, own, other)


def reduce_kernel(weight, diag, pieces, sent):
    feats, _, piece, panel = pieces.shape
    total = []
    for v in range(2):
        total.append(pieces[0, v].astype(jnp.float32))
        for w in range(1, feats):
            total[v] = total[v] + pieces[w, v].astype(jnp.float32)
    frob = jnp.sum(total[0] * total[1], keepdims=True)
    loss_part = diag[...] + weight * frob
    part = jnp.broadcast_to(loss_part, (piece, 128))
    high = part.astype(jnp.bfloat16).astype(jnp.float32)
    middle = (part - high).astype(jnp.bfloat16).astype(jnp.float32)
    low = part - high - middle
    lane = lax.broadcasted_iota(jnp.int32, part.shape, 1)
    extra = jnp.where(lane == 0, high, jnp.where(lane == 1, middle, jnp.where(lane == 2, low, 0.0)))
    extra = extra.astype(jnp.bfloat16)
    for v in range(2):
        low_gram = total[v].astype(jnp.bfloat16)
        for w in range(feats):
            sent[w, v, :, :panel] = low_gram
            sent[w, v, :, panel:] = extra


def reduce_parts(pieces, diag, weight):
    feats, _, piece, panel = pieces.shape
    return pl.pallas_call(
        lambda *refs: reduce_kernel(weight, *refs),
        out_shape=jax.ShapeDtypeStruct((feats, 2, piece, panel + 128), jnp.bfloat16),
        compiler_params=pltpu.CompilerParams(vmem_limit_bytes=LIMIT),
        name="reduce",
    )(diag, pieces)


def product_kernel(coupling, total_rows, full, tail, cols, rows, diag_grad, mine, sent, sums, acc):
    step = pl.program_id(0)
    feats, _, piece, depth = full.shape
    count = rows.shape[1] // 2
    for v in range(2):
        low_gram = full[:, 1 - v].reshape(feats * piece, depth)
        product = jnp.dot(low_gram, cols[v], preferred_element_type=jnp.float32)

        @pl.when(step == 0)
        def _():
            acc[v] = product

        @pl.when(step > 0)
        def _():
            acc[v] += product

    @pl.when(step == pl.num_programs(0) - 1)
    def _():
        for v in range(2):
            near = coupling * acc[v, :count] + diag_grad[...] * (
                rows[1 - v, :count].astype(jnp.float32) * (1.0 / total_rows)
            )
            far = coupling * acc[v, count:]
            mine[v] = near
            sent[v] = far.astype(jnp.bfloat16)
            sums[2 * v : 2 * v + 1] = jnp.sum(near, 0, keepdims=True) + jnp.sum(
                far, 0, keepdims=True
            )
            sums[2 * v + 1 : 2 * v + 2] = jnp.sum(
                near * rows[v, :count].astype(jnp.float32), 0, keepdims=True
            ) + jnp.sum(far * rows[v, count:].astype(jnp.float32), 0, keepdims=True)
        first = tail[:, 0, 0:1, :].astype(jnp.float32).reshape(feats, 128)
        loss = jnp.sum(first, keepdims=True)
        sums[4:8] = jnp.broadcast_to(loss, (4, sums.shape[1]))


def products(full, cols, rows, diag_grad, coupling, total_rows):
    feats, _, piece, wide = full.shape
    _, panel, width = cols.shape
    count = rows.shape[1] // 2
    depth = 256
    whole = lambda shape: pl.BlockSpec(shape, lambda k: (0,) * len(shape))
    return pl.pallas_call(
        lambda *refs: product_kernel(coupling, total_rows, *refs),
        grid=(panel // depth,),
        in_specs=[
            pl.BlockSpec((feats, 2, piece, depth), lambda k: (0, 0, 0, k)),
            pl.BlockSpec((feats, 2, piece, 128), lambda k: (0, 0, 0, panel // 128)),
            pl.BlockSpec((2, depth, width), lambda k: (0, k, 0)),
            whole((2, 2 * count, width)),
            whole((1, width)),
        ],
        out_specs=[
            whole((2, count, width)),
            whole((2, count, width)),
            whole((8, width)),
        ],
        out_shape=[
            jax.ShapeDtypeStruct((2, count, width), jnp.float32),
            jax.ShapeDtypeStruct((2, count, width), jnp.bfloat16),
            jax.ShapeDtypeStruct((8, width), jnp.float32),
        ],
        scratch_shapes=[pltpu.VMEM((2, 2 * count, width), jnp.float32)],
        compiler_params=pltpu.CompilerParams(vmem_limit_bytes=LIMIT),
        name="products",
    )(full, full, cols, rows, diag_grad)


def final_kernel(scale, total_rows, parts, rstd, mine, received, rows, grad_a, grad_b, loss):
    total = parts[0]
    for k in range(1, parts.shape[0]):
        total = total + parts[k]
    total = total * (1.0 / total_rows)
    count = mine.shape[1]
    for v, out in ((0, grad_a), (1, grad_b)):
        out[...] = (
            (scale * rstd[v : v + 1])
            * (
                mine[v]
                + received[v].astype(jnp.float32)
                - total[2 * v : 2 * v + 1]
                - rows[v, :count].astype(jnp.float32) * total[2 * v + 1 : 2 * v + 2]
            )
        ).astype(jnp.bfloat16)
    loss[...] = total[4:5, :128] * total_rows


def finish(parts, rstd, mine, received, rows, scale, total_rows):
    _, count, width = mine.shape
    return pl.pallas_call(
        lambda *refs: final_kernel(scale, total_rows, *refs),
        out_shape=[
            jax.ShapeDtypeStruct((count, width), jnp.bfloat16),
            jax.ShapeDtypeStruct((count, width), jnp.bfloat16),
            jax.ShapeDtypeStruct((1, 128), jnp.float32),
        ],
        compiler_params=pltpu.CompilerParams(vmem_limit_bytes=LIMIT),
        name="finish",
    )(parts, rstd, mine, received, rows)


def shards(view_a, view_b):
    row_count, _ = view_a.shape
    batch_total = row_count * lax.axis_size(ROWS)
    feats = lax.axis_size(FEAT)
    both = jnp.stack([view_a, view_b])
    gathered = lax.all_gather(both, ("z", "c"))
    other = lax.ppermute(both, "yh", SWAP)

    floats = both.astype(jnp.float32)
    moments = batch_sum(jnp.stack([jnp.sum(floats, 1), jnp.sum(floats * floats, 1)]))
    mean = moments[0] / batch_total
    rstd = lax.rsqrt(moments[1] / batch_total - mean * mean + eps_var)

    own_a = standardize(view_a, mean[0], rstd[0]).astype(jnp.float32)
    own_b = standardize(view_b, mean[1], rstd[1]).astype(jnp.float32)
    corr_diag = batch_sum(jnp.sum(own_a * own_b, 0)[None]) / batch_total
    diag_part = jnp.sum((1.0 - corr_diag) ** 2) - redund_weight * jnp.sum(corr_diag * corr_diag)
    diag_grad = -2.0 * (1.0 - corr_diag) - 2.0 * redund_weight * corr_diag
    diag_share = (diag_part / lax.axis_size(ROWS)).reshape(1, 1)

    cols, rows, parts = gram_parts(mean, rstd, gathered, both, other, feats)
    pieces = lax.all_to_all(parts, FEAT, 0, 0)
    sent = reduce_parts(pieces, diag_share, redund_weight / (batch_total * batch_total))
    full = lax.all_to_all(sent, FEAT, 0, 0)
    coupling = 2.0 * redund_weight / (batch_total * batch_total)
    mine, leaving, sums = products(full, cols, rows, diag_grad, coupling, batch_total)
    received = lax.ppermute(leaving, "yh", SWAP)
    back = spread(pair_sum(sums))
    scale = batch_total * batch_total / (redund_weight * WIDTH)
    grad_a, grad_b, loss = finish(back, rstd, mine, received, rows, scale, batch_total)
    return grad_a, grad_b, loss[0, 0]


def solution(mesh):
    fine = Mesh(mesh.devices.reshape(8, 2, 2, 2, 4), ROWS + FEAT)
    return jax.shard_map(
        shards,
        mesh=fine,
        in_specs=(P(ROWS, FEAT), P(ROWS, FEAT)),
        out_specs=(P(ROWS, FEAT), P(ROWS, FEAT), P()),
        check_vma=False,
    )
```

time: 221 us -> 204 us (0.923)
  blocking collectives: 0 us -> 47.2 us
  other arithmetic: 38.4 us -> 4.12 us
  waiting for transfers between devices: 102 us -> 75.7 us
  Pallas kernels: 0 us -> 22.9 us
  starting transfers between devices: 47.7 us -> 34.1 us
  local copies, waits for them, and re-layouts: 8 us -> 2.74 us
  matrix products: 5.23 us -> 0 us
  between operations: 19.1 us -> 15.5 us
    all_to_all x0 -> x2, blocking collectives: none -> 47.2 us  [the longest x1 33.4 us: shards(): full = lax.all_to_all(sent, FEAT, 0, 0)]
    all_to_all x5 -> x3, waiting for transfers between devices: 74.4 us -> 31.8 us  [the longest x1 25.2 us: shards(): pieces = lax.all_to_all(parts, FEAT, 0, 0)]
    convert_element_type x6 -> x0, other arithmetic: 27.9 us -> none  [the longest x4 14.3 us: standardize(): ((values.astype(jnp.float32) - mean[view]) * rstd[view]).astype(jnp.bfloa...]
    pallas_call x0 -> x4, Pallas kernels: none -> 22.9 us  [the longest x1 11 us: gram_parts(): pl.pallas_call(gram_kernel, grid=(blocks // step,), in_specs=[whole((2, w...]
    all_to_all x5 -> x3, starting transfers between devices: 36.1 us -> 14.7 us  [the longest x2 9.79 us: spread(): lax.all_to_all(jnp.broadcast_to(values[None], (count,) + values.shape), '...]
    ppermute x4 -> x7, waiting for transfers between devices: 5.52 us -> 18.1 us  [the longest x3 16.5 us: pair_sum(): return values + lax.ppermute(values, 'yh', SWAP)]
    ppermute x4 -> x7, starting transfers between devices: 8.68 us -> 16.4 us  [the longest x3 9.04 us: pair_sum(): values = values + lax.ppermute(values, 'c', SWAP)]
    dot_general x4 -> x0, matrix products: 5.23 us -> none  [the longest x2 2.69 us: shards(): lax.dot_general(rows[v], cols[v], (((1,), (1,)), ((), ())), preferred_ele...]
  transfers between devices with their start and end apart: 11 -> 12, of which waited for: 10 -> 8; matrix products, arithmetic and copies ran while one was open for 16% -> 2% of each run, Pallas kernels for 0% -> 5%
where the time goes in v2:
time: 204 us; the launch traced here: 202 us
  waiting for transfers between devices  75.7 us (37%)
  blocking collectives  47.2 us (23%)
  starting transfers between devices  34.1 us (17%)
  Pallas kernels  22.9 us (11%)
  between operations  15.5 us (8%)
  other arithmetic  4.12 us (2%)
  local copies, waits for them, and re-layouts  2.74 us (1%)
    all_to_all x1, blocking collectives, shards(): full = lax.all_to_all(sent, FEAT, 0, 0)  33.4 us
    all_gather x1, waiting for transfers between devices, shards(): gathered = lax.all_gather(both, ('z', 'c'))  25.8 us
    all_to_all x1, waiting for transfers between devices, shards(): pieces = lax.all_to_all(parts, FEAT, 0, 0)  25.2 us
    ppermute x3, waiting for transfers between devices, pair_sum(): return values + lax.ppermute(values, 'yh', SWAP)  16.5 us
    all_to_all x1, blocking collectives, spread(): lax.all_to_all(jnp.broadcast_to(values[None], (count,) + values.shape), '...  13.9 us
    pallas_call x1, Pallas kernels, gram_parts(): pl.pallas_call(gram_kernel, grid=(blocks // step,), in_specs=[whole((2, w...  11 us
    pallas_call x1, Pallas kernels, products(): pl.pallas_call(lambda *refs: product_kernel(coupling, total_rows, *refs),...  10.4 us
    all_to_all x2, starting transfers between devices, spread(): lax.all_to_all(jnp.broadcast_to(values[None], (count,) + values.shape), '...  9.79 us
  transfers between devices with their start and end apart: 12, of which 8 were waited for; matrix products, arithmetic and copies ran while one was open for 2% of the time, Pallas kernels for 5%

profile of v2, /device:TPU:1, one launch (start us, length us, event | category | flops | bytes accessed | tf_op | source)
XLA Modules:
  0.0 202.3 jit_solution(2745037923517900506)
XLA Ops:
  7.2 0.0 copy-start.3
  7.2 0.0 copy-start.2
  7.2 0.0 all-gather.3.cloned.1.call-start
  7.2 1.9 pad_maximum_fusion.own
  9.2 0.0 copy-start
  9.2 0.0 all-gather.3.cloned.1.call-update
  9.2 1.3 convert_reduce_fusion
  10.5 3.3 %collective-permute-start = (f32[2,2,1024]{2,1,0:T(2,128)S(1)}, f32[2,2,1024]{2,1,0:T(2,128)S(1)}, u32[]{:S(2)}, u32[]{:S(2)}) collective-permute-start(f32[2,2,1024]{2,1,0:T(2,128)S(1)} %pad_maximum_fusion.1), channel_id=1, source_target_pairs={{0,8},{8,0},{1,9},{9,1},{2,10},{10,2},{3,11},{11,3},{4,12},{12,4},... | collective-permute-start | bytes 49160 | tf_op jit(solution)/shard_map/ppermute | solution.py:20
  13.8 0.8 collective-permute-done
  14.7 1.3 collective-permute-start.1
  15.9 2.9 %collective-permute-done.1 = f32[2,2,1024]{2,1,0:T(2,128)S(1)} collective-permute-done((f32[2,2,1024]{2,1,0:T(2,128)S(1)}, f32[2,2,1024]{2,1,0:T(2,128)S(1)}, u32[]{:S(2)}, u32[]{:S(2)}) %collective-permute-start.1) | collective-permute-done | bytes 16416 | tf_op jit(solution)/shard_map/ppermute | solution.py:21
  18.9 0.7 broadcast_in_dim.10
  19.5 6.5 %all-to-all-start = ((f32[8,2,2,1024]{3,2,1,0:T(2,128)}), f32[8,2,2,1024]{3,2,1,0:T(2,128)S(1)}, u32[]{:S(2)}, u32[]{:S(2)}) async-start(f32[8,2,2,1024]{3,2,1,0:T(2,128)} %broadcast_in_dim.10), calls=%async_computation | async-start | bytes 262144 | tf_op jit(solution)/shard_map/all_to_all | solution.py:26
  26.0 2.9 %collective-permute-start.4 = (bf16[2,128,1024]{2,1,0:T(8,128)(2,1)}, bf16[2,128,1024]{2,1,0:T(8,128)(2,1)S(1)}, u32[]{:S(2)}, u32[]{:S(2)}) collective-permute-start(bf16[2,128,1024]{2,1,0:T(8,128)(2,1)} %pad_maximum_fusion.own), channel_id=1, source_target_pairs={{0,16},{16,0},{1,17},{17,1},{2,18},{18,2},{3,19},{19,3},{4,20},{20... | collective-permute-start | bytes 1572872 | tf_op jit(solution)/shard_map/ppermute | solution.py:228
  28.9 6.6 %all-to-all-done = f32[8,2,2,1024]{3,2,1,0:T(2,128)S(1)} async-done(((f32[8,2,2,1024]{3,2,1,0:T(2,128)}), f32[8,2,2,1024]{3,2,1,0:T(2,128)S(1)}, u32[]{:S(2)}, u32[]{:S(2)}) %all-to-all-start) | async-done | bytes 131104 | tf_op jit(solution)/shard_map/all_to_all | solution.py:26
  35.6 0.0 copy-done.3
  35.6 0.0 copy-done.2
  35.6 0.2 multiply_reduce_fusion
  35.8 3.1 %collective-permute-start.2 = (f32[1,1024]{1,0:T(1,128)S(1)}, f32[1,1024]{1,0:T(1,128)S(1)}, u32[]{:S(2)}, u32[]{:S(2)}) collective-permute-start(f32[1,1024]{1,0:T(1,128)S(1)} %bitcast.38), channel_id=1, source_target_pairs={{0,8},{8,0},{1,9},{9,1},{2,10},{10,2},{3,11},{11,3},{4,12},{12,4},... | collective-permute-start | bytes 12296 | tf_op jit(solution)/shard_map/ppermute | solution.py:20
  38.9 0.8 collective-permute-done.2
  39.7 2.9 %collective-permute-start.3 = (f32[1,1024]{1,0:T(1,128)S(1)}, f32[1,1024]{1,0:T(1,128)S(1)}, u32[]{:S(2)}, u32[]{:S(2)}) collective-permute-start(f32[1,1024]{1,0:T(1,128)S(1)} %add.28), channel_id=1, source_target_pairs={{0,16},{16,0},{1,17},{17,1},{2,18},{18,2},{3,19},{19,3},{4,20},{20... | collective-permute-start | bytes 12296 | tf_op jit(solution)/shard_map/ppermute | solution.py:21
  42.6 1.1 collective-permute-done.3
  43.7 0.6 broadcast_in_dim.26
  44.3 3.3 %all-to-all-start.1 = ((f32[8,1,1024]{2,1,0:T(1,128)}), f32[8,1,1024]{2,1,0:T(1,128)S(1)}, u32[]{:S(2)}, u32[]{:S(2)}) async-start(f32[8,1,1024]{2,1,0:T(1,128)} %broadcast_in_dim.26), calls=%async_computation.1 | async-start | bytes 65536 | tf_op jit(solution)/shard_map/all_to_all | solution.py:26
  47.7 0.0 collective-permute-done.4.other
  47.7 25.8 %all-gather.3.cloned.1.call-done = bf16[32,128,1024]{2,1,0:T(8,128)(2,1)} async-done(((bf16[2,128,1024]{2,1,0:T(8,128)(2,1)}), bf16[32,128,1024]{2,1,0:T(8,128)(2,1)}) %all-gather.3.cloned.1.call-update) | async-done | bytes 8388624 | tf_op jit(solution)/shard_map/all_gather | solution.py:227
  73.5 0.0 copy-done
  73.5 11.0 %gram.1 = (bf16[2,2048,1024]{2,1,0:T(8,128)(2,1)}, bf16[2,256,1024]{2,1,0:T(8,128)(2,1)S(1)}, bf16[8,2,32,2048]{3,2,1,0:T(8,128)(2,1)S(1)}) custom-call(f32[2,1024]{1,0:T(2,128)S(1)} %get-tuple-element.25.mean, f32[2,1024]{1,0:T(2,128)S(1)} %fusion.4.rstd.refs_1_, bf16[16,2,128,1024]{3,2,1,0:T(8,128)(2,1)} %bitcast.27, bf16[2,128,1024]{2,1,0:T(8,128)(2,1)S(1)} %copy-done, ...), custom_call_target="tpu_custom_call" | custom-call | tf_op jit(solution)/shard_map/gram/pallas_call | solution.py:63
  84.5 0.0 copy-start.1
  84.5 1.4 copy-done.1
  85.9 0.0 all-to-all-done.1
  85.9 4.9 %all-to-all-start.2 = ((bf16[8,2,32,2048]{3,2,1,0:T(8,128)(2,1)}), bf16[8,2,32,2048]{3,2,1,0:T(8,128)(2,1)S(1)}, u32[]{:S(2)}, u32[]{:S(2)}) async-start(bf16[8,2,32,2048]{3,2,1,0:T(8,128)(2,1)} %copy-done.1), calls=%async_computation.2 | async-start | bytes 4194304 | tf_op jit(solution)/shard_map/all_to_all | solution.py:243
  90.8 0.6 multiply_reduce_fusion.1
  92.7 25.2 %all-to-all-done.2.refs_1_ = bf16[8,2,32,2048]{3,2,1,0:T(8,128)(2,1)S(1)} async-done(((bf16[8,2,32,2048]{3,2,1,0:T(8,128)(2,1)}), bf16[8,2,32,2048]{3,2,1,0:T(8,128)(2,1)S(1)}, u32[]{:S(2)}, u32[]{:S(2)}) %all-to-all-start.2) | async-done | bytes 2097184 | tf_op jit(solution)/shard_map/all_to_all | solution.py:243
  117.9 0.6 reduce.4
  118.5 33.4 %all_to_all.25.refs_0_.refs_1_ = bf16[8,2,32,2176]{3,2,1,0:T(8,128)(2,1)S(1)} all-to-all(bf16[8,2,32,2176]{3,2,1,0:T(8,128)(2,1)S(1)} %reduce.4), channel_id=1, replica_groups=mesh['z'=8,'yh'=2,'c'=2,'yl'=2,'x'=4] {'yl','x'}, dimensions={0} | all-to-all | bytes 4456448 | tf_op jit(solution)/shard_map/all_to_all | solution.py:245
  151.8 10.4 %products.1 = (f32[2,128,1024]{2,1,0:T(8,128)S(1)}, bf16[2,128,1024]{2,1,0:T(8,128)(2,1)S(1)}, f32[8,1024]{1,0:T(8,128)S(1)}) custom-call(bf16[8,2,32,2176]{3,2,1,0:T(8,128)(2,1)S(1)} %all_to_all.25.refs_0_.refs_1_, bf16[8,2,32,2176]{3,2,1,0:T(8,128)(2,1)S(1)} %all_to_all.25.refs_0_.refs_1_, bf16[2,2048,1024]{2,1,0:T(8,128)(2,1)} %get-tuple-element.13.refs_2_, ...), custom_call_target="tpu_custom_call" | custom-call | tf_op jit(solution)/shard_map/products/pallas_call | solution.py:163
  162.2 2.6 %collective-permute-start.5 = (f32[8,1024]{1,0:T(8,128)S(1)}, f32[8,1024]{1,0:T(8,128)S(1)}, u32[]{:S(2)}, u32[]{:S(2)}) collective-permute-start(f32[8,1024]{1,0:T(8,128)S(1)} %get-tuple-element.15), channel_id=1, source_target_pairs={{0,8},{8,0},{1,9},{9,1},{2,10},{10,2},{3,11},{11,3},{4,12},{12,4},... | collective-permute-start | bytes 98312 | tf_op jit(solution)/shard_map/ppermute | solution.py:20
  164.8 2.4 %collective-permute-start.7 = (bf16[2,128,1024]{2,1,0:T(8,128)(2,1)S(1)}, bf16[2,128,1024]{2,1,0:T(8,128)(2,1)S(1)}, u32[]{:S(2)}, u32[]{:S(2)}) collective-permute-start(bf16[2,128,1024]{2,1,0:T(8,128)(2,1)S(1)} %get-tuple-element.17), channel_id=1, source_target_pairs={{0,16},{16,0},{1,17},{17,1},{2,18},{18,2},{3,19},{19,3},{4,20},{20... | collective-permute-start | bytes 1572872 | tf_op jit(solution)/shard_map/ppermute | solution.py:248
  167.2 0.0 collective-permute-done.5
  167.2 0.8 collective-permute-start.6
  168.0 12.5 %collective-permute-done.6 = f32[8,1024]{1,0:T(8,128)S(1)} collective-permute-done((f32[8,1024]{1,0:T(8,128)S(1)}, f32[8,1024]{1,0:T(8,128)S(1)}, u32[]{:S(2)}, u32[]{:S(2)}) %collective-permute-start.6) | collective-permute-done | bytes 32800 | tf_op jit(solution)/shard_map/ppermute | solution.py:21
  180.6 13.9 %all_to_all.26.refs_0_ = f32[8,8,1024]{2,1,0:T(8,128)S(1)} all-to-all(f32[8,8,1024]{2,1,0:T(8,128)S(1)} %broadcast_in_dim.27), channel_id=1, replica_groups=mesh['z'=8,'yh'=2,'c'=2,'yl'=2,'x'=4] {'z'}, dimensions={0} | all-to-all | bytes 524288 | tf_op jit(solution)/shard_map/all_to_all | solution.py:26
  194.4 0.0 collective-permute-done.7.refs_3_
  194.4 1.0 finish.1
  (14 shorter events, 0.2 us)
Async XLA Ops:
  7.2 28.5 %copy-start.3 = (bf16[128,1024]{1,0:T(8,128)(2,1)S(1)}, bf16[128,1024]{1,0:T(8,128)(2,1)}, u32[]{:S(2)}) copy-start(bf16[128,1024]{1,0:T(8,128)(2,1)} %param.3) | copy-start | bytes 786436
  7.2 28.5 %copy-start.2 = (bf16[128,1024]{1,0:T(8,128)(2,1)S(1)}, bf16[128,1024]{1,0:T(8,128)(2,1)}, u32[]{:S(2)}) copy-start(bf16[128,1024]{1,0:T(8,128)(2,1)} %param.2) | copy-start | bytes 786436
  7.2 66.3 %all-gather.3.cloned.1.call-start = ((), (), s32[]{:S(2)}) async-start(), calls=%async_computation.5 | async-start | bytes 8912896 | tf_op jit(solution)/shard_map/all_gather | solution.py:227
  9.2 64.4 %copy-start = (bf16[2,128,1024]{2,1,0:T(8,128)(2,1)S(1)}, bf16[2,128,1024]{2,1,0:T(8,128)(2,1)}, u32[]{:S(2)}) copy-start(bf16[2,128,1024]{2,1,0:T(8,128)(2,1)} %pad_maximum_fusion.own) | copy-start | bytes 1572868
  10.5 4.2 %collective-permute-start = (f32[2,2,1024]{2,1,0:T(2,128)S(1)}, f32[2,2,1024]{2,1,0:T(2,128)S(1)}, u32[]{:S(2)}, u32[]{:S(2)}) collective-permute-start(f32[2,2,1024]{2,1,0:T(2,128)S(1)} %pad_maximum_fusion.1), channel_id=1, source_target_pairs={{0,8},{8,0},{1,9},{9,1},{2,10},{10,2},{3,11},{11,3},{4,12},{12,4},... | collective-permute-start | bytes 49160 | tf_op jit(solution)/shard_map/ppermute | solution.py:20
  14.7 4.2 %collective-permute-start.1 = (f32[2,2,1024]{2,1,0:T(2,128)S(1)}, f32[2,2,1024]{2,1,0:T(2,128)S(1)}, u32[]{:S(2)}, u32[]{:S(2)}) collective-permute-start(f32[2,2,1024]{2,1,0:T(2,128)S(1)} %fusion.6), channel_id=1, source_target_pairs={{0,16},{16,0},{1,17},{17,1},{2,18},{18,2},{3,19},{19,3},{4,20},{20... | collective-permute-start | bytes 49160 | tf_op jit(solution)/shard_map/ppermute | solution.py:21
  19.5 16.0 %all-to-all-start = ((f32[8,2,2,1024]{3,2,1,0:T(2,128)}), f32[8,2,2,1024]{3,2,1,0:T(2,128)S(1)}, u32[]{:S(2)}, u32[]{:S(2)}) async-start(f32[8,2,2,1024]{3,2,1,0:T(2,128)} %broadcast_in_dim.10), calls=%async_computation | async-start | bytes 262144 | tf_op jit(solution)/shard_map/all_to_all | solution.py:26
  26.0 21.7 %collective-permute-start.4 = (bf16[2,128,1024]{2,1,0:T(8,128)(2,1)}, bf16[2,128,1024]{2,1,0:T(8,128)(2,1)S(1)}, u32[]{:S(2)}, u32[]{:S(2)}) collective-permute-start(bf16[2,128,1024]{2,1,0:T(8,128)(2,1)} %pad_maximum_fusion.own), channel_id=1, source_target_pairs={{0,16},{16,0},{1,17},{17,1},{2,18},{18,2},{3,19},{19,3},{4,20},{20... | collective-permute-start | bytes 1572872 | tf_op jit(solution)/shard_map/ppermute | solution.py:228
  35.8 3.9 %collective-permute-start.2 = (f32[1,1024]{1,0:T(1,128)S(1)}, f32[1,1024]{1,0:T(1,128)S(1)}, u32[]{:S(2)}, u32[]{:S(2)}) collective-permute-start(f32[1,1024]{1,0:T(1,128)S(1)} %bitcast.38), channel_id=1, source_target_pairs={{0,8},{8,0},{1,9},{9,1},{2,10},{10,2},{3,11},{11,3},{4,12},{12,4},... | collective-permute-start | bytes 12296 | tf_op jit(solution)/shard_map/ppermute | solution.py:20
  39.7 4.0 %collective-permute-start.3 = (f32[1,1024]{1,0:T(1,128)S(1)}, f32[1,1024]{1,0:T(1,128)S(1)}, u32[]{:S(2)}, u32[]{:S(2)}) collective-permute-start(f32[1,1024]{1,0:T(1,128)S(1)} %add.28), channel_id=1, source_target_pairs={{0,16},{16,0},{1,17},{17,1},{2,18},{18,2},{3,19},{19,3},{4,20},{20... | collective-permute-start | bytes 12296 | tf_op jit(solution)/shard_map/ppermute | solution.py:21
  44.3 41.6 %all-to-all-start.1 = ((f32[8,1,1024]{2,1,0:T(1,128)}), f32[8,1,1024]{2,1,0:T(1,128)S(1)}, u32[]{:S(2)}, u32[]{:S(2)}) async-start(f32[8,1,1024]{2,1,0:T(1,128)} %broadcast_in_dim.26), calls=%async_computation.1 | async-start | bytes 65536 | tf_op jit(solution)/shard_map/all_to_all | solution.py:26
  84.5 1.4 copy-start.1
  85.9 32.0 %all-to-all-start.2 = ((bf16[8,2,32,2048]{3,2,1,0:T(8,128)(2,1)}), bf16[8,2,32,2048]{3,2,1,0:T(8,128)(2,1)S(1)}, u32[]{:S(2)}, u32[]{:S(2)}) async-start(bf16[8,2,32,2048]{3,2,1,0:T(8,128)(2,1)} %copy-done.1), calls=%async_computation.2 | async-start | bytes 4194304 | tf_op jit(solution)/shard_map/all_to_all | solution.py:243
  162.2 5.0 %collective-permute-start.5 = (f32[8,1024]{1,0:T(8,128)S(1)}, f32[8,1024]{1,0:T(8,128)S(1)}, u32[]{:S(2)}, u32[]{:S(2)}) collective-permute-start(f32[8,1024]{1,0:T(8,128)S(1)} %get-tuple-element.15), channel_id=1, source_target_pairs={{0,8},{8,0},{1,9},{9,1},{2,10},{10,2},{3,11},{11,3},{4,12},{12,4},... | collective-permute-start | bytes 98312 | tf_op jit(solution)/shard_map/ppermute | solution.py:20
  164.8 29.6 %collective-permute-start.7 = (bf16[2,128,1024]{2,1,0:T(8,128)(2,1)S(1)}, bf16[2,128,1024]{2,1,0:T(8,128)(2,1)S(1)}, u32[]{:S(2)}, u32[]{:S(2)}) collective-permute-start(bf16[2,128,1024]{2,1,0:T(8,128)(2,1)S(1)} %get-tuple-element.17), channel_id=1, source_target_pairs={{0,16},{16,0},{1,17},{17,1},{2,18},{18,2},{3,19},{19,3},{4,20},{20... | collective-permute-start | bytes 1572872 | tf_op jit(solution)/shard_map/ppermute | solution.py:248
  167.2 13.3 %collective-permute-start.6 = (f32[8,1024]{1,0:T(8,128)S(1)}, f32[8,1024]{1,0:T(8,128)S(1)}, u32[]{:S(2)}, u32[]{:S(2)}) collective-permute-start(f32[8,1024]{1,0:T(8,128)S(1)} %add.30), channel_id=1, source_target_pairs={{0,16},{16,0},{1,17},{17,1},{2,18},{18,2},{3,19},{19,3},{4,20},{20... | collective-permute-start | bytes 98312 | tf_op jit(solution)/shard_map/ppermute | solution.py:21
Sparse Core Ops, SparseCore 0:
  9.8 63.6 all-gather.2

commit v3 on v2

v3 whole, which is shorter than its diff:
```python
import jax
import jax.numpy as jnp
from jax import lax
from jax.experimental import pallas as pl
from jax.experimental.pallas import tpu as pltpu
from jax.sharding import Mesh, PartitionSpec as P

WIDTH = 8192

redund_weight = 0.0051
eps_var = 1e-05

ROWS = ("z", "yh", "c")
FEAT = ("yl", "x")
SWAP = [(0, 1), (1, 0)]
LIMIT = 40 * 1024 * 1024
VMEM = pl.BlockSpec(memory_space=pltpu.VMEM)
ANY = pl.BlockSpec(memory_space=pl.ANY)


def pair_sum(values):
    values = values + lax.ppermute(values, "c", SWAP)
    return values + lax.ppermute(values, "yh", SWAP)


def spread(values):
    count = lax.axis_size("z")
    return lax.all_to_all(jnp.broadcast_to(values[None], (count,) + values.shape), "z", 0, 0)


def batch_sum(values):
    return jnp.sum(spread(pair_sum(values)), 0)


def standardize(values, mean, rstd):
    return ((values.astype(jnp.float32) - mean) * rstd).astype(jnp.bfloat16)


def start_kernel(view_a, view_b, both, moments):
    for v, view in enumerate((view_a, view_b)):
        values = view[...]
        both[v] = values
        floats = values.astype(jnp.float32)
        moments[v : v + 1] = jnp.sum(floats, 0, keepdims=True)
        moments[v + 2 : v + 3] = jnp.sum(floats * floats, 0, keepdims=True)


def start(view_a, view_b):
    return pl.pallas_call(
        start_kernel,
        in_specs=[VMEM] * 2,
        out_specs=[VMEM] * 2,
        out_shape=[
            jax.ShapeDtypeStruct((2,) + view_a.shape, view_a.dtype),
            jax.ShapeDtypeStruct((4, view_a.shape[1]), jnp.float32),
        ],
        compiler_params=pltpu.CompilerParams(vmem_limit_bytes=LIMIT),
        name="start",
    )(view_a, view_b)


def gram_kernel(step, mean, rstd, own, other, source, cols, rows, parts, raw, sems):
    blocks, _, count, _ = raw.shape
    piece = parts.shape[2]
    copies = [
        pltpu.make_async_copy(source.at[pl.ds(k, step)], raw.at[pl.ds(k, step)], sems.at[k // step])
        for k in range(0, blocks, step)
    ]
    for copy in copies:
        copy.start()
    for v in range(2):
        rows[v, :count] = standardize(own[v], mean[v : v + 1], rstd[v : v + 1])
        rows[v, count:] = standardize(other[v], mean[v : v + 1], rstd[v : v + 1])
    for n, copy in enumerate(copies):
        copy.wait()
        first, last = n * step * count, (n + 1) * step * count
        for v in range(2):
            for k in range(n * step, (n + 1) * step):
                cols[v, k * count : (k + 1) * count] = standardize(
                    raw[k, v], mean[v : v + 1], rstd[v : v + 1]
                )
            gram = lax.dot_general(
                cols[v, first:last],
                rows[v],
                (((1,), (1,)), ((), ())),
                preferred_element_type=jnp.float32,
            )
            parts[first // piece : last // piece, v] = gram.astype(jnp.bfloat16).reshape(
                (last - first) // piece, piece, 2 * count
            )


def gram_parts(mean, rstd, gathered, own, other, feats):
    blocks, _, count, width = gathered.shape
    step = 4
    return pl.pallas_call(
        lambda *refs: gram_kernel(step, *refs),
        in_specs=[VMEM] * 4 + [ANY],
        out_specs=[VMEM] * 3,
        out_shape=[
            jax.ShapeDtypeStruct((2, blocks * count, width), jnp.bfloat16),
            jax.ShapeDtypeStruct((2, 2 * count, width), jnp.bfloat16),
            jax.ShapeDtypeStruct((feats, 2, blocks * count // feats, 2 * count), jnp.bfloat16),
        ],
        scratch_shapes=[
            pltpu.VMEM(gathered.shape, jnp.bfloat16),
            pltpu.SemaphoreType.DMA((blocks // step,)),
        ],
        compiler_params=pltpu.CompilerParams(vmem_limit_bytes=LIMIT),
        name="gram",
    )(mean, rstd, own, other, gathered)


def reduce_kernel(weight, diag, pieces, sent):
    feats, _, piece, row_count = pieces.shape
    total = []
    for v in range(2):
        total.append(pieces[0, v].astype(jnp.float32))
        for w in range(1, feats):
            total[v] = total[v] + pieces[w, v].astype(jnp.float32)
    frob = jnp.sum(total[0] * total[1], keepdims=True)
    part = jnp.broadcast_to(diag[...] + weight * frob, (16, piece))
    high = part.astype(jnp.bfloat16).astype(jnp.float32)
    middle = (part - high).astype(jnp.bfloat16).astype(jnp.float32)
    low = part - high - middle
    lane = lax.broadcasted_iota(jnp.int32, part.shape, 1)
    extra = jnp.where(lane == 0, high, jnp.where(lane == 1, middle, jnp.where(lane == 2, low, 0.0)))
    extra = extra.astype(jnp.bfloat16)
    for v in range(2):
        low_gram = total[v].T.astype(jnp.bfloat16)
        for w in range(feats):
            sent[w, v, :row_count] = low_gram
            sent[w, v, row_count:] = extra


def reduce_parts(pieces, diag, weight):
    feats, _, piece, row_count = pieces.shape
    return pl.pallas_call(
        lambda *refs: reduce_kernel(weight, *refs),
        in_specs=[VMEM] * 2,
        out_specs=VMEM,
        out_shape=jax.ShapeDtypeStruct((feats, 2, row_count + 16, piece), jnp.bfloat16),
        compiler_params=pltpu.CompilerParams(vmem_limit_bytes=LIMIT),
        name="reduce",
    )(diag, pieces)


def product_kernel(coupling, total_rows, full, cols, rows, diag_grad, mine, sent, sums):
    feats, _, _, piece = full.shape
    count = rows.shape[1] // 2
    width = cols.shape[2]
    chunk = 512
    for v in range(2):
        for f in range(0, width, chunk):
            here = slice(f, f + chunk)
            product = None
            for w in range(feats):
                term = jnp.dot(
                    full[w, 1 - v, : 2 * count],
                    cols[v, w * piece : (w + 1) * piece, here],
                    preferred_element_type=jnp.float32,
                )
                product = term if product is None else product + term
            product = coupling * product
            near = product[:count] + diag_grad[:, here] * (
                rows[1 - v, :count, here].astype(jnp.float32) * (1.0 / total_rows)
            )
            far = product[count:]
            mine[v, :, here] = near
            sent[v, :, here] = far.astype(jnp.bfloat16)
            plain = jnp.sum(near, 0, keepdims=True) + jnp.sum(far, 0, keepdims=True)
            cross = jnp.sum(
                near * rows[v, :count, here].astype(jnp.float32), 0, keepdims=True
            ) + jnp.sum(far * rows[v, count:, here].astype(jnp.float32), 0, keepdims=True)
            for k in range(chunk // 128):
                row = 2 * v * (width // 128) + f // 128 + k
                sums[row : row + 1] = plain[:, k * 128 : (k + 1) * 128]
                row += width // 128
                sums[row : row + 1] = cross[:, k * 128 : (k + 1) * 128]
    pieces = full[:, 0, 2 * count : 2 * count + 16, :128].astype(jnp.float32)
    loss = jnp.sum(pieces[:, 0:1, :].reshape(feats, 128), keepdims=True)
    last = 4 * (width // 128)
    sums[last : last + 8] = jnp.broadcast_to(loss, (8, 128))


def products(full, cols, rows, diag_grad, coupling, total_rows):
    _, _, width = cols.shape
    count = rows.shape[1] // 2
    return pl.pallas_call(
        lambda *refs: product_kernel(coupling, total_rows, *refs),
        in_specs=[VMEM] * 4,
        out_specs=[VMEM] * 3,
        out_shape=[
            jax.ShapeDtypeStruct((2, count, width), jnp.float32),
            jax.ShapeDtypeStruct((2, count, width), jnp.bfloat16),
            jax.ShapeDtypeStruct((4 * (width // 128) + 8, 128), jnp.float32),
        ],
        compiler_params=pltpu.CompilerParams(vmem_limit_bytes=LIMIT),
        name="products",
    )(full, cols, rows, diag_grad)


def final_kernel(scale, total_rows, parts, rstd, mine, received, rows, grad_a, grad_b, loss):
    total = parts[0]
    for k in range(1, parts.shape[0]):
        total = total + parts[k]
    total = total * (1.0 / total_rows)
    _, count, width = mine.shape
    lanes = width // 128
    for v, out in ((0, grad_a), (1, grad_b)):
        for k in range(lanes):
            here = slice(k * 128, (k + 1) * 128)
            plain = 2 * v * lanes + k
            cross = plain + lanes
            out[:, here] = (
                (scale * rstd[v : v + 1, here])
                * (
                    mine[v, :, here]
                    + received[v, :, here].astype(jnp.float32)
                    - total[plain : plain + 1]
                    - rows[v, :count, here].astype(jnp.float32) * total[cross : cross + 1]
                )
            ).astype(jnp.bfloat16)
    loss[...] = total[4 * lanes : 4 * lanes + 1] * total_rows


def finish(parts, rstd, mine, received, rows, scale, total_rows):
    _, count, width = mine.shape
    return pl.pallas_call(
        lambda *refs: final_kernel(scale, total_rows, *refs),
        in_specs=[VMEM] * 5,
        out_specs=[VMEM] * 3,
        out_shape=[
            jax.ShapeDtypeStruct((count, width), jnp.bfloat16),
            jax.ShapeDtypeStruct((count, width), jnp.bfloat16),
            jax.ShapeDtypeStruct((1, 128), jnp.float32),
        ],
        compiler_params=pltpu.CompilerParams(vmem_limit_bytes=LIMIT),
        name="finish",
    )(parts, rstd, mine, received, rows)


def shards(view_a, view_b):
    row_count, _ = view_a.shape
    batch_total = row_count * lax.axis_size(ROWS)
    feats = lax.axis_size(FEAT)
    both, moments = start(view_a, view_b)
    gathered = lax.all_gather(both, ("z", "c"))
    other = lax.ppermute(both, "yh", SWAP)

    moments = batch_sum(moments)
    mean = moments[:2] / batch_total
    rstd = lax.rsqrt(moments[2:] / batch_total - mean * mean + eps_var)

    own_a = standardize(view_a, mean[0], rstd[0]).astype(jnp.float32)
    own_b = standardize(view_b, mean[1], rstd[1]).astype(jnp.float32)
    corr_diag = batch_sum(jnp.sum(own_a * own_b, 0)[None]) / batch_total
    diag_part = jnp.sum((1.0 - corr_diag) ** 2) - redund_weight * jnp.sum(corr_diag * corr_diag)
    diag_grad = -2.0 * (1.0 - corr_diag) - 2.0 * redund_weight * corr_diag
    diag_share = (diag_part / lax.axis_size(ROWS)).reshape(1, 1)

    cols, rows, parts = gram_parts(mean, rstd, gathered, both, other, feats)
    pieces = lax.all_to_all(parts, FEAT, 0, 0)
    sent = reduce_parts(pieces, diag_share, redund_weight / (batch_total * batch_total))
    full = lax.all_to_all(sent, FEAT, 0, 0)
    coupling = 2.0 * redund_weight / (batch_total * batch_total)
    mine, leaving, sums = products(full, cols, rows, diag_grad, coupling, batch_total)
    sums, leaving = lax.optimization_barrier((pair_sum(sums), leaving))
    received = lax.ppermute(leaving, "yh", SWAP)
    back = spread(sums)
    scale = batch_total * batch_total / (redund_weight * WIDTH)
    grad_a, grad_b, loss = finish(back, rstd, mine, received, rows, scale, batch_total)
    return grad_a, grad_b, loss[0, 0]


def solution(mesh):
    fine = Mesh(mesh.devices.reshape(8, 2, 2, 2, 4), ROWS + FEAT)
    return jax.shard_map(
        shards,
        mesh=fine,
        in_specs=(P(ROWS, FEAT), P(ROWS, FEAT)),
        out_specs=(P(ROWS, FEAT), P(ROWS, FEAT), P()),
        check_vma=False,
    )
```

time: 204 us -> 185 us (0.907)
  Pallas kernels: 22.9 us -> 11.1 us
  waiting for transfers between devices: 75.7 us -> 65.4 us
  local copies, waits for them, and re-layouts: 2.74 us -> 7.82 us
  other arithmetic: 4.12 us -> 1.91 us
    ppermute x3, waiting for transfers between devices: 16.5 us -> 5.68 us  [pair_sum(): return values + lax.ppermute(values, 'yh', SWAP)]
    pallas_call x1, Pallas kernels: 10.4 us -> 2.56 us  [products(): pl.pallas_call(lambda *refs: product_kernel(coupling, total_rows, *refs),...]
    unnamed x8 -> x10, local copies, waits for them, and re-layouts: 1.38 us -> 6.49 us
    pallas_call x3 -> x4, Pallas kernels: 12.6 us -> 8.52 us  [the longest x1 5.9 us: gram_parts(): pl.pallas_call(lambda *refs: gram_kernel(step, *refs), in_specs=[VMEM] *...]
  transfers between devices with their start and end apart: 12 -> 12, of which waited for: 8 -> 9; matrix products, arithmetic and copies ran while one was open for 2% -> 2% of each run, Pallas kernels for 5% -> 3%
where the time goes in v3:
time: 185 us; the launch traced here: 183 us
  waiting for transfers between devices  65.4 us (35%)
  blocking collectives  45.7 us (25%)
  starting transfers between devices  36 us (19%)
  between operations  15.4 us (8%)
  Pallas kernels  11.1 us (6%)
  local copies, waits for them, and re-layouts  7.82 us (4%)
  other arithmetic  1.91 us (1%)
    all_to_all x1, blocking collectives, shards(): full = lax.all_to_all(sent, FEAT, 0, 0)  33.5 us
    all_gather x1, waiting for transfers between devices, shards(): gathered = lax.all_gather(both, ('z', 'c'))  25.9 us
    all_to_all x1, waiting for transfers between devices, shards(): pieces = lax.all_to_all(parts, FEAT, 0, 0)  25.2 us
    all_to_all x1, blocking collectives, spread(): lax.all_to_all(jnp.broadcast_to(values[None], (count,) + values.shape), '...  12.2 us
    all_to_all x2, starting transfers between devices, spread(): lax.all_to_all(jnp.broadcast_to(values[None], (count,) + values.shape), '...  9.79 us
    ppermute x3, starting transfers between devices, pair_sum(): values = values + lax.ppermute(values, 'c', SWAP)  9.33 us
    ppermute x3, starting transfers between devices, pair_sum(): return values + lax.ppermute(values, 'yh', SWAP)  6.56 us
    unnamed x10, local copies, waits for them, and re-layouts  6.49 us
  transfers between devices with their start and end apart: 12, of which 9 were waited for; matrix products, arithmetic and copies ran while one was open for 2% of the time, Pallas kernels for 3%

profile of v3, /device:TPU:1, one launch (start us, length us, event | category | flops | bytes accessed | tf_op | source)
XLA Modules:
  0.0 183.3 jit_solution(14324944666556587569)
XLA Ops:
  7.2 0.0 all-gather.3.cloned.1.call-start
  7.2 0.0 copy-start.3
  7.2 0.9 copy-done.3
  8.2 0.0 copy-start.4
  8.2 0.9 copy-done.4
  9.1 0.9 start.1
  10.0 0.0 all-gather.3.cloned.1.call-update
  10.0 3.3 %collective-permute-start = (f32[4,1024]{1,0:T(4,128)S(1)}, f32[4,1024]{1,0:T(4,128)S(1)}, u32[]{:S(2)}, u32[]{:S(2)}) collective-permute-start(f32[4,1024]{1,0:T(4,128)S(1)} %get-tuple-element.16), channel_id=1, source_target_pairs={{0,8},{8,0},{1,9},{9,1},{2,10},{10,2},{3,11},{11,3},{4,12},{12,4},... | collective-permute-start | bytes 49160 | tf_op jit(solution)/shard_map/ppermute | solution.py:22
  13.3 0.8 collective-permute-done
  14.2 1.2 collective-permute-start.1
  15.4 2.9 %collective-permute-done.1 = f32[4,1024]{1,0:T(4,128)S(1)} collective-permute-done((f32[4,1024]{1,0:T(4,128)S(1)}, f32[4,1024]{1,0:T(4,128)S(1)}, u32[]{:S(2)}, u32[]{:S(2)}) %collective-permute-start.1) | collective-permute-done | bytes 16416 | tf_op jit(solution)/shard_map/ppermute | solution.py:23
  18.3 0.7 broadcast_in_dim.10
  19.0 6.5 %all-to-all-start = ((f32[8,4,1024]{2,1,0:T(4,128)}), f32[8,4,1024]{2,1,0:T(4,128)S(1)}, u32[]{:S(2)}, u32[]{:S(2)}) async-start(f32[8,4,1024]{2,1,0:T(4,128)} %broadcast_in_dim.10), calls=%async_computation | async-start | bytes 262144 | tf_op jit(solution)/shard_map/all_to_all | solution.py:28
  25.4 2.9 %collective-permute-start.4 = (bf16[2,128,1024]{2,1,0:T(8,128)(2,1)}, bf16[2,128,1024]{2,1,0:T(8,128)(2,1)S(1)}, u32[]{:S(2)}, u32[]{:S(2)}) collective-permute-start(bf16[2,128,1024]{2,1,0:T(8,128)(2,1)} %get-tuple-element.17.refs_2_), channel_id=1, source_target_pairs={{0,16},{16,0},{1,17},{17,1},{2,18},{18,2},{3,19},{19,3},{4,20},{20... | collective-permute-start | bytes 1572872 | tf_op jit(solution)/shard_map/ppermute | solution.py:249
  28.3 6.2 %all-to-all-done = f32[8,4,1024]{2,1,0:T(4,128)S(1)} async-done(((f32[8,4,1024]{2,1,0:T(4,128)}), f32[8,4,1024]{2,1,0:T(4,128)S(1)}, u32[]{:S(2)}, u32[]{:S(2)}) %all-to-all-start) | async-done | bytes 131104 | tf_op jit(solution)/shard_map/all_to_all | solution.py:28
  34.6 1.2 multiply_reduce_fusion
  35.8 3.3 %collective-permute-start.2 = (f32[1,1024]{1,0:T(1,128)S(1)}, f32[1,1024]{1,0:T(1,128)S(1)}, u32[]{:S(2)}, u32[]{:S(2)}) collective-permute-start(f32[1,1024]{1,0:T(1,128)S(1)} %bitcast.13), channel_id=1, source_target_pairs={{0,8},{8,0},{1,9},{9,1},{2,10},{10,2},{3,11},{11,3},{4,12},{12,4},... | collective-permute-start | bytes 12296 | tf_op jit(solution)/shard_map/ppermute | solution.py:22
  39.1 0.8 collective-permute-done.2
  39.9 2.9 %collective-permute-start.3 = (f32[1,1024]{1,0:T(1,128)S(1)}, f32[1,1024]{1,0:T(1,128)S(1)}, u32[]{:S(2)}, u32[]{:S(2)}) collective-permute-start(f32[1,1024]{1,0:T(1,128)S(1)} %add.28), channel_id=1, source_target_pairs={{0,16},{16,0},{1,17},{17,1},{2,18},{18,2},{3,19},{19,3},{4,20},{20... | collective-permute-start | bytes 12296 | tf_op jit(solution)/shard_map/ppermute | solution.py:23
  42.9 1.1 collective-permute-done.3
  44.0 0.6 broadcast_in_dim.26
  44.6 3.3 %all-to-all-start.1 = ((f32[8,1,1024]{2,1,0:T(1,128)}), f32[8,1,1024]{2,1,0:T(1,128)S(1)}, u32[]{:S(2)}, u32[]{:S(2)}) async-start(f32[8,1,1024]{2,1,0:T(1,128)} %broadcast_in_dim.26), calls=%async_computation.1 | async-start | bytes 65536 | tf_op jit(solution)/shard_map/all_to_all | solution.py:28
  47.9 0.0 collective-permute-done.4.refs_3_
  48.0 25.9 %all-gather.3.cloned.1.call-done = bf16[32,128,1024]{2,1,0:T(8,128)(2,1)} async-done(((bf16[2,128,1024]{2,1,0:T(8,128)(2,1)}), bf16[32,128,1024]{2,1,0:T(8,128)(2,1)}) %all-gather.3.cloned.1.call-update) | async-done | bytes 8388624 | tf_op jit(solution)/shard_map/all_gather | solution.py:248
  73.8 5.9 %gram.1 = (bf16[2,2048,1024]{2,1,0:T(8,128)(2,1)S(1)}, bf16[2,256,1024]{2,1,0:T(8,128)(2,1)S(1)}, bf16[8,2,256,256]{3,2,1,0:T(8,128)(2,1)S(1)}) custom-call(f32[2,1024]{1,0:T(2,128)S(1)} %get-tuple-element.31.refs_0_, f32[2,1024]{1,0:T(2,128)S(1)} %get-tuple-element.32.refs_1_, bf16[2,128,1024]{2,1,0:T(8,128)(2,1)} %get-tuple-element.17.refs_2_, ...), custom_call_target="tpu_custom_call" | custom-call | tf_op jit(solution)/shard_map/gram/pallas_call | solution.py:96
  79.7 0.0 copy-start
  79.7 3.2 %copy-done = bf16[2,2048,1024]{2,1,0:T(8,128)(2,1)} copy-done((bf16[2,2048,1024]{2,1,0:T(8,128)(2,1)}, bf16[2,2048,1024]{2,1,0:T(8,128)(2,1)S(1)}, u32[]{:S(2)}) %copy-start) | copy-done | bytes 8388632
  82.9 0.0 copy-start.2
  82.9 1.4 copy-done.2
  84.3 0.0 all-to-all-done.1
  84.3 4.9 %all-to-all-start.2 = ((bf16[8,2,256,256]{3,2,1,0:T(8,128)(2,1)}), bf16[8,2,256,256]{3,2,1,0:T(8,128)(2,1)S(1)}, u32[]{:S(2)}, u32[]{:S(2)}) async-start(bf16[8,2,256,256]{3,2,1,0:T(8,128)(2,1)} %copy-done.2), calls=%async_computation.2 | async-start | bytes 4194304 | tf_op jit(solution)/shard_map/all_to_all | solution.py:263
  89.2 0.6 multiply_reduce_fusion.1
  91.2 25.2 %all-to-all-done.2.refs_1_ = bf16[8,2,256,256]{3,2,1,0:T(8,128)(2,1)S(1)} async-done(((bf16[8,2,256,256]{3,2,1,0:T(8,128)(2,1)}), bf16[8,2,256,256]{3,2,1,0:T(8,128)(2,1)S(1)}, u32[]{:S(2)}, u32[]{:S(2)}) %all-to-all-start.2) | async-done | bytes 2097184 | tf_op jit(solution)/shard_map/all_to_all | solution.py:263
  116.3 0.0 copy-start.1
  116.3 0.7 reduce.4
  117.1 33.5 %all_to_all.25.refs_0_ = bf16[8,2,272,256]{3,2,1,0:T(8,128)(2,1)S(1)} all-to-all(bf16[8,2,272,256]{3,2,1,0:T(8,128)(2,1)S(1)} %reduce.4), channel_id=1, replica_groups=mesh['z'=8,'yh'=2,'c'=2,'yl'=2,'x'=4] {'yl','x'}, dimensions={0} | all-to-all | bytes 4456448 | tf_op jit(solution)/shard_map/all_to_all | solution.py:265
  150.6 0.0 copy-done.1
  150.6 2.6 %products.1 = (f32[2,128,1024]{2,1,0:T(8,128)S(1)}, bf16[2,128,1024]{2,1,0:T(8,128)(2,1)S(1)}, f32[40,128]{1,0:T(8,128)S(1)}) custom-call(bf16[8,2,272,256]{3,2,1,0:T(8,128)(2,1)S(1)} %all_to_all.25.refs_0_, bf16[2,2048,1024]{2,1,0:T(8,128)(2,1)S(1)} %copy-done.1, bf16[2,256,1024]{2,1,0:T(8,128)(2,1)S(1)} %get-tuple-element.20.refs_2_.refs_4_, ...), custom_call_target="tpu_custom_call" | custom-call | tf_op jit(solution)/shard_map/products/pallas_call | solution.py:189
  153.2 2.7 %collective-permute-start.5 = (f32[40,128]{1,0:T(8,128)S(1)}, f32[40,128]{1,0:T(8,128)S(1)}, u32[]{:S(2)}, u32[]{:S(2)}) collective-permute-start(f32[40,128]{1,0:T(8,128)S(1)} %get-tuple-element.21), channel_id=1, source_target_pairs={{0,8},{8,0},{1,9},{9,1},{2,10},{10,2},{3,11},{11,3},{4,12},{12,4},... | collective-permute-start | bytes 61448 | tf_op jit(solution)/shard_map/ppermute | solution.py:22
  155.8 0.8 collective-permute-done.5
  156.7 2.4 %collective-permute-start.6 = (f32[40,128]{1,0:T(8,128)S(1)}, f32[40,128]{1,0:T(8,128)S(1)}, u32[]{:S(2)}, u32[]{:S(2)}) collective-permute-start(f32[40,128]{1,0:T(8,128)S(1)} %add.30), channel_id=1, source_target_pairs={{0,16},{16,0},{1,17},{17,1},{2,18},{18,2},{3,19},{19,3},{4,20},{20... | collective-permute-start | bytes 61448 | tf_op jit(solution)/shard_map/ppermute | solution.py:23
  159.1 1.7 collective-permute-done.6
  160.8 2.4 %collective-permute-start.7 = (bf16[2,128,1024]{2,1,0:T(8,128)(2,1)S(1)}, bf16[2,128,1024]{2,1,0:T(8,128)(2,1)S(1)}, u32[]{:S(2)}, u32[]{:S(2)}) collective-permute-start(bf16[2,128,1024]{2,1,0:T(8,128)(2,1)S(1)} %get-tuple-element.25), channel_id=1, source_target_pairs={{0,16},{16,0},{1,17},{17,1},{2,18},{18,2},{3,19},{19,3},{4,20},{20... | collective-permute-start | bytes 1572872 | tf_op jit(solution)/shard_map/ppermute | solution.py:269
  163.3 12.2 %all_to_all.26.refs_0_ = f32[8,40,128]{2,1,0:T(8,128)S(1)} all-to-all(f32[8,40,128]{2,1,0:T(8,128)S(1)} %broadcast_in_dim.27), channel_id=1, replica_groups=mesh['z'=8,'yh'=2,'c'=2,'yl'=2,'x'=4] {'z'}, dimensions={0} | all-to-all | bytes 327680 | tf_op jit(solution)/shard_map/all_to_all | solution.py:28
  175.5 0.0 collective-permute-done.7.refs_3_
  175.5 1.0 finish.1
  (11 shorter events, 0.1 us)
Async XLA Ops:
  7.2 66.6 %all-gather.3.cloned.1.call-start = ((), (), s32[]{:S(2)}) async-start(), calls=%async_computation.5 | async-start | bytes 8912896 | tf_op jit(solution)/shard_map/all_gather | solution.py:248
  7.2 1.0 copy-start.3
  8.2 0.9 copy-start.4
  10.0 4.2 %collective-permute-start = (f32[4,1024]{1,0:T(4,128)S(1)}, f32[4,1024]{1,0:T(4,128)S(1)}, u32[]{:S(2)}, u32[]{:S(2)}) collective-permute-start(f32[4,1024]{1,0:T(4,128)S(1)} %get-tuple-element.16), channel_id=1, source_target_pairs={{0,8},{8,0},{1,9},{9,1},{2,10},{10,2},{3,11},{11,3},{4,12},{12,4},... | collective-permute-start | bytes 49160 | tf_op jit(solution)/shard_map/ppermute | solution.py:22
  14.2 4.1 %collective-permute-start.1 = (f32[4,1024]{1,0:T(4,128)S(1)}, f32[4,1024]{1,0:T(4,128)S(1)}, u32[]{:S(2)}, u32[]{:S(2)}) collective-permute-start(f32[4,1024]{1,0:T(4,128)S(1)} %add.24), channel_id=1, source_target_pairs={{0,16},{16,0},{1,17},{17,1},{2,18},{18,2},{3,19},{19,3},{4,20},{20... | collective-permute-start | bytes 49160 | tf_op jit(solution)/shard_map/ppermute | solution.py:23
  19.0 15.5 %all-to-all-start = ((f32[8,4,1024]{2,1,0:T(4,128)}), f32[8,4,1024]{2,1,0:T(4,128)S(1)}, u32[]{:S(2)}, u32[]{:S(2)}) async-start(f32[8,4,1024]{2,1,0:T(4,128)} %broadcast_in_dim.10), calls=%async_computation | async-start | bytes 262144 | tf_op jit(solution)/shard_map/all_to_all | solution.py:28
  25.4 22.5 %collective-permute-start.4 = (bf16[2,128,1024]{2,1,0:T(8,128)(2,1)}, bf16[2,128,1024]{2,1,0:T(8,128)(2,1)S(1)}, u32[]{:S(2)}, u32[]{:S(2)}) collective-permute-start(bf16[2,128,1024]{2,1,0:T(8,128)(2,1)} %get-tuple-element.17.refs_2_), channel_id=1, source_target_pairs={{0,16},{16,0},{1,17},{17,1},{2,18},{18,2},{3,19},{19,3},{4,20},{20... | collective-permute-start | bytes 1572872 | tf_op jit(solution)/shard_map/ppermute | solution.py:249
  35.8 4.2 %collective-permute-start.2 = (f32[1,1024]{1,0:T(1,128)S(1)}, f32[1,1024]{1,0:T(1,128)S(1)}, u32[]{:S(2)}, u32[]{:S(2)}) collective-permute-start(f32[1,1024]{1,0:T(1,128)S(1)} %bitcast.13), channel_id=1, source_target_pairs={{0,8},{8,0},{1,9},{9,1},{2,10},{10,2},{3,11},{11,3},{4,12},{12,4},... | collective-permute-start | bytes 12296 | tf_op jit(solution)/shard_map/ppermute | solution.py:22
  39.9 4.0 %collective-permute-start.3 = (f32[1,1024]{1,0:T(1,128)S(1)}, f32[1,1024]{1,0:T(1,128)S(1)}, u32[]{:S(2)}, u32[]{:S(2)}) collective-permute-start(f32[1,1024]{1,0:T(1,128)S(1)} %add.28), channel_id=1, source_target_pairs={{0,16},{16,0},{1,17},{17,1},{2,18},{18,2},{3,19},{19,3},{4,20},{20... | collective-permute-start | bytes 12296 | tf_op jit(solution)/shard_map/ppermute | solution.py:23
  44.6 39.7 %all-to-all-start.1 = ((f32[8,1,1024]{2,1,0:T(1,128)}), f32[8,1,1024]{2,1,0:T(1,128)S(1)}, u32[]{:S(2)}, u32[]{:S(2)}) async-start(f32[8,1,1024]{2,1,0:T(1,128)} %broadcast_in_dim.26), calls=%async_computation.1 | async-start | bytes 65536 | tf_op jit(solution)/shard_map/all_to_all | solution.py:28
  79.7 3.2 %copy-start = (bf16[2,2048,1024]{2,1,0:T(8,128)(2,1)}, bf16[2,2048,1024]{2,1,0:T(8,128)(2,1)S(1)}, u32[]{:S(2)}) copy-start(bf16[2,2048,1024]{2,1,0:T(8,128)(2,1)S(1)} %get-tuple-element.19.refs_1_) | copy-start | bytes 25165828
  82.9 1.4 copy-start.2
  84.3 32.0 %all-to-all-start.2 = ((bf16[8,2,256,256]{3,2,1,0:T(8,128)(2,1)}), bf16[8,2,256,256]{3,2,1,0:T(8,128)(2,1)S(1)}, u32[]{:S(2)}, u32[]{:S(2)}) async-start(bf16[8,2,256,256]{3,2,1,0:T(8,128)(2,1)} %copy-done.2), calls=%async_computation.2 | async-start | bytes 4194304 | tf_op jit(solution)/shard_map/all_to_all | solution.py:263
  116.3 34.3 %copy-start.1 = (bf16[2,2048,1024]{2,1,0:T(8,128)(2,1)S(1)}, bf16[2,2048,1024]{2,1,0:T(8,128)(2,1)}, u32[]{:S(2)}) copy-start(bf16[2,2048,1024]{2,1,0:T(8,128)(2,1)} %copy-done) | copy-start | bytes 25165828
  153.2 3.5 %collective-permute-start.5 = (f32[40,128]{1,0:T(8,128)S(1)}, f32[40,128]{1,0:T(8,128)S(1)}, u32[]{:S(2)}, u32[]{:S(2)}) collective-permute-start(f32[40,128]{1,0:T(8,128)S(1)} %get-tuple-element.21), channel_id=1, source_target_pairs={{0,8},{8,0},{1,9},{9,1},{2,10},{10,2},{3,11},{11,3},{4,12},{12,4},... | collective-permute-start | bytes 61448 | tf_op jit(solution)/shard_map/ppermute | solution.py:22
  156.7 4.1 %collective-permute-start.6 = (f32[40,128]{1,0:T(8,128)S(1)}, f32[40,128]{1,0:T(8,128)S(1)}, u32[]{:S(2)}, u32[]{:S(2)}) collective-permute-start(f32[40,128]{1,0:T(8,128)S(1)} %add.30), channel_id=1, source_target_pairs={{0,16},{16,0},{1,17},{17,1},{2,18},{18,2},{3,19},{19,3},{4,20},{20... | collective-permute-start | bytes 61448 | tf_op jit(solution)/shard_map/ppermute | solution.py:23
  160.8 14.7 %collective-permute-start.7 = (bf16[2,128,1024]{2,1,0:T(8,128)(2,1)S(1)}, bf16[2,128,1024]{2,1,0:T(8,128)(2,1)S(1)}, u32[]{:S(2)}, u32[]{:S(2)}) collective-permute-start(bf16[2,128,1024]{2,1,0:T(8,128)(2,1)S(1)} %get-tuple-element.25), channel_id=1, source_target_pairs={{0,16},{16,0},{1,17},{17,1},{2,18},{18,2},{3,19},{19,3},{4,20},{20... | collective-permute-start | bytes 1572872 | tf_op jit(solution)/shard_map/ppermute | solution.py:269
Sparse Core Ops, SparseCore 0:
  10.1 63.6 all-gather.2

commit v4 on v3

--- a/solution.py
+++ b/solution.py
@@ -13,23 +13,23 @@
 ROWS = ("z", "yh", "c")
 FEAT = ("yl", "x")
 SWAP = [(0, 1), (1, 0)]
-LIMIT = 40 * 1024 * 1024
+LIMIT = 32 * 1024 * 1024
 VMEM = pl.BlockSpec(memory_space=pltpu.VMEM)
 ANY = pl.BlockSpec(memory_space=pl.ANY)
 
 
-def pair_sum(values):
-    values = values + lax.ppermute(values, "c", SWAP)
-    return values + lax.ppermute(values, "yh", SWAP)
+def partner(values, axis):
+    return lax.ppermute(values, axis, SWAP)
+
+
+def shift(values, steps):
+    count = lax.axis_size("z")
+    return lax.ppermute(values, "z", [(k, (k + steps) % count) for k in range(count)])
 
 
 def spread(values):
     count = lax.axis_size("z")
     return lax.all_to_all(jnp.broadcast_to(values[None], (count,) + values.shape), "z", 0, 0)
-
-
-def batch_sum(values):
-    return jnp.sum(spread(pair_sum(values)), 0)
 
 
 def standardize(values, mean, rstd):
@@ -59,67 +59,109 @@
     )(view_a, view_b)
 
 
-def gram_kernel(step, mean, rstd, own, other, source, cols, rows, parts, raw, sems):
-    blocks, _, count, _ = raw.shape
-    piece = parts.shape[2]
-    copies = [
-        pltpu.make_async_copy(source.at[pl.ds(k, step)], raw.at[pl.ds(k, step)], sems.at[k // step])
-        for k in range(0, blocks, step)
-    ]
-    for copy in copies:
-        copy.start()
+def moments_kernel(far, *refs):
+    before, *blocks = refs[:-1]
+    moments = refs[-1]
+    if far:
+        moments[...] = before[...] + blocks.pop(0)[...]
+    else:
+        moments[...] = before[...]
+    for block in blocks:
+        for v in range(2):
+            floats = block[v].astype(jnp.float32)
+            moments[v : v + 1] += jnp.sum(floats, 0, keepdims=True)
+            moments[v + 2 : v + 3] += jnp.sum(floats * floats, 0, keepdims=True)
+
+
+def add_moments(before, blocks, far=None):
+    given = [before] + ([] if far is None else [far]) + list(blocks)
+    return pl.pallas_call(
+        lambda *refs: moments_kernel(far is not None, *refs),
+        in_specs=[VMEM] * len(given),
+        out_specs=VMEM,
+        out_shape=jax.ShapeDtypeStruct(before.shape, jnp.float32),
+        compiler_params=pltpu.CompilerParams(vmem_limit_bytes=LIMIT),
+        name="moments",
+    )(*given)
+
+
+def gram_kernel(total_rows, near, far, own, other, *refs):
+    blocks = refs[:-5]
+    cols, rows, parts, cross, rstd = refs[-5:]
+    count = own.shape[1]
+    feats, _, piece, _ = parts.shape
+    sums = (near[...] + far[...]) * (1.0 / total_rows)
+    mean = sums[:2]
+    scale = lax.rsqrt(sums[2:] - mean * mean + eps_var)
+    rstd[...] = scale
     for v in range(2):
-        rows[v, :count] = standardize(own[v], mean[v : v + 1], rstd[v : v + 1])
-        rows[v, count:] = standardize(other[v], mean[v : v + 1], rstd[v : v + 1])
-    for n, copy in enumerate(copies):
-        copy.wait()
-        first, last = n * step * count, (n + 1) * step * count
+        rows[v, :count] = standardize(own[v], mean[v : v + 1], scale[v : v + 1])
+        rows[v, count:] = standardize(other[v], mean[v : v + 1], scale[v : v + 1])
+    products = jnp.zeros(cross.shape, jnp.float32)
+    flat = iter(blocks)
+    place = 0
+    while place < cols.shape[1]:
+        first = place
+        while place < first + 2 * piece:
+            pair = [next(flat)]
+            if pair[0].shape[0] == 1:
+                pair.append(next(flat))
+            values = [
+                standardize(pair[v if len(pair) == 2 else 0][v if len(pair) == 1 else 0],
+                            mean[v : v + 1], scale[v : v + 1])
+                for v in range(2)
+            ]
+            for v in range(2):
+                cols[v, place : place + count] = values[v]
+            products = products + jnp.sum(
+                values[0].astype(jnp.float32) * values[1].astype(jnp.float32), 0, keepdims=True
+            )
+            place += count
         for v in range(2):
-            for k in range(n * step, (n + 1) * step):
-                cols[v, k * count : (k + 1) * count] = standardize(
-                    raw[k, v], mean[v : v + 1], rstd[v : v + 1]
-                )
             gram = lax.dot_general(
-                cols[v, first:last],
+                cols[v, first:place],
                 rows[v],
                 (((1,), (1,)), ((), ())),
                 preferred_element_type=jnp.float32,
             )
-            parts[first // piece : last // piece, v] = gram.astype(jnp.bfloat16).reshape(
-                (last - first) // piece, piece, 2 * count
+            parts[first // piece : place // piece, v] = gram.astype(jnp.bfloat16).reshape(
+                2, piece, 2 * count
             )
-
-
-def gram_parts(mean, rstd, gathered, own, other, feats):
-    blocks, _, count, width = gathered.shape
-    step = 4
-    return pl.pallas_call(
-        lambda *refs: gram_kernel(step, *refs),
-        in_specs=[VMEM] * 4 + [ANY],
-        out_specs=[VMEM] * 3,
-        out_shape=[
-            jax.ShapeDtypeStruct((2, blocks * count, width), jnp.bfloat16),
+    cross[...] = products
+
+
+def gram_parts(near, far, own, other, blocks, feats, total_rows):
+    _, count, width = own.shape
+    panel = count * sum(block.shape[0] for block in blocks) // 2
+    return pl.pallas_call(
+        lambda *refs: gram_kernel(total_rows, *refs),
+        in_specs=[VMEM] * (4 + len(blocks)),
+        out_specs=[VMEM] * 5,
+        out_shape=[
+            jax.ShapeDtypeStruct((2, panel, width), jnp.bfloat16),
             jax.ShapeDtypeStruct((2, 2 * count, width), jnp.bfloat16),
-            jax.ShapeDtypeStruct((feats, 2, blocks * count // feats, 2 * count), jnp.bfloat16),
-        ],
-        scratch_shapes=[
-            pltpu.VMEM(gathered.shape, jnp.bfloat16),
-            pltpu.SemaphoreType.DMA((blocks // step,)),
+            jax.ShapeDtypeStruct((feats, 2, panel // feats, 2 * count), jnp.bfloat16),
+            jax.ShapeDtypeStruct((1, width), jnp.float32),
+            jax.ShapeDtypeStruct((2, width), jnp.float32),
         ],
         compiler_params=pltpu.CompilerParams(vmem_limit_bytes=LIMIT),
         name="gram",
-    )(mean, rstd, own, other, gathered)
-
-
-def reduce_kernel(weight, diag, pieces, sent):
+    )(near, far, own, other, *blocks)
+
+
+def reduce_kernel(weight, total_rows, share, near, far, pieces, sent, diag_grad):
     feats, _, piece, row_count = pieces.shape
+    corr = (near[...] + far[...]) * (1.0 / total_rows)
+    miss = 1.0 - corr
+    diag_grad[...] = -2.0 * miss - 2.0 * redund_weight * corr
+    diag = jnp.sum(miss * miss - redund_weight * (corr * corr), keepdims=True) * share
     total = []
     for v in range(2):
         total.append(pieces[0, v].astype(jnp.float32))
         for w in range(1, feats):
             total[v] = total[v] + pieces[w, v].astype(jnp.float32)
     frob = jnp.sum(total[0] * total[1], keepdims=True)
-    part = jnp.broadcast_to(diag[...] + weight * frob, (16, piece))
+    part = jnp.broadcast_to(diag + weight * frob, (16, piece))
     high = part.astype(jnp.bfloat16).astype(jnp.float32)
     middle = (part - high).astype(jnp.bfloat16).astype(jnp.float32)
     low = part - high - middle
@@ -133,16 +175,20 @@
             sent[w, v, row_count:] = extra
 
 
-def reduce_parts(pieces, diag, weight):
+def reduce_parts(near, far, pieces, total_rows, share):
     feats, _, piece, row_count = pieces.shape
-    return pl.pallas_call(
-        lambda *refs: reduce_kernel(weight, *refs),
-        in_specs=[VMEM] * 2,
-        out_specs=VMEM,
-        out_shape=jax.ShapeDtypeStruct((feats, 2, row_count + 16, piece), jnp.bfloat16),
+    weight = redund_weight / (total_rows * total_rows)
+    return pl.pallas_call(
+        lambda *refs: reduce_kernel(weight, total_rows, share, *refs),
+        in_specs=[VMEM] * 3,
+        out_specs=[VMEM] * 2,
+        out_shape=[
+            jax.ShapeDtypeStruct((feats, 2, row_count + 16, piece), jnp.bfloat16),
+            jax.ShapeDtypeStruct(near.shape, jnp.float32),
+        ],
         compiler_params=pltpu.CompilerParams(vmem_limit_bytes=LIMIT),
         name="reduce",
-    )(diag, pieces)
+    )(near, far, pieces)
 
 
 def product_kernel(coupling, total_rows, full, cols, rows, diag_grad, mine, sent, sums):
@@ -244,29 +290,35 @@
     row_count, _ = view_a.shape
     batch_total = row_count * lax.axis_size(ROWS)
     feats = lax.axis_size(FEAT)
-    both, moments = start(view_a, view_b)
-    gathered = lax.all_gather(both, ("z", "c"))
-    other = lax.ppermute(both, "yh", SWAP)
-
-    moments = batch_sum(moments)
-    mean = moments[:2] / batch_total
-    rstd = lax.rsqrt(moments[2:] / batch_total - mean * mean + eps_var)
-
-    own_a = standardize(view_a, mean[0], rstd[0]).astype(jnp.float32)
-    own_b = standardize(view_b, mean[1], rstd[1]).astype(jnp.float32)
-    corr_diag = batch_sum(jnp.sum(own_a * own_b, 0)[None]) / batch_total
-    diag_part = jnp.sum((1.0 - corr_diag) ** 2) - redund_weight * jnp.sum(corr_diag * corr_diag)
-    diag_grad = -2.0 * (1.0 - corr_diag) - 2.0 * redund_weight * corr_diag
-    diag_share = (diag_part / lax.axis_size(ROWS)).reshape(1, 1)
-
-    cols, rows, parts = gram_parts(mean, rstd, gathered, both, other, feats)
+    both, sums = start(view_a, view_b)
+
+    right = left = both
+    blocks = [[both]]
+    other = partner(both, "yh")
+    opposite = shift(sums, lax.axis_size("z") // 2)
+    for _ in range(lax.axis_size("z") // 2 - 1):
+        right, left = shift(right, 1), shift(left, -1)
+        blocks += [[right], [left]]
+        sums = add_moments(sums, (right, left), opposite if len(blocks) == 7 else None)
+    blocks.append([shift(right[:1], 1), shift(left[1:], -1)])
+    flat = []
+    for block in blocks:
+        flat += block + [partner(half, "c") for half in block]
+    sums = sums + partner(sums, "c")
+    cols, rows, parts, cross, rstd = gram_parts(
+        sums, partner(sums, "yh"), both, other, flat, feats, batch_total
+    )
+    cross_far = partner(cross, "yh")
     pieces = lax.all_to_all(parts, FEAT, 0, 0)
-    sent = reduce_parts(pieces, diag_share, redund_weight / (batch_total * batch_total))
+    sent, diag_grad = reduce_parts(
+        cross, cross_far, pieces, batch_total, 1.0 / lax.axis_size(ROWS)
+    )
     full = lax.all_to_all(sent, FEAT, 0, 0)
     coupling = 2.0 * redund_weight / (batch_total * batch_total)
     mine, leaving, sums = products(full, cols, rows, diag_grad, coupling, batch_total)
-    sums, leaving = lax.optimization_barrier((pair_sum(sums), leaving))
-    received = lax.ppermute(leaving, "yh", SWAP)
+    sums = sums + partner(sums, "c")
+    sums, leaving = lax.optimization_barrier((sums + partner(sums, "yh"), leaving))
+    received = partner(leaving, "yh")
     back = spread(sums)
     scale = batch_total * batch_total / (redund_weight * WIDTH)
     grad_a, grad_b, loss = finish(back, rstd, mine, received, rows, scale, batch_total)

time: 185 us -> 173 us (0.935)
  between operations: 15.4 us -> 0.77 us
  starting transfers between devices: 36 us -> 50.5 us
  waiting for transfers between devices: 65.4 us -> 57.4 us
  local copies, waits for them, and re-layouts: 7.82 us -> 9.98 us
  Pallas kernels: 11.1 us -> 9.04 us
  other arithmetic: 1.91 us -> 0.01 us
    ppermute x8 -> x25, waiting for transfers between devices: 8.19 us -> 38.5 us  [the longest x9 28.4 us: shift(): lax.ppermute(values, 'z', [(k, (k + steps) % count) for k in range(count)])]
    all_gather x1 -> x0, waiting for transfers between devices: 25.9 us -> none  [shards(): gathered = lax.all_gather(both, ('z', 'c'))]
    ppermute x8 -> x25, starting transfers between devices: 21.2 us -> 45.5 us  [the longest x16 28.3 us: partner(): return lax.ppermute(values, axis, SWAP)]
    all_to_all x2 -> x0, starting transfers between devices: 9.79 us -> none  [spread(): lax.all_to_all(jnp.broadcast_to(values[None], (count,) + values.shape), '...]
    all_to_all x1, waiting for transfers between devices: 25.2 us -> 18.9 us  [shards(): pieces = lax.all_to_all(parts, FEAT, 0, 0)]
    all_to_all x2 -> x0, waiting for transfers between devices: 6.16 us -> none  [spread(): lax.all_to_all(jnp.broadcast_to(values[None], (count,) + values.shape), '...]
    unnamed x10, local copies, waits for them, and re-layouts: 6.49 us -> 9.93 us
    all_to_all x1, blocking collectives: 33.5 us -> 30.9 us  [shards(): full = lax.all_to_all(sent, FEAT, 0, 0)]
  transfers between devices with their start and end apart: 12 -> 26, of which waited for: 9 -> 11; matrix products, arithmetic and copies ran while one was open for 2% -> 0% of each run, Pallas kernels for 3% -> 0%
where the time goes in v4:
time: 173 us; the launch traced here: 172 us
  waiting for transfers between devices  57.4 us (33%)
  starting transfers between devices  50.5 us (29%)
  blocking collectives  43.9 us (25%)
  local copies, waits for them, and re-layouts  9.98 us (6%)
  Pallas kernels  9.04 us (5%)
    all_to_all x1, blocking collectives, shards(): full = lax.all_to_all(sent, FEAT, 0, 0)  30.9 us
    ppermute x9, waiting for transfers between devices, shift(): lax.ppermute(values, 'z', [(k, (k + steps) % count) for k in range(count)])  28.4 us
    ppermute x16, starting transfers between devices, partner(): return lax.ppermute(values, axis, SWAP)  28.3 us
    all_to_all x1, waiting for transfers between devices, shards(): pieces = lax.all_to_all(parts, FEAT, 0, 0)  18.9 us
    ppermute x9, starting transfers between devices, shift(): lax.ppermute(values, 'z', [(k, (k + steps) % count) for k in range(count)])  17.1 us
    all_to_all x1, blocking collectives, spread(): lax.all_to_all(jnp.broadcast_to(values[None], (count,) + values.shape), '...  13.1 us
    ppermute x16, waiting for transfers between devices, partner(): return lax.ppermute(values, axis, SWAP)  10.1 us
    unnamed x10, local copies, waits for them, and re-layouts  9.93 us
  transfers between devices with their start and end apart: 26, of which 11 were waited for; matrix products, arithmetic and copies ran while one was open for 0% of the time, Pallas kernels for 0%

profile of v4, /device:TPU:1, one launch (start us, length us, event | category | flops | bytes accessed | tf_op | source)
XLA Modules:
  0.0 171.6 jit_solution(8389843834912431952)
XLA Ops:
  0.6 0.9 copy-done.3
  1.6 0.9 copy-done.4
  2.5 0.1 start.1
  2.7 6.5 %collective-permute-start.1 = (bf16[2,128,1024]{2,1,0:T(8,128)(2,1)S(1)}, bf16[2,128,1024]{2,1,0:T(8,128)(2,1)S(1)}, u32[]{:S(2)}, u32[]{:S(2)}) collective-permute-start(bf16[2,128,1024]{2,1,0:T(8,128)(2,1)S(1)} %get-tuple-element.21.refs_2_.refs_4_), channel_id=1, source_target_pairs={{0,224},{32,0},{64,32},{96,64},{128,96},{160,128},{192,160},{224,1... | collective-permute-start | bytes 1572872 | tf_op jit(solution)/shard_map/ppermute | solution.py:27
  9.1 0.0 collective-permute-start
  9.2 10.6 %collective-permute-done.1.refs_2_.refs_8_ = bf16[2,128,1024]{2,1,0:T(8,128)(2,1)S(1)} collective-permute-done((bf16[2,128,1024]{2,1,0:T(8,128)(2,1)S(1)}, bf16[2,128,1024]{2,1,0:T(8,128)(2,1)S(1)}, u32[]{:S(2)}, u32[]{:S(2)}) %collective-permute-start.1) | collective-permute-done | bytes 524320 | tf_op jit(solution)/shard_map/ppermute | solution.py:27
  19.7 3.4 %collective-permute-start.3 = (bf16[2,128,1024]{2,1,0:T(8,128)(2,1)S(1)}, bf16[2,128,1024]{2,1,0:T(8,128)(2,1)S(1)}, u32[]{:S(2)}, u32[]{:S(2)}) collective-permute-start(bf16[2,128,1024]{2,1,0:T(8,128)(2,1)S(1)} %collective-permute-done.1.refs_2_.refs_8_), channel_id=1, source_target_pairs={{0,224},{32,0},{64,32},{96,64},{128,96},{160,128},{192,160},{224,1... | collective-permute-start | bytes 1572872 | tf_op jit(solution)/shard_map/ppermute | solution.py:27
  23.2 0.0 collective-permute-done.refs_1_.refs_6_
  23.2 0.0 collective-permute-start.2
  23.2 1.8 %collective-permute-start.10 = (bf16[2,128,1024]{2,1,0:T(8,128)(2,1)S(1)}, bf16[2,128,1024]{2,1,0:T(8,128)(2,1)S(1)}, u32[]{:S(2)}, u32[]{:S(2)}) collective-permute-start(bf16[2,128,1024]{2,1,0:T(8,128)(2,1)S(1)} %get-tuple-element.21.refs_2_.refs_4_), channel_id=1, source_target_pairs={{0,8},{8,0},{1,9},{9,1},{2,10},{10,2},{3,11},{11,3},{4,12},{12,4},... | collective-permute-start | bytes 1572872 | tf_op jit(solution)/shard_map/ppermute | solution.py:22
  25.0 7.8 %collective-permute-done.3.refs_2_.refs_12_ = bf16[2,128,1024]{2,1,0:T(8,128)(2,1)S(1)} collective-permute-done((bf16[2,128,1024]{2,1,0:T(8,128)(2,1)S(1)}, bf16[2,128,1024]{2,1,0:T(8,128)(2,1)S(1)}, u32[]{:S(2)}, u32[]{:S(2)}) %collective-permute-start.3) | collective-permute-done | bytes 524320 | tf_op jit(solution)/shard_map/ppermute | solution.py:27
  32.8 3.4 %collective-permute-start.6 = (bf16[2,128,1024]{2,1,0:T(8,128)(2,1)S(1)}, bf16[2,128,1024]{2,1,0:T(8,128)(2,1)S(1)}, u32[]{:S(2)}, u32[]{:S(2)}) collective-permute-start(bf16[2,128,1024]{2,1,0:T(8,128)(2,1)S(1)} %collective-permute-done.3.refs_2_.refs_12_), channel_id=1, source_target_pairs={{0,224},{32,0},{64,32},{96,64},{128,96},{160,128},{192,160},{224,1... | collective-permute-start | bytes 1572872 | tf_op jit(solution)/shard_map/ppermute | solution.py:27
  36.2 1.7 %collective-permute-start.4 = (f32[4,1024]{1,0:T(4,128)S(1)}, f32[4,1024]{1,0:T(4,128)S(1)}, u32[]{:S(2)}, u32[]{:S(2)}) collective-permute-start(f32[4,1024]{1,0:T(4,128)S(1)} %get-tuple-element.20.refs_0_), channel_id=1, source_target_pairs={{0,128},{32,160},{64,192},{96,224},{128,0},{160,32},{192,64},{224,... | collective-permute-start | bytes 49160 | tf_op jit(solution)/shard_map/ppermute | solution.py:27
  38.0 0.0 collective-permute-done.2.refs_1_.refs_10_
  38.0 0.0 collective-permute-start.5
  38.0 2.9 %collective-permute-start.9 = (bf16[2,128,1024]{2,1,0:T(8,128)(2,1)S(1)}, bf16[2,128,1024]{2,1,0:T(8,128)(2,1)S(1)}, u32[]{:S(2)}, u32[]{:S(2)}) collective-permute-start(bf16[2,128,1024]{2,1,0:T(8,128)(2,1)S(1)} %get-tuple-element.21.refs_2_.refs_4_), channel_id=1, source_target_pairs={{0,16},{16,0},{1,17},{17,1},{2,18},{18,2},{3,19},{19,3},{4,20},{20... | collective-permute-start | bytes 1572872 | tf_op jit(solution)/shard_map/ppermute | solution.py:22
  40.9 2.0 %collective-permute-done.4.refs_1_ = f32[4,1024]{1,0:T(4,128)S(1)} collective-permute-done((f32[4,1024]{1,0:T(4,128)S(1)}, f32[4,1024]{1,0:T(4,128)S(1)}, u32[]{:S(2)}, u32[]{:S(2)}) %collective-permute-start.4) | collective-permute-done | bytes 16416 | tf_op jit(solution)/shard_map/ppermute | solution.py:27
  42.9 4.0 %collective-permute-start.12 = (bf16[2,128,1024]{2,1,0:T(8,128)(2,1)S(1)}, bf16[2,128,1024]{2,1,0:T(8,128)(2,1)S(1)}, u32[]{:S(2)}, u32[]{:S(2)}) collective-permute-start(bf16[2,128,1024]{2,1,0:T(8,128)(2,1)S(1)} %collective-permute-done.1.refs_2_.refs_8_), channel_id=1, source_target_pairs={{0,8},{8,0},{1,9},{9,1},{2,10},{10,2},{3,11},{11,3},{4,12},{12,4},... | collective-permute-start | bytes 1572872 | tf_op jit(solution)/shard_map/ppermute | solution.py:22
  46.9 0.0 collective-permute-done.10.refs_5_
  46.9 0.0 collective-permute-start.11
  46.9 0.0 collective-permute-done.6.refs_3_.refs_16_
  46.9 2.2 %collective-permute-start.14 = (bf16[2,128,1024]{2,1,0:T(8,128)(2,1)S(1)}, bf16[2,128,1024]{2,1,0:T(8,128)(2,1)S(1)}, u32[]{:S(2)}, u32[]{:S(2)}) collective-permute-start(bf16[2,128,1024]{2,1,0:T(8,128)(2,1)S(1)} %collective-permute-done.3.refs_2_.refs_12_), channel_id=1, source_target_pairs={{0,8},{8,0},{1,9},{9,1},{2,10},{10,2},{3,11},{11,3},{4,12},{12,4},... | collective-permute-start | bytes 1572872 | tf_op jit(solution)/shard_map/ppermute | solution.py:22
  49.1 0.3 moments.3.refs_0_
  49.4 1.0 collective-permute-done.5.refs_2_.refs_14_
  50.3 3.6 %collective-permute-start.13 = (bf16[2,128,1024]{2,1,0:T(8,128)(2,1)S(1)}, bf16[2,128,1024]{2,1,0:T(8,128)(2,1)S(1)}, u32[]{:S(2)}, u32[]{:S(2)}) collective-permute-start(bf16[2,128,1024]{2,1,0:T(8,128)(2,1)S(1)} %collective-permute-done.2.refs_1_.refs_10_), channel_id=1, source_target_pairs={{0,8},{8,0},{1,9},{9,1},{2,10},{10,2},{3,11},{11,3},{4,12},{12,4},... | collective-permute-start | bytes 1572872 | tf_op jit(solution)/shard_map/ppermute | solution.py:22
  53.9 0.3 moments.4.refs_0_
  54.1 0.3 moments.5
  54.4 0.0 collective-permute-done.9.refs_3_
  54.4 0.1 collective-permute-start.7
  54.6 0.0 collective-permute-done.12.refs_9_
  54.6 2.1 %collective-permute-start.18 = (bf16[1,128,1024]{2,1,0:T(8,128)(2,1)S(1)}, bf16[1,128,1024]{2,1,0:T(8,128)(2,1)S(1)}, u32[]{:S(2)}, u32[]{:S(2)}) collective-permute-start(bf16[1,128,1024]{2,1,0:T(8,128)(2,1)S(1)} %slice.13), channel_id=1, source_target_pairs={{0,224},{32,0},{64,32},{96,64},{128,96},{160,128},{192,160},{224,1... | collective-permute-start | bytes 786440 | tf_op jit(solution)/shard_map/ppermute | solution.py:27
  56.6 0.0 collective-permute-done.11.refs_7_
  56.7 0.5 collective-permute-start.16
  57.2 0.0 collective-permute-done.7
  57.2 0.3 collective-permute-start.15
  57.5 4.9 %collective-permute-done.18.refs_19_ = bf16[1,128,1024]{2,1,0:T(8,128)(2,1)S(1)} collective-permute-done((bf16[1,128,1024]{2,1,0:T(8,128)(2,1)S(1)}, bf16[1,128,1024]{2,1,0:T(8,128)(2,1)S(1)}, u32[]{:S(2)}, u32[]{:S(2)}) %collective-permute-start.18) | collective-permute-done | bytes 262176 | tf_op jit(solution)/shard_map/ppermute | solution.py:27
  62.4 1.0 collective-permute-start.20
  63.4 2.1 %collective-permute-done.17.refs_18_ = bf16[1,128,1024]{2,1,0:T(8,128)(2,1)S(1)} collective-permute-done((bf16[1,128,1024]{2,1,0:T(8,128)(2,1)S(1)}, bf16[1,128,1024]{2,1,0:T(8,128)(2,1)S(1)}, u32[]{:S(2)}, u32[]{:S(2)}) %collective-permute-start.17) | collective-permute-done | bytes 262176 | tf_op jit(solution)/shard_map/ppermute | solution.py:27
  65.5 1.1 collective-permute-start.19
  66.6 0.0 collective-permute-done.13.refs_11_
  66.6 3.0 %collective-permute-start.8 = (f32[4,1024]{1,0:T(4,128)S(1)}, f32[4,1024]{1,0:T(4,128)S(1)}, u32[]{:S(2)}, u32[]{:S(2)}) collective-permute-start(f32[4,1024]{1,0:T(4,128)S(1)} %add.9.refs_0_), channel_id=1, source_target_pairs={{0,16},{16,0},{1,17},{17,1},{2,18},{18,2},{3,19},{19,3},{4,20},{20... | collective-permute-start | bytes 49160 | tf_op jit(solution)/shard_map/ppermute | solution.py:22
  69.6 1.2 collective-permute-done.8.refs_1_
  70.8 0.0 collective-permute-done.20.refs_21_
  70.8 0.0 collective-permute-done.19.refs_20_
  70.8 0.0 collective-permute-done.16.refs_17_
  70.8 0.0 collective-permute-done.15.refs_15_
  70.8 3.9 %gram.1 = (bf16[2,2048,1024]{2,1,0:T(8,128)(2,1)S(1)}, bf16[2,256,1024]{2,1,0:T(8,128)(2,1)S(1)}, bf16[8,2,256,256]{3,2,1,0:T(8,128)(2,1)S(1)}, f32[1,1024]{1,0:T(1,128)S(1)}, f32[2,1024]{1,0:T(2,128)S(1)}) custom-call(f32[4,1024]{1,0:T(4,128)S(1)} %add.9.refs_0_, f32[4,1024]{1,0:T(4,128)S(1)} %collective-permute-done.8.refs_1_, ...), custom_call_target="tpu_custom_call" | custom-call | tf_op jit(solution)/shard_map/gram/pallas_call | solution.py:136
  74.7 3.3 %copy-done = bf16[2,2048,1024]{2,1,0:T(8,128)(2,1)} copy-done((bf16[2,2048,1024]{2,1,0:T(8,128)(2,1)}, bf16[2,2048,1024]{2,1,0:T(8,128)(2,1)S(1)}, u32[]{:S(2)}) %copy-start) | copy-done | bytes 8388632
  78.0 1.4 copy-done.2
  79.4 5.0 %all-to-all-start = ((bf16[8,2,256,256]{3,2,1,0:T(8,128)(2,1)}), bf16[8,2,256,256]{3,2,1,0:T(8,128)(2,1)S(1)}, u32[]{:S(2)}, u32[]{:S(2)}) async-start(bf16[8,2,256,256]{3,2,1,0:T(8,128)(2,1)} %copy-done.2), calls=%async_computation | async-start | bytes 4194304 | tf_op jit(solution)/shard_map/all_to_all | solution.py:312
  84.4 2.6 %collective-permute-start.21 = (f32[1,1024]{1,0:T(1,128)S(1)}, f32[1,1024]{1,0:T(1,128)S(1)}, u32[]{:S(2)}, u32[]{:S(2)}) collective-permute-start(f32[1,1024]{1,0:T(1,128)S(1)} %get-tuple-element.22.refs_0_), channel_id=1, source_target_pairs={{0,16},{16,0},{1,17},{17,1},{2,18},{18,2},{3,19},{19,3},{4,20},{20... | collective-permute-start | bytes 12296 | tf_op jit(solution)/shard_map/ppermute | solution.py:22
  87.1 5.5 %collective-permute-done.21.refs_1_ = f32[1,1024]{1,0:T(1,128)S(1)} collective-permute-done((f32[1,1024]{1,0:T(1,128)S(1)}, f32[1,1024]{1,0:T(1,128)S(1)}, u32[]{:S(2)}, u32[]{:S(2)}) %collective-permute-start.21) | collective-permute-done | bytes 4128 | tf_op jit(solution)/shard_map/ppermute | solution.py:22
  92.5 18.9 %all-to-all-done.refs_2_ = bf16[8,2,256,256]{3,2,1,0:T(8,128)(2,1)S(1)} async-done(((bf16[8,2,256,256]{3,2,1,0:T(8,128)(2,1)}), bf16[8,2,256,256]{3,2,1,0:T(8,128)(2,1)S(1)}, u32[]{:S(2)}, u32[]{:S(2)}) %all-to-all-start) | async-done | bytes 2097184 | tf_op jit(solution)/shard_map/all_to_all | solution.py:312
  111.5 0.5 reduce.1
  112.0 30.9 %all_to_all.15.refs_0_ = bf16[8,2,272,256]{3,2,1,0:T(8,128)(2,1)S(1)} all-to-all(bf16[8,2,272,256]{3,2,1,0:T(8,128)(2,1)S(1)} %get-tuple-element.24), channel_id=1, replica_groups=mesh['z'=8,'yh'=2,'c'=2,'yl'=2,'x'=4] {'yl','x'}, dimensions={0} | all-to-all | bytes 4456448 | tf_op jit(solution)/shard_map/all_to_all | solution.py:316
  142.9 3.4 %copy-done.1 = bf16[2,2048,1024]{2,1,0:T(8,128)(2,1)S(1)} copy-done((bf16[2,2048,1024]{2,1,0:T(8,128)(2,1)S(1)}, bf16[2,2048,1024]{2,1,0:T(8,128)(2,1)}, u32[]{:S(2)}) %copy-start.1) | copy-done | bytes 8388632
  146.3 2.7 %products.1 = (f32[2,128,1024]{2,1,0:T(8,128)S(1)}, bf16[2,128,1024]{2,1,0:T(8,128)(2,1)S(1)}, f32[40,128]{1,0:T(8,128)S(1)}) custom-call(bf16[8,2,272,256]{3,2,1,0:T(8,128)(2,1)S(1)} %all_to_all.15.refs_0_, bf16[2,2048,1024]{2,1,0:T(8,128)(2,1)S(1)} %copy-done.1, bf16[2,256,1024]{2,1,0:T(8,128)(2,1)S(1)} %get-tuple-element.26.refs_2_.refs_4_, ...), custom_call_target="tpu_custom_call" | custom-call | tf_op jit(solution)/shard_map/products/pallas_call | solution.py:235
  148.9 2.0 %collective-permute-start.22 = (f32[40,128]{1,0:T(8,128)S(1)}, f32[40,128]{1,0:T(8,128)S(1)}, u32[]{:S(2)}, u32[]{:S(2)}) collective-permute-start(f32[40,128]{1,0:T(8,128)S(1)} %get-tuple-element.28), channel_id=1, source_target_pairs={{0,8},{8,0},{1,9},{9,1},{2,10},{10,2},{3,11},{11,3},{4,12},{12,4},... | collective-permute-start | bytes 61448 | tf_op jit(solution)/shard_map/ppermute | solution.py:22
  151.0 0.8 collective-permute-done.22
  151.8 1.6 collective-permute-start.23
  153.4 2.6 %collective-permute-done.23 = f32[40,128]{1,0:T(8,128)S(1)} collective-permute-done((f32[40,128]{1,0:T(8,128)S(1)}, f32[40,128]{1,0:T(8,128)S(1)}, u32[]{:S(2)}, u32[]{:S(2)}) %collective-permute-start.23) | collective-permute-done | bytes 20512 | tf_op jit(solution)/shard_map/ppermute | solution.py:22
  156.0 1.6 collective-permute-start.24
  157.5 13.1 %all_to_all.16.refs_0_ = f32[8,40,128]{2,1,0:T(8,128)S(1)} all-to-all(f32[8,40,128]{2,1,0:T(8,128)S(1)} %broadcast_in_dim.2), channel_id=1, replica_groups=mesh['z'=8,'yh'=2,'c'=2,'yl'=2,'x'=4] {'z'}, dimensions={0} | all-to-all | bytes 327680 | tf_op jit(solution)/shard_map/all_to_all | solution.py:32
  170.6 1.0 finish.1
  (14 shorter events, 0.1 us)
Async XLA Ops:
  0.6 1.0 copy-start.3
  1.6 0.9 copy-start.4
  2.7 17.1 %collective-permute-start.1 = (bf16[2,128,1024]{2,1,0:T(8,128)(2,1)S(1)}, bf16[2,128,1024]{2,1,0:T(8,128)(2,1)S(1)}, u32[]{:S(2)}, u32[]{:S(2)}) collective-permute-start(bf16[2,128,1024]{2,1,0:T(8,128)(2,1)S(1)} %get-tuple-element.21.refs_2_.refs_4_), channel_id=1, source_target_pairs={{0,224},{32,0},{64,32},{96,64},{128,96},{160,128},{192,160},{224,1... | collective-permute-start | bytes 1572872 | tf_op jit(solution)/shard_map/ppermute | solution.py:27
  9.1 14.0 %collective-permute-start = (bf16[2,128,1024]{2,1,0:T(8,128)(2,1)S(1)}, bf16[2,128,1024]{2,1,0:T(8,128)(2,1)S(1)}, u32[]{:S(2)}, u32[]{:S(2)}) collective-permute-start(bf16[2,128,1024]{2,1,0:T(8,128)(2,1)S(1)} %get-tuple-element.21.refs_2_.refs_4_), channel_id=1, source_target_pairs={{0,32},{32,64},{64,96},{96,128},{128,160},{160,192},{192,224},{224... | collective-permute-start | bytes 1572872 | tf_op jit(solution)/shard_map/ppermute | solution.py:27
  19.7 13.1 %collective-permute-start.3 = (bf16[2,128,1024]{2,1,0:T(8,128)(2,1)S(1)}, bf16[2,128,1024]{2,1,0:T(8,128)(2,1)S(1)}, u32[]{:S(2)}, u32[]{:S(2)}) collective-permute-start(bf16[2,128,1024]{2,1,0:T(8,128)(2,1)S(1)} %collective-permute-done.1.refs_2_.refs_8_), channel_id=1, source_target_pairs={{0,224},{32,0},{64,32},{96,64},{128,96},{160,128},{192,160},{224,1... | collective-permute-start | bytes 1572872 | tf_op jit(solution)/shard_map/ppermute | solution.py:27
  23.2 14.8 %collective-permute-start.2 = (bf16[2,128,1024]{2,1,0:T(8,128)(2,1)S(1)}, bf16[2,128,1024]{2,1,0:T(8,128)(2,1)S(1)}, u32[]{:S(2)}, u32[]{:S(2)}) collective-permute-start(bf16[2,128,1024]{2,1,0:T(8,128)(2,1)S(1)} %collective-permute-done.refs_1_.refs_6_), channel_id=1, source_target_pairs={{0,32},{32,64},{64,96},{96,128},{128,160},{160,192},{192,224},{224... | collective-permute-start | bytes 1572872 | tf_op jit(solution)/shard_map/ppermute | solution.py:27
  23.2 23.7 %collective-permute-start.10 = (bf16[2,128,1024]{2,1,0:T(8,128)(2,1)S(1)}, bf16[2,128,1024]{2,1,0:T(8,128)(2,1)S(1)}, u32[]{:S(2)}, u32[]{:S(2)}) collective-permute-start(bf16[2,128,1024]{2,1,0:T(8,128)(2,1)S(1)} %get-tuple-element.21.refs_2_.refs_4_), channel_id=1, source_target_pairs={{0,8},{8,0},{1,9},{9,1},{2,10},{10,2},{3,11},{11,3},{4,12},{12,4},... | collective-permute-start | bytes 1572872 | tf_op jit(solution)/shard_map/ppermute | solution.py:22
  32.8 14.1 %collective-permute-start.6 = (bf16[2,128,1024]{2,1,0:T(8,128)(2,1)S(1)}, bf16[2,128,1024]{2,1,0:T(8,128)(2,1)S(1)}, u32[]{:S(2)}, u32[]{:S(2)}) collective-permute-start(bf16[2,128,1024]{2,1,0:T(8,128)(2,1)S(1)} %collective-permute-done.3.refs_2_.refs_12_), channel_id=1, source_target_pairs={{0,224},{32,0},{64,32},{96,64},{128,96},{160,128},{192,160},{224,1... | collective-permute-start | bytes 1572872 | tf_op jit(solution)/shard_map/ppermute | solution.py:27
  36.2 6.6 %collective-permute-start.4 = (f32[4,1024]{1,0:T(4,128)S(1)}, f32[4,1024]{1,0:T(4,128)S(1)}, u32[]{:S(2)}, u32[]{:S(2)}) collective-permute-start(f32[4,1024]{1,0:T(4,128)S(1)} %get-tuple-element.20.refs_0_), channel_id=1, source_target_pairs={{0,128},{32,160},{64,192},{96,224},{128,0},{160,32},{192,64},{224,... | collective-permute-start | bytes 49160 | tf_op jit(solution)/shard_map/ppermute | solution.py:27
  38.0 12.3 %collective-permute-start.5 = (bf16[2,128,1024]{2,1,0:T(8,128)(2,1)S(1)}, bf16[2,128,1024]{2,1,0:T(8,128)(2,1)S(1)}, u32[]{:S(2)}, u32[]{:S(2)}) collective-permute-start(bf16[2,128,1024]{2,1,0:T(8,128)(2,1)S(1)} %collective-permute-done.2.refs_1_.refs_10_), channel_id=1, source_target_pairs={{0,32},{32,64},{64,96},{96,128},{128,160},{160,192},{192,224},{224... | collective-permute-start | bytes 1572872 | tf_op jit(solution)/shard_map/ppermute | solution.py:27
  38.0 16.4 %collective-permute-start.9 = (bf16[2,128,1024]{2,1,0:T(8,128)(2,1)S(1)}, bf16[2,128,1024]{2,1,0:T(8,128)(2,1)S(1)}, u32[]{:S(2)}, u32[]{:S(2)}) collective-permute-start(bf16[2,128,1024]{2,1,0:T(8,128)(2,1)S(1)} %get-tuple-element.21.refs_2_.refs_4_), channel_id=1, source_target_pairs={{0,16},{16,0},{1,17},{17,1},{2,18},{18,2},{3,19},{19,3},{4,20},{20... | collective-permute-start | bytes 1572872 | tf_op jit(solution)/shard_map/ppermute | solution.py:22
  42.9 11.7 %collective-permute-start.12 = (bf16[2,128,1024]{2,1,0:T(8,128)(2,1)S(1)}, bf16[2,128,1024]{2,1,0:T(8,128)(2,1)S(1)}, u32[]{:S(2)}, u32[]{:S(2)}) collective-permute-start(bf16[2,128,1024]{2,1,0:T(8,128)(2,1)S(1)} %collective-permute-done.1.refs_2_.refs_8_), channel_id=1, source_target_pairs={{0,8},{8,0},{1,9},{9,1},{2,10},{10,2},{3,11},{11,3},{4,12},{12,4},... | collective-permute-start | bytes 1572872 | tf_op jit(solution)/shard_map/ppermute | solution.py:22
  46.9 9.8 %collective-permute-start.11 = (bf16[2,128,1024]{2,1,0:T(8,128)(2,1)S(1)}, bf16[2,128,1024]{2,1,0:T(8,128)(2,1)S(1)}, u32[]{:S(2)}, u32[]{:S(2)}) collective-permute-start(bf16[2,128,1024]{2,1,0:T(8,128)(2,1)S(1)} %collective-permute-done.refs_1_.refs_6_), channel_id=1, source_target_pairs={{0,8},{8,0},{1,9},{9,1},{2,10},{10,2},{3,11},{11,3},{4,12},{12,4},... | collective-permute-start | bytes 1572872 | tf_op jit(solution)/shard_map/ppermute | solution.py:22
  46.9 9.8 %collective-permute-start.14 = (bf16[2,128,1024]{2,1,0:T(8,128)(2,1)S(1)}, bf16[2,128,1024]{2,1,0:T(8,128)(2,1)S(1)}, u32[]{:S(2)}, u32[]{:S(2)}) collective-permute-start(bf16[2,128,1024]{2,1,0:T(8,128)(2,1)S(1)} %collective-permute-done.3.refs_2_.refs_12_), channel_id=1, source_target_pairs={{0,8},{8,0},{1,9},{9,1},{2,10},{10,2},{3,11},{11,3},{4,12},{12,4},... | collective-permute-start | bytes 1572872 | tf_op jit(solution)/shard_map/ppermute | solution.py:22
  50.3 16.3 %collective-permute-start.13 = (bf16[2,128,1024]{2,1,0:T(8,128)(2,1)S(1)}, bf16[2,128,1024]{2,1,0:T(8,128)(2,1)S(1)}, u32[]{:S(2)}, u32[]{:S(2)}) collective-permute-start(bf16[2,128,1024]{2,1,0:T(8,128)(2,1)S(1)} %collective-permute-done.2.refs_1_.refs_10_), channel_id=1, source_target_pairs={{0,8},{8,0},{1,9},{9,1},{2,10},{10,2},{3,11},{11,3},{4,12},{12,4},... | collective-permute-start | bytes 1572872 | tf_op jit(solution)/shard_map/ppermute | solution.py:22
  54.4 2.8 %collective-permute-start.7 = (f32[4,1024]{1,0:T(4,128)S(1)}, f32[4,1024]{1,0:T(4,128)S(1)}, u32[]{:S(2)}, u32[]{:S(2)}) collective-permute-start(f32[4,1024]{1,0:T(4,128)S(1)} %moments.5), channel_id=1, source_target_pairs={{0,8},{8,0},{1,9},{9,1},{2,10},{10,2},{3,11},{11,3},{4,12},{12,4},... | collective-permute-start | bytes 49160 | tf_op jit(solution)/shard_map/ppermute | solution.py:22
  54.6 7.8 %collective-permute-start.18 = (bf16[1,128,1024]{2,1,0:T(8,128)(2,1)S(1)}, bf16[1,128,1024]{2,1,0:T(8,128)(2,1)S(1)}, u32[]{:S(2)}, u32[]{:S(2)}) collective-permute-start(bf16[1,128,1024]{2,1,0:T(8,128)(2,1)S(1)} %slice.13), channel_id=1, source_target_pairs={{0,224},{32,0},{64,32},{96,64},{128,96},{160,128},{192,160},{224,1... | collective-permute-start | bytes 786440 | tf_op jit(solution)/shard_map/ppermute | solution.py:27
  56.6 8.8 %collective-permute-start.17 = (bf16[1,128,1024]{2,1,0:T(8,128)(2,1)S(1)}, bf16[1,128,1024]{2,1,0:T(8,128)(2,1)S(1)}, u32[]{:S(2)}, u32[]{:S(2)}) collective-permute-start(bf16[1,128,1024]{2,1,0:T(8,128)(2,1)S(1)} %slice.12), channel_id=1, source_target_pairs={{0,32},{32,64},{64,96},{96,128},{128,160},{160,192},{192,224},{224... | collective-permute-start | bytes 786440 | tf_op jit(solution)/shard_map/ppermute | solution.py:27
  56.7 14.1 %collective-permute-start.16 = (bf16[2,128,1024]{2,1,0:T(8,128)(2,1)S(1)}, bf16[2,128,1024]{2,1,0:T(8,128)(2,1)S(1)}, u32[]{:S(2)}, u32[]{:S(2)}) collective-permute-start(bf16[2,128,1024]{2,1,0:T(8,128)(2,1)S(1)} %collective-permute-done.6.refs_3_.refs_16_), channel_id=1, source_target_pairs={{0,8},{8,0},{1,9},{9,1},{2,10},{10,2},{3,11},{11,3},{4,12},{12,4},... | collective-permute-start | bytes 1572872 | tf_op jit(solution)/shard_map/ppermute | solution.py:22
  57.2 13.6 %collective-permute-start.15 = (bf16[2,128,1024]{2,1,0:T(8,128)(2,1)S(1)}, bf16[2,128,1024]{2,1,0:T(8,128)(2,1)S(1)}, u32[]{:S(2)}, u32[]{:S(2)}) collective-permute-start(bf16[2,128,1024]{2,1,0:T(8,128)(2,1)S(1)} %collective-permute-done.5.refs_2_.refs_14_), channel_id=1, source_target_pairs={{0,8},{8,0},{1,9},{9,1},{2,10},{10,2},{3,11},{11,3},{4,12},{12,4},... | collective-permute-start | bytes 1572872 | tf_op jit(solution)/shard_map/ppermute | solution.py:22
  62.4 8.4 %collective-permute-start.20 = (bf16[1,128,1024]{2,1,0:T(8,128)(2,1)S(1)}, bf16[1,128,1024]{2,1,0:T(8,128)(2,1)S(1)}, u32[]{:S(2)}, u32[]{:S(2)}) collective-permute-start(bf16[1,128,1024]{2,1,0:T(8,128)(2,1)S(1)} %collective-permute-done.18.refs_19_), channel_id=1, source_target_pairs={{0,8},{8,0},{1,9},{9,1},{2,10},{10,2},{3,11},{11,3},{4,12},{12,4},... | collective-permute-start | bytes 786440 | tf_op jit(solution)/shard_map/ppermute | solution.py:22
  65.5 5.3 %collective-permute-start.19 = (bf16[1,128,1024]{2,1,0:T(8,128)(2,1)S(1)}, bf16[1,128,1024]{2,1,0:T(8,128)(2,1)S(1)}, u32[]{:S(2)}, u32[]{:S(2)}) collective-permute-start(bf16[1,128,1024]{2,1,0:T(8,128)(2,1)S(1)} %collective-permute-done.17.refs_18_), channel_id=1, source_target_pairs={{0,8},{8,0},{1,9},{9,1},{2,10},{10,2},{3,11},{11,3},{4,12},{12,4},... | collective-permute-start | bytes 786440 | tf_op jit(solution)/shard_map/ppermute | solution.py:22
  66.6 4.2 %collective-permute-start.8 = (f32[4,1024]{1,0:T(4,128)S(1)}, f32[4,1024]{1,0:T(4,128)S(1)}, u32[]{:S(2)}, u32[]{:S(2)}) collective-permute-start(f32[4,1024]{1,0:T(4,128)S(1)} %add.9.refs_0_), channel_id=1, source_target_pairs={{0,16},{16,0},{1,17},{17,1},{2,18},{18,2},{3,19},{19,3},{4,20},{20... | collective-permute-start | bytes 49160 | tf_op jit(solution)/shard_map/ppermute | solution.py:22
  74.7 3.3 %copy-start = (bf16[2,2048,1024]{2,1,0:T(8,128)(2,1)}, bf16[2,2048,1024]{2,1,0:T(8,128)(2,1)S(1)}, u32[]{:S(2)}) copy-start(bf16[2,2048,1024]{2,1,0:T(8,128)(2,1)S(1)} %get-tuple-element.25.refs_1_) | copy-start | bytes 25165828
  78.0 1.4 copy-start.2
  79.4 32.1 %all-to-all-start = ((bf16[8,2,256,256]{3,2,1,0:T(8,128)(2,1)}), bf16[8,2,256,256]{3,2,1,0:T(8,128)(2,1)S(1)}, u32[]{:S(2)}, u32[]{:S(2)}) async-start(bf16[8,2,256,256]{3,2,1,0:T(8,128)(2,1)} %copy-done.2), calls=%async_computation | async-start | bytes 4194304 | tf_op jit(solution)/shard_map/all_to_all | solution.py:312
  84.4 8.1 %collective-permute-start.21 = (f32[1,1024]{1,0:T(1,128)S(1)}, f32[1,1024]{1,0:T(1,128)S(1)}, u32[]{:S(2)}, u32[]{:S(2)}) collective-permute-start(f32[1,1024]{1,0:T(1,128)S(1)} %get-tuple-element.22.refs_0_), channel_id=1, source_target_pairs={{0,16},{16,0},{1,17},{17,1},{2,18},{18,2},{3,19},{19,3},{4,20},{20... | collective-permute-start | bytes 12296 | tf_op jit(solution)/shard_map/ppermute | solution.py:22
  142.9 3.4 %copy-start.1 = (bf16[2,2048,1024]{2,1,0:T(8,128)(2,1)S(1)}, bf16[2,2048,1024]{2,1,0:T(8,128)(2,1)}, u32[]{:S(2)}) copy-start(bf16[2,2048,1024]{2,1,0:T(8,128)(2,1)} %copy-done) | copy-start | bytes 25165828
  148.9 2.9 %collective-permute-start.22 = (f32[40,128]{1,0:T(8,128)S(1)}, f32[40,128]{1,0:T(8,128)S(1)}, u32[]{:S(2)}, u32[]{:S(2)}) collective-permute-start(f32[40,128]{1,0:T(8,128)S(1)} %get-tuple-element.28), channel_id=1, source_target_pairs={{0,8},{8,0},{1,9},{9,1},{2,10},{10,2},{3,11},{11,3},{4,12},{12,4},... | collective-permute-start | bytes 61448 | tf_op jit(solution)/shard_map/ppermute | solution.py:22
  151.8 4.1 %collective-permute-start.23 = (f32[40,128]{1,0:T(8,128)S(1)}, f32[40,128]{1,0:T(8,128)S(1)}, u32[]{:S(2)}, u32[]{:S(2)}) collective-permute-start(f32[40,128]{1,0:T(8,128)S(1)} %add.10), channel_id=1, source_target_pairs={{0,16},{16,0},{1,17},{17,1},{2,18},{18,2},{3,19},{19,3},{4,20},{20... | collective-permute-start | bytes 61448 | tf_op jit(solution)/shard_map/ppermute | solution.py:22
  156.0 14.6 %collective-permute-start.24 = (bf16[2,128,1024]{2,1,0:T(8,128)(2,1)S(1)}, bf16[2,128,1024]{2,1,0:T(8,128)(2,1)S(1)}, u32[]{:S(2)}, u32[]{:S(2)}) collective-permute-start(bf16[2,128,1024]{2,1,0:T(8,128)(2,1)S(1)} %get-tuple-element.33), channel_id=1, source_target_pairs={{0,16},{16,0},{1,17},{17,1},{2,18},{18,2},{3,19},{19,3},{4,20},{20... | collective-permute-start | bytes 1572872 | tf_op jit(solution)/shard_map/ppermute | solution.py:22

commit v5 on v4

--- a/solution.py
+++ b/solution.py
@@ -16,6 +16,7 @@
 LIMIT = 32 * 1024 * 1024
 VMEM = pl.BlockSpec(memory_space=pltpu.VMEM)
 ANY = pl.BlockSpec(memory_space=pl.ANY)
+SMEM = pl.BlockSpec(memory_space=pltpu.SMEM)
 
 
 def partner(values, axis):
@@ -27,6 +28,20 @@
     return lax.ppermute(values, "z", [(k, (k + steps) % count) for k in range(count)])
 
 
+def quad(values):
+    return [
+        lax.ppermute(values, ("yh", "c"), [(k, k ^ step) for k in range(4)]) for step in (3, 2, 1)
+    ]
+
+
+def peers(values):
+    count = lax.axis_size(FEAT)
+    return {
+        step: lax.ppermute(value, FEAT, [(k, k ^ step) for k in range(count)])
+        for step, value in values
+    }
+
+
 def spread(values):
     count = lax.axis_size("z")
     return lax.all_to_all(jnp.broadcast_to(values[None], (count,) + values.shape), "z", 0, 0)
@@ -36,11 +51,16 @@
     return ((values.astype(jnp.float32) - mean) * rstd).astype(jnp.bfloat16)
 
 
-def start_kernel(view_a, view_b, both, moments):
-    for v, view in enumerate((view_a, view_b)):
-        values = view[...]
-        both[v] = values
-        floats = values.astype(jnp.float32)
+def start_kernel(view_a, view_b, both, moments, sems):
+    copies = [
+        pltpu.make_async_copy(view, both.at[v], sems.at[v])
+        for v, view in enumerate((view_a, view_b))
+    ]
+    for copy in copies:
+        copy.start()
+    for v, copy in enumerate(copies):
+        copy.wait()
+        floats = both[v].astype(jnp.float32)
         moments[v : v + 1] = jnp.sum(floats, 0, keepdims=True)
         moments[v + 2 : v + 3] = jnp.sum(floats * floats, 0, keepdims=True)
 
@@ -48,12 +68,13 @@
 def start(view_a, view_b):
     return pl.pallas_call(
         start_kernel,
-        in_specs=[VMEM] * 2,
+        in_specs=[ANY] * 2,
         out_specs=[VMEM] * 2,
         out_shape=[
             jax.ShapeDtypeStruct((2,) + view_a.shape, view_a.dtype),
             jax.ShapeDtypeStruct((4, view_a.shape[1]), jnp.float32),
         ],
+        scratch_shapes=[pltpu.SemaphoreType.DMA((2,))],
         compiler_params=pltpu.CompilerParams(vmem_limit_bytes=LIMIT),
         name="start",
     )(view_a, view_b)
@@ -85,81 +106,80 @@
     )(*given)
 
 
-def gram_kernel(total_rows, near, far, own, other, *refs):
-    blocks = refs[:-5]
-    cols, rows, parts, cross, rstd = refs[-5:]
+def gram_kernel(total_rows, count_parts, me, *refs):
+    sums = refs[:4]
+    own, other = refs[4:6]
+    blocks = refs[6 : -count_parts - 4]
+    parts = refs[-count_parts - 4 : -4]
+    cols, rows, cross, rstd = refs[-4:]
     count = own.shape[1]
-    feats, _, piece, _ = parts.shape
-    sums = (near[...] + far[...]) * (1.0 / total_rows)
-    mean = sums[:2]
-    scale = lax.rsqrt(sums[2:] - mean * mean + eps_var)
+    piece = cols.shape[1] // count_parts
+    moments = (sums[0][...] + sums[1][...] + sums[2][...] + sums[3][...]) * (1.0 / total_rows)
+    mean = moments[:2]
+    scale = lax.rsqrt(moments[2:] - mean * mean + eps_var)
     rstd[...] = scale
     for v in range(2):
         rows[v, :count] = standardize(own[v], mean[v : v + 1], scale[v : v + 1])
         rows[v, count:] = standardize(other[v], mean[v : v + 1], scale[v : v + 1])
     products = jnp.zeros(cross.shape, jnp.float32)
     flat = iter(blocks)
-    place = 0
-    while place < cols.shape[1]:
-        first = place
-        while place < first + 2 * piece:
-            pair = [next(flat)]
-            if pair[0].shape[0] == 1:
-                pair.append(next(flat))
-            values = [
-                standardize(pair[v if len(pair) == 2 else 0][v if len(pair) == 1 else 0],
-                            mean[v : v + 1], scale[v : v + 1])
-                for v in range(2)
-            ]
-            for v in range(2):
-                cols[v, place : place + count] = values[v]
-            products = products + jnp.sum(
-                values[0].astype(jnp.float32) * values[1].astype(jnp.float32), 0, keepdims=True
-            )
-            place += count
+    for place in range(0, cols.shape[1], count):
+        block = next(flat)
+        pair = [block.at[0], block.at[1]] if block.shape[0] == 2 else [block.at[0], next(flat).at[0]]
+        values = [
+            standardize(pair[v][...], mean[v : v + 1], scale[v : v + 1]) for v in range(2)
+        ]
+        for v in range(2):
+            cols[v, place : place + count] = values[v]
+        products = products + jnp.sum(
+            values[0].astype(jnp.float32) * values[1].astype(jnp.float32), 0, keepdims=True
+        )
+    cross[...] = products
+    for step, part in enumerate(parts):
+        first = pl.multiple_of((me[0] ^ step) * piece, piece)
         for v in range(2):
             gram = lax.dot_general(
-                cols[v, first:place],
+                cols[v, pl.ds(first, piece)],
                 rows[v],
                 (((1,), (1,)), ((), ())),
                 preferred_element_type=jnp.float32,
             )
-            parts[first // piece : place // piece, v] = gram.astype(jnp.bfloat16).reshape(
-                2, piece, 2 * count
-            )
-    cross[...] = products
-
-
-def gram_parts(near, far, own, other, blocks, feats, total_rows):
+            part[v] = gram.astype(jnp.bfloat16)
+
+
+def gram_parts(me, sums, own, other, blocks, feats, total_rows):
     _, count, width = own.shape
     panel = count * sum(block.shape[0] for block in blocks) // 2
-    return pl.pallas_call(
-        lambda *refs: gram_kernel(total_rows, *refs),
-        in_specs=[VMEM] * (4 + len(blocks)),
-        out_specs=[VMEM] * 5,
-        out_shape=[
+    out = pl.pallas_call(
+        lambda *refs: gram_kernel(total_rows, feats, *refs),
+        in_specs=[SMEM] + [VMEM] * (6 + len(blocks)),
+        out_specs=[VMEM] * (feats + 4),
+        out_shape=[jax.ShapeDtypeStruct((2, panel // feats, 2 * count), jnp.bfloat16)] * feats
+        + [
             jax.ShapeDtypeStruct((2, panel, width), jnp.bfloat16),
             jax.ShapeDtypeStruct((2, 2 * count, width), jnp.bfloat16),
-            jax.ShapeDtypeStruct((feats, 2, panel // feats, 2 * count), jnp.bfloat16),
             jax.ShapeDtypeStruct((1, width), jnp.float32),
             jax.ShapeDtypeStruct((2, width), jnp.float32),
         ],
         compiler_params=pltpu.CompilerParams(vmem_limit_bytes=LIMIT),
         name="gram",
-    )(near, far, own, other, *blocks)
-
-
-def reduce_kernel(weight, total_rows, share, near, far, pieces, sent, diag_grad):
-    feats, _, piece, row_count = pieces.shape
+    )(me, *sums, own, other, *blocks)
+    return out[:feats], *out[feats:]
+
+
+def reduce_kernel(weight, total_rows, share, near, far, *refs):
+    pieces = refs[:-2]
+    sent, diag_grad = refs[-2:]
+    _, piece, row_count = pieces[0].shape
     corr = (near[...] + far[...]) * (1.0 / total_rows)
     miss = 1.0 - corr
     diag_grad[...] = -2.0 * miss - 2.0 * redund_weight * corr
     diag = jnp.sum(miss * miss - redund_weight * (corr * corr), keepdims=True) * share
     total = []
     for v in range(2):
-        total.append(pieces[0, v].astype(jnp.float32))
-        for w in range(1, feats):
-            total[v] = total[v] + pieces[w, v].astype(jnp.float32)
+        total.append(pieces[0][v].astype(jnp.float32))
+        for other in pieces[1:]:
+            total[v] = total[v] + other[v].astype(jnp.float32)
     frob = jnp.sum(total[0] * total[1], keepdims=True)
     part = jnp.broadcast_to(diag + weight * frob, (16, piece))
     high = part.astype(jnp.bfloat16).astype(jnp.float32)
@@ -167,32 +187,31 @@
     low = part - high - middle
     lane = lax.broadcasted_iota(jnp.int32, part.shape, 1)
     extra = jnp.where(lane == 0, high, jnp.where(lane == 1, middle, jnp.where(lane == 2, low, 0.0)))
-    extra = extra.astype(jnp.bfloat16)
     for v in range(2):
-        low_gram = total[v].T.astype(jnp.bfloat16)
-        for w in range(feats):
-            sent[w, v, :row_count] = low_gram
-            sent[w, v, row_count:] = extra
+        sent[v, :row_count] = total[v].T.astype(jnp.bfloat16)
+        sent[v, row_count:] = extra.astype(jnp.bfloat16)
 
 
 def reduce_parts(near, far, pieces, total_rows, share):
-    feats, _, piece, row_count = pieces.shape
+    _, piece, row_count = pieces[0].shape
     weight = redund_weight / (total_rows * total_rows)
     return pl.pallas_call(
         lambda *refs: reduce_kernel(weight, total_rows, share, *refs),
-        in_specs=[VMEM] * 3,
+        in_specs=[VMEM] * (2 + len(pieces)),
         out_specs=[VMEM] * 2,
         out_shape=[
-            jax.ShapeDtypeStruct((feats, 2, row_count + 16, piece), jnp.bfloat16),
+            jax.ShapeDtypeStruct((2, row_count + 16, piece), jnp.bfloat16),
             jax.ShapeDtypeStruct(near.shape, jnp.float32),
         ],
         compiler_params=pltpu.CompilerParams(vmem_limit_bytes=LIMIT),
         name="reduce",
-    )(near, far, pieces)
-
-
-def product_kernel(coupling, total_rows, full, cols, rows, diag_grad, mine, sent, sums):
-    feats, _, _, piece = full.shape
+    )(near, far, *pieces)
+
+
+def product_kernel(coupling, total_rows, me, cols, rows, diag_grad, *refs):
+    full = refs[:-3]
+    mine, sent, sums = refs[-3:]
+    _, _, piece = full[0].shape
     count = rows.shape[1] // 2
     width = cols.shape[2]
     chunk = 512
@@ -200,10 +219,11 @@
         for f in range(0, width, chunk):
             here = slice(f, f + chunk)
             product = None
-            for w in range(feats):
+            for step, part in enumerate(full):
+                first = pl.multiple_of((me[0] ^ step) * piece, piece)
                 term = jnp.dot(
-                    full[w, 1 - v, : 2 * count],
-                    cols[v, w * piece : (w + 1) * piece, here],
+                    part[1 - v, : 2 * count],
+                    cols[v, pl.ds(first, piece), here],
                     preferred_element_type=jnp.float32,
                 )
                 product = term if product is None else product + term
@@ -223,18 +243,20 @@
                 sums[row : row + 1] = plain[:, k * 128 : (k + 1) * 128]
                 row += width // 128
                 sums[row : row + 1] = cross[:, k * 128 : (k + 1) * 128]
-    pieces = full[:, 0, 2 * count : 2 * count + 16, :128].astype(jnp.float32)
-    loss = jnp.sum(pieces[:, 0:1, :].reshape(feats, 128), keepdims=True)
+    loss = jnp.zeros((16, 128), jnp.float32)
+    for part in full:
+        loss = loss + part[0, 2 * count : 2 * count + 16, :128].astype(jnp.float32)
+    loss = jnp.sum(loss[:1], keepdims=True)
     last = 4 * (width // 128)
     sums[last : last + 8] = jnp.broadcast_to(loss, (8, 128))
 
 
-def products(full, cols, rows, diag_grad, coupling, total_rows):
+def products(me, full, cols, rows, diag_grad, coupling, total_rows):
     _, _, width = cols.shape
     count = rows.shape[1] // 2
     return pl.pallas_call(
         lambda *refs: product_kernel(coupling, total_rows, *refs),
-        in_specs=[VMEM] * 4,
+        in_specs=[SMEM] + [VMEM] * (3 + len(full)),
         out_specs=[VMEM] * 3,
         out_shape=[
             jax.ShapeDtypeStruct((2, count, width), jnp.float32),
@@ -243,7 +265,7 @@
         ],
         compiler_params=pltpu.CompilerParams(vmem_limit_bytes=LIMIT),
         name="products",
-    )(full, cols, rows, diag_grad)
+    )(me, cols, rows, diag_grad, *full)
 
 
 def final_kernel(scale, total_rows, parts, rstd, mine, received, rows, grad_a, grad_b, loss):
@@ -304,20 +326,26 @@
     flat = []
     for block in blocks:
         flat += block + [partner(half, "c") for half in block]
-    sums = sums + partner(sums, "c")
-    cols, rows, parts, cross, rstd = gram_parts(
-        sums, partner(sums, "yh"), both, other, flat, feats, batch_total
+    me = lax.axis_index(FEAT).astype(jnp.int32).reshape(1)
+    parts, cols, rows, cross, rstd = gram_parts(
+        me, [sums] + quad(sums), both, other, flat, feats, batch_total
     )
+    order = [7, 6, 5, 4, 3, 2, 1][: feats - 1]
     cross_far = partner(cross, "yh")
-    pieces = lax.all_to_all(parts, FEAT, 0, 0)
+    come = peers([(step, parts[step]) for step in order])
     sent, diag_grad = reduce_parts(
-        cross, cross_far, pieces, batch_total, 1.0 / lax.axis_size(ROWS)
+        cross,
+        cross_far,
+        [parts[0]] + [come[step] for step in range(1, feats)],
+        batch_total,
+        1.0 / lax.axis_size(ROWS),
     )
-    full = lax.all_to_all(sent, FEAT, 0, 0)
+    come = peers([(step, sent) for step in order])
+    full = [sent] + [come[step] for step in range(1, feats)]
     coupling = 2.0 * redund_weight / (batch_total * batch_total)
-    mine, leaving, sums = products(full, cols, rows, diag_grad, coupling, batch_total)
-    sums = sums + partner(sums, "c")
-    sums, leaving = lax.optimization_barrier((sums + partner(sums, "yh"), leaving))
+    mine, leaving, sums = products(me, full, cols, rows, diag_grad, coupling, batch_total)
+    near = quad(sums)
+    sums, leaving = lax.optimization_barrier((sums + near[0] + near[1] + near[2], leaving))
     received = partner(leaving, "yh")
     back = spread(sums)
     scale = batch_total * batch_total / (redund_weight * WIDTH)

time: 173 us -> 187 us (1.081)
  blocking collectives: 43.9 us -> 12.9 us
  waiting for transfers between devices: 57.4 us -> 76.9 us
  starting transfers between devices: 50.5 us -> 68.5 us
  Pallas kernels: 9.04 us -> 14.4 us
  local copies, waits for them, and re-layouts: 9.98 us -> 13.2 us
    ppermute x0 -> x20, waiting for transfers between devices: none -> 49.2 us  [the longest x14 41.5 us: peers(): lax.ppermute(value, FEAT, [(k, k ^ step) for k in range(count)])]
    ppermute x0 -> x20, starting transfers between devices: none -> 30.9 us  [the longest x14 16.1 us: peers(): lax.ppermute(value, FEAT, [(k, k ^ step) for k in range(count)])]
    all_to_all x1 -> x0, blocking collectives: 30.9 us -> none  [shards(): full = lax.all_to_all(sent, FEAT, 0, 0)]
    all_to_all x1 -> x0, waiting for transfers between devices: 18.9 us -> none  [shards(): pieces = lax.all_to_all(parts, FEAT, 0, 0)]
    ppermute x16 -> x12, waiting for transfers between devices: 10.1 us -> 2.55 us  [partner(): return lax.ppermute(values, axis, SWAP)]
    ppermute x16 -> x12, starting transfers between devices: 28.3 us -> 21 us  [partner(): return lax.ppermute(values, axis, SWAP)]
    pallas_call x2, Pallas kernels: 4.07 us -> 9.48 us  [the longest x1 9.28 us: gram_parts(): pl.pallas_call(lambda *refs: gram_kernel(total_rows, feats, *refs), in_sp...]
    all_to_all x1 -> x0, starting transfers between devices: 5.03 us -> none  [shards(): pieces = lax.all_to_all(parts, FEAT, 0, 0)]
  transfers between devices with their start and end apart: 26 -> 41, of which waited for: 11 -> 17; matrix products, arithmetic and copies ran while one was open for 0% -> 0% of each run, Pallas kernels for 0% -> 0%
where the time goes in v5:
time: 187 us
  waiting for transfers between devices  76.9 us (41%)
  starting transfers between devices  68.5 us (37%)
  Pallas kernels  14.4 us (8%)
  local copies, waits for them, and re-layouts  13.2 us (7%)
  blocking collectives  12.9 us (7%)
    ppermute x14, waiting for transfers between devices, peers(): lax.ppermute(value, FEAT, [(k, k ^ step) for k in range(count)])  41.5 us
    ppermute x9, waiting for transfers between devices, shift(): lax.ppermute(values, 'z', [(k, (k + steps) % count) for k in range(count)])  25.2 us
    ppermute x12, starting transfers between devices, partner(): return lax.ppermute(values, axis, SWAP)  21 us
    ppermute x9, starting transfers between devices, shift(): lax.ppermute(values, 'z', [(k, (k + steps) % count) for k in range(count)])  16.6 us
    ppermute x14, starting transfers between devices, peers(): lax.ppermute(value, FEAT, [(k, k ^ step) for k in range(count)])  16.1 us
    ppermute x6, starting transfers between devices, quad(): lax.ppermute(values, ('yh', 'c'), [(k, k ^ step) for k in range(4)])  14.7 us
    unnamed x32, local copies, waits for them, and re-layouts  13.2 us
    all_to_all x1, blocking collectives, spread(): lax.all_to_all(jnp.broadcast_to(values[None], (count,) + values.shape), '...  12.9 us
  transfers between devices with their start and end apart: 41, of which 17 were waited for; matrix products, arithmetic and copies ran while one was open for 0% of the time, Pallas kernels for 0%

profile of v5, /device:TPU:1, one launch (start us, length us, event | category | flops | bytes accessed | tf_op | source)
XLA Modules:
  0.0 186.7 jit_solution(15977849419048939556)
XLA Ops:
  0.6 0.9 copy-done.14
  1.6 0.9 copy-done.15
  2.7 6.5 %collective-permute-start.1 = (bf16[2,128,1024]{2,1,0:T(8,128)(2,1)S(1)}, bf16[2,128,1024]{2,1,0:T(8,128)(2,1)S(1)}, u32[]{:S(2)}, u32[]{:S(2)}) collective-permute-start(bf16[2,128,1024]{2,1,0:T(8,128)(2,1)S(1)} %get-tuple-element.28.refs_5_.refs_7_), channel_id=1, source_target_pairs={{0,224},{32,0},{64,32},{96,64},{128,96},{160,128},{192,160},{224,1... | collective-permute-start | bytes 1572872 | tf_op jit(solution)/shard_map/ppermute | solution.py:28
  9.2 10.6 %collective-permute-done.1.refs_2_.refs_11_ = bf16[2,128,1024]{2,1,0:T(8,128)(2,1)S(1)} collective-permute-done((bf16[2,128,1024]{2,1,0:T(8,128)(2,1)S(1)}, bf16[2,128,1024]{2,1,0:T(8,128)(2,1)S(1)}, u32[]{:S(2)}, u32[]{:S(2)}) %collective-permute-start.1) | collective-permute-done | bytes 524320 | tf_op jit(solution)/shard_map/ppermute | solution.py:28
  19.8 3.4 %collective-permute-start.3 = (bf16[2,128,1024]{2,1,0:T(8,128)(2,1)S(1)}, bf16[2,128,1024]{2,1,0:T(8,128)(2,1)S(1)}, u32[]{:S(2)}, u32[]{:S(2)}) collective-permute-start(bf16[2,128,1024]{2,1,0:T(8,128)(2,1)S(1)} %collective-permute-done.1.refs_2_.refs_11_), channel_id=1, source_target_pairs={{0,224},{32,0},{64,32},{96,64},{128,96},{160,128},{192,160},{224,1... | collective-permute-start | bytes 1572872 | tf_op jit(solution)/shard_map/ppermute | solution.py:28
  23.2 1.8 collective-permute-start.11
  25.1 7.8 %collective-permute-done.3.refs_2_.refs_15_ = bf16[2,128,1024]{2,1,0:T(8,128)(2,1)S(1)} collective-permute-done((bf16[2,128,1024]{2,1,0:T(8,128)(2,1)S(1)}, bf16[2,128,1024]{2,1,0:T(8,128)(2,1)S(1)}, u32[]{:S(2)}, u32[]{:S(2)}) %collective-permute-start.3) | collective-permute-done | bytes 524320 | tf_op jit(solution)/shard_map/ppermute | solution.py:28
  32.9 3.4 %collective-permute-start.6 = (bf16[2,128,1024]{2,1,0:T(8,128)(2,1)S(1)}, bf16[2,128,1024]{2,1,0:T(8,128)(2,1)S(1)}, u32[]{:S(2)}, u32[]{:S(2)}) collective-permute-start(bf16[2,128,1024]{2,1,0:T(8,128)(2,1)S(1)} %collective-permute-done.3.refs_2_.refs_15_), channel_id=1, source_target_pairs={{0,224},{32,0},{64,32},{96,64},{128,96},{160,128},{192,160},{224,1... | collective-permute-start | bytes 1572872 | tf_op jit(solution)/shard_map/ppermute | solution.py:28
  36.3 1.8 collective-permute-start.4
  38.1 2.9 %collective-permute-start.10 = (bf16[2,128,1024]{2,1,0:T(8,128)(2,1)S(1)}, bf16[2,128,1024]{2,1,0:T(8,128)(2,1)S(1)}, u32[]{:S(2)}, u32[]{:S(2)}) collective-permute-start(bf16[2,128,1024]{2,1,0:T(8,128)(2,1)S(1)} %get-tuple-element.28.refs_5_.refs_7_), channel_id=1, source_target_pairs={{0,16},{16,0},{1,17},{17,1},{2,18},{18,2},{3,19},{19,3},{4,20},{20... | collective-permute-start | bytes 1572872 | tf_op jit(solution)/shard_map/ppermute | solution.py:23
  41.1 6.7 %collective-permute-done.4.refs_1_ = f32[4,1024]{1,0:T(4,128)S(1)} collective-permute-done((f32[4,1024]{1,0:T(4,128)S(1)}, f32[4,1024]{1,0:T(4,128)S(1)}, u32[]{:S(2)}, u32[]{:S(2)}) %collective-permute-start.4) | collective-permute-done | bytes 16416 | tf_op jit(solution)/shard_map/ppermute | solution.py:28
  47.8 3.7 %collective-permute-start.13 = (bf16[2,128,1024]{2,1,0:T(8,128)(2,1)S(1)}, bf16[2,128,1024]{2,1,0:T(8,128)(2,1)S(1)}, u32[]{:S(2)}, u32[]{:S(2)}) collective-permute-start(bf16[2,128,1024]{2,1,0:T(8,128)(2,1)S(1)} %collective-permute-done.1.refs_2_.refs_11_), channel_id=1, source_target_pairs={{0,8},{8,0},{1,9},{9,1},{2,10},{10,2},{3,11},{11,3},{4,12},{12,4},... | collective-permute-start | bytes 1572872 | tf_op jit(solution)/shard_map/ppermute | solution.py:23
  51.6 0.4 collective-permute-start.15
  52.0 0.6 collective-permute-start.14
  52.6 0.8 copy-done.4
  53.4 0.8 copy-done.6
  54.2 1.5 collective-permute-start.18
  55.7 0.8 copy-done.8
  56.5 2.8 %collective-permute-start.17 = (bf16[2,128,1024]{2,1,0:T(8,128)(2,1)S(1)}, bf16[2,128,1024]{2,1,0:T(8,128)(2,1)}, u32[]{:S(2)}, u32[]{:S(2)}) collective-permute-start(bf16[2,128,1024]{2,1,0:T(8,128)(2,1)S(1)} %collective-permute-done.6.refs_3_.refs_19_), channel_id=1, source_target_pairs={{0,8},{8,0},{1,9},{9,1},{2,10},{10,2},{3,11},{11,3},{4,12},{12,4},... | collective-permute-start | bytes 1572872 | tf_op jit(solution)/shard_map/ppermute | solution.py:23
  59.3 0.8 copy-done.10
  60.1 2.1 %collective-permute-start.21 = (bf16[1,128,1024]{2,1,0:T(8,128)(2,1)S(1)}, bf16[1,128,1024]{2,1,0:T(8,128)(2,1)}, u32[]{:S(2)}, u32[]{:S(2)}) collective-permute-start(bf16[1,128,1024]{2,1,0:T(8,128)(2,1)S(1)} %collective-permute-done.19.refs_22_), channel_id=1, source_target_pairs={{0,8},{8,0},{1,9},{9,1},{2,10},{10,2},{3,11},{11,3},{4,12},{12,4},... | collective-permute-start | bytes 786440 | tf_op jit(solution)/shard_map/ppermute | solution.py:23
  62.1 4.0 %collective-permute-start.20 = (bf16[1,128,1024]{2,1,0:T(8,128)(2,1)}, bf16[1,128,1024]{2,1,0:T(8,128)(2,1)}, u32[]{:S(2)}, u32[]{:S(2)}) collective-permute-start(bf16[1,128,1024]{2,1,0:T(8,128)(2,1)} %collective-permute-done.18.refs_21_), channel_id=1, source_target_pairs={{0,8},{8,0},{1,9},{9,1},{2,10},{10,2},{3,11},{11,3},{4,12},{12,4},... | collective-permute-start | bytes 786440 | tf_op jit(solution)/shard_map/ppermute | solution.py:23
  66.9 0.8 copy-done.12
  67.7 1.2 collective-permute-done.9.refs_4_
  68.9 2.9 %collective-permute-start.8 = (f32[4,1024]{1,0:T(4,128)S(1)}, f32[4,1024]{1,0:T(4,128)S(1)}, u32[]{:S(2)}, u32[]{:S(2)}) collective-permute-start(f32[4,1024]{1,0:T(4,128)S(1)} %moments.5.refs_1_), channel_id=1, source_target_pairs={{0,16},{8,24},{16,0},{24,8},{1,17},{9,25},{17,1},{25,9},{2,18},{10... | collective-permute-start | bytes 49160 | tf_op jit(solution)/shard_map/ppermute | solution.py:33
  71.8 1.2 collective-permute-done.8.refs_3_
  73.0 4.1 %collective-permute-start.7 = (f32[4,1024]{1,0:T(4,128)S(1)}, f32[4,1024]{1,0:T(4,128)S(1)}, u32[]{:S(2)}, u32[]{:S(2)}) collective-permute-start(f32[4,1024]{1,0:T(4,128)S(1)} %moments.5.refs_1_), channel_id=1, source_target_pairs={{0,24},{8,16},{16,8},{24,0},{1,25},{9,17},{17,9},{25,1},{2,26},{10... | collective-permute-start | bytes 49160 | tf_op jit(solution)/shard_map/ppermute | solution.py:33
  77.1 1.5 collective-permute-done.7.refs_2_
  78.6 1.0 copy-done.1
  79.7 1.0 copy-done.3
  80.7 1.0 copy-done.5
  81.8 1.0 copy-done.7
  82.8 1.0 copy-done.9
  83.8 1.0 copy-done.11
  84.9 1.0 copy-done.13
  85.9 9.3 %gram.1 = (bf16[2,256,256]{2,1,0:T(8,128)(2,1)S(1)}, bf16[2,256,256]{2,1,0:T(8,128)(2,1)S(1)}, bf16[2,256,256]{2,1,0:T(8,128)(2,1)S(1)}, bf16[2,256,256]{2,1,0:T...) custom-call(s32[1]{0:T(128)} %bitcast.refs_0_, ...), custom_call_target="tpu_custom_call" | custom-call | tf_op jit(solution)/shard_map/gram/pallas_call | solution.py:153
  95.2 1.3 collective-permute-start.23
  96.5 2.5 %collective-permute-start.24 = (bf16[2,256,256]{2,1,0:T(8,128)(2,1)S(1)}, bf16[2,256,256]{2,1,0:T(8,128)(2,1)S(1)}, u32[]{:S(2)}, u32[]{:S(2)}) collective-permute-start(bf16[2,256,256]{2,1,0:T(8,128)(2,1)S(1)} %get-tuple-element.34), channel_id=1, source_target_pairs={{0,2},{1,3},{2,0},{3,1},{4,6},{5,7},{6,4},{7,5},{8,10},{9,11},{10,... | collective-permute-start | bytes 786440 | tf_op jit(solution)/shard_map/ppermute | solution.py:40
  99.0 2.0 %collective-permute-start.22 = (f32[1,1024]{1,0:T(1,128)S(1)}, f32[1,1024]{1,0:T(1,128)S(1)}, u32[]{:S(2)}, u32[]{:S(2)}) collective-permute-start(f32[1,1024]{1,0:T(1,128)S(1)} %get-tuple-element.31.refs_0_), channel_id=1, source_target_pairs={{0,16},{16,0},{1,17},{17,1},{2,18},{18,2},{3,19},{19,3},{4,20},{20... | collective-permute-start | bytes 12296 | tf_op jit(solution)/shard_map/ppermute | solution.py:23
  101.5 1.4 collective-permute-done.22.refs_1_
  103.0 3.2 %collective-permute-start.28 = (bf16[2,256,256]{2,1,0:T(8,128)(2,1)S(1)}, bf16[2,256,256]{2,1,0:T(8,128)(2,1)S(1)}, u32[]{:S(2)}, u32[]{:S(2)}) collective-permute-start(bf16[2,256,256]{2,1,0:T(8,128)(2,1)S(1)} %get-tuple-element.38), channel_id=1, source_target_pairs={{0,6},{1,7},{2,4},{3,5},{4,2},{5,3},{6,0},{7,1},{8,14},{9,15},{10,... | collective-permute-start | bytes 786440 | tf_op jit(solution)/shard_map/ppermute | solution.py:40
  106.1 4.5 %collective-permute-done.24.refs_4_ = bf16[2,256,256]{2,1,0:T(8,128)(2,1)S(1)} collective-permute-done((bf16[2,256,256]{2,1,0:T(8,128)(2,1)S(1)}, bf16[2,256,256]{2,1,0:T(8,128)(2,1)S(1)}, u32[]{:S(2)}, u32[]{:S(2)}) %collective-permute-start.24) | collective-permute-done | bytes 262176 | tf_op jit(solution)/shard_map/ppermute | solution.py:40
  110.7 4.3 %collective-permute-done.25.refs_5_ = bf16[2,256,256]{2,1,0:T(8,128)(2,1)S(1)} collective-permute-done((bf16[2,256,256]{2,1,0:T(8,128)(2,1)S(1)}, bf16[2,256,256]{2,1,0:T(8,128)(2,1)S(1)}, u32[]{:S(2)}, u32[]{:S(2)}) %collective-permute-start.25) | collective-permute-done | bytes 262176 | tf_op jit(solution)/shard_map/ppermute | solution.py:40
  115.0 8.0 %collective-permute-done.28.refs_8_ = bf16[2,256,256]{2,1,0:T(8,128)(2,1)S(1)} collective-permute-done((bf16[2,256,256]{2,1,0:T(8,128)(2,1)S(1)}, bf16[2,256,256]{2,1,0:T(8,128)(2,1)S(1)}, u32[]{:S(2)}, u32[]{:S(2)}) %collective-permute-start.28) | collective-permute-done | bytes 262176 | tf_op jit(solution)/shard_map/ppermute | solution.py:40
  123.0 3.3 %collective-permute-done.29.refs_9_ = bf16[2,256,256]{2,1,0:T(8,128)(2,1)S(1)} collective-permute-done((bf16[2,256,256]{2,1,0:T(8,128)(2,1)S(1)}, bf16[2,256,256]{2,1,0:T(8,128)(2,1)S(1)}, u32[]{:S(2)}, u32[]{:S(2)}) %collective-permute-start.29) | collective-permute-done | bytes 262176 | tf_op jit(solution)/shard_map/ppermute | solution.py:40
  126.3 0.4 reduce.1
  126.8 2.1 %collective-permute-start.36 = (bf16[2,272,256]{2,1,0:T(8,128)(2,1)S(1)}, bf16[2,272,256]{2,1,0:T(8,128)(2,1)S(1)}, u32[]{:S(2)}, u32[]{:S(2)}) collective-permute-start(bf16[2,272,256]{2,1,0:T(8,128)(2,1)S(1)} %get-tuple-element.41.refs_4_), channel_id=1, source_target_pairs={{0,7},{1,6},{2,5},{3,4},{4,3},{5,2},{6,1},{7,0},{8,15},{9,14},{10,... | collective-permute-start | bytes 835592 | tf_op jit(solution)/shard_map/ppermute | solution.py:40
  129.3 2.3 %collective-permute-start.34 = (bf16[2,272,256]{2,1,0:T(8,128)(2,1)S(1)}, bf16[2,272,256]{2,1,0:T(8,128)(2,1)S(1)}, u32[]{:S(2)}, u32[]{:S(2)}) collective-permute-start(bf16[2,272,256]{2,1,0:T(8,128)(2,1)S(1)} %get-tuple-element.41.refs_4_), channel_id=1, source_target_pairs={{0,5},{1,4},{2,7},{3,6},{4,1},{5,0},{6,3},{7,2},{8,13},{9,12},{10,... | collective-permute-start | bytes 835592 | tf_op jit(solution)/shard_map/ppermute | solution.py:40
  131.6 0.6 collective-permute-start.33
  132.2 1.4 collective-permute-start.32
  133.6 11.0 %collective-permute-done.36.refs_11_ = bf16[2,272,256]{2,1,0:T(8,128)(2,1)S(1)} collective-permute-done((bf16[2,272,256]{2,1,0:T(8,128)(2,1)S(1)}, bf16[2,272,256]{2,1,0:T(8,128)(2,1)S(1)}, u32[]{:S(2)}, u32[]{:S(2)}) %collective-permute-start.36) | collective-permute-done | bytes 278560 | tf_op jit(solution)/shard_map/ppermute | solution.py:40
  144.6 1.8 collective-permute-start.30
  146.4 9.1 %collective-permute-done.33.refs_8_ = bf16[2,272,256]{2,1,0:T(8,128)(2,1)S(1)} collective-permute-done((bf16[2,272,256]{2,1,0:T(8,128)(2,1)S(1)}, bf16[2,272,256]{2,1,0:T(8,128)(2,1)S(1)}, u32[]{:S(2)}, u32[]{:S(2)}) %collective-permute-start.33) | collective-permute-done | bytes 278560 | tf_op jit(solution)/shard_map/ppermute | solution.py:40
  155.5 1.2 collective-permute-done.30.refs_5_
  156.6 2.7 %products.1 = (f32[2,128,1024]{2,1,0:T(8,128)S(1)}, bf16[2,128,1024]{2,1,0:T(8,128)(2,1)S(1)}, f32[40,128]{1,0:T(8,128)S(1)}) custom-call(s32[1]{0:T(128)} %bitcast.refs_0_, bf16[2,2048,1024]{2,1,0:T(8,128)(2,1)S(1)} %get-tuple-element.29.refs_1_, bf16[2,256,1024]{2,1,0:T(8,128)(2,1)S(1)} %get-tuple-element.30.refs_2_.refs_4_, ...), custom_call_target="tpu_custom_call" | custom-call | tf_op jit(solution)/shard_map/products/pallas_call | solution.py:257
  159.3 4.5 %collective-permute-start.39 = (f32[40,128]{1,0:T(8,128)S(1)}, f32[40,128]{1,0:T(8,128)S(1)}, u32[]{:S(2)}, u32[]{:S(2)}) collective-permute-start(f32[40,128]{1,0:T(8,128)S(1)} %get-tuple-element.42), channel_id=1, source_target_pairs={{0,8},{8,0},{16,24},{24,16},{1,9},{9,1},{17,25},{25,17},{2,10},{10... | collective-permute-start | bytes 61448 | tf_op jit(solution)/shard_map/ppermute | solution.py:33
  163.8 2.4 %collective-permute-start.38 = (f32[40,128]{1,0:T(8,128)S(1)}, f32[40,128]{1,0:T(8,128)S(1)}, u32[]{:S(2)}, u32[]{:S(2)}) collective-permute-start(f32[40,128]{1,0:T(8,128)S(1)} %get-tuple-element.42), channel_id=1, source_target_pairs={{0,16},{8,24},{16,0},{24,8},{1,17},{9,25},{17,1},{25,9},{2,18},{10... | collective-permute-start | bytes 61448 | tf_op jit(solution)/shard_map/ppermute | solution.py:33
  166.2 0.8 collective-permute-start.37
  167.0 0.9 collective-permute-done.38
  168.0 3.0 %collective-permute-done.37 = f32[40,128]{1,0:T(8,128)S(1)} collective-permute-done((f32[40,128]{1,0:T(8,128)S(1)}, f32[40,128]{1,0:T(8,128)S(1)}, u32[]{:S(2)}, u32[]{:S(2)}) %collective-permute-start.37) | collective-permute-done | bytes 20512 | tf_op jit(solution)/shard_map/ppermute | solution.py:33
  170.9 0.7 collective-permute-start.40
  171.6 12.9 %all_to_all.5.refs_0_ = f32[8,40,128]{2,1,0:T(8,128)S(1)} all-to-all(f32[8,40,128]{2,1,0:T(8,128)S(1)} %broadcast_in_dim.2), channel_id=1, replica_groups=mesh['z'=8,'yh'=2,'c'=2,'yl'=2,'x'=4] {'z'}, dimensions={0} | all-to-all | bytes 327680 | tf_op jit(solution)/shard_map/all_to_all | solution.py:47
  184.5 1.2 collective-permute-done.40.refs_3_
  185.7 1.0 finish.1
  (63 shorter events, 2.3 us)
Async XLA Ops:
  0.6 1.0 copy-start.14
  1.6 0.9 copy-start.15
  2.7 17.1 %collective-permute-start.1 = (bf16[2,128,1024]{2,1,0:T(8,128)(2,1)S(1)}, bf16[2,128,1024]{2,1,0:T(8,128)(2,1)S(1)}, u32[]{:S(2)}, u32[]{:S(2)}) collective-permute-start(bf16[2,128,1024]{2,1,0:T(8,128)(2,1)S(1)} %get-tuple-element.28.refs_5_.refs_7_), channel_id=1, source_target_pairs={{0,224},{32,0},{64,32},{96,64},{128,96},{160,128},{192,160},{224,1... | collective-permute-start | bytes 1572872 | tf_op jit(solution)/shard_map/ppermute | solution.py:28
  9.2 14.0 %collective-permute-start = (bf16[2,128,1024]{2,1,0:T(8,128)(2,1)S(1)}, bf16[2,128,1024]{2,1,0:T(8,128)(2,1)S(1)}, u32[]{:S(2)}, u32[]{:S(2)}) collective-permute-start(bf16[2,128,1024]{2,1,0:T(8,128)(2,1)S(1)} %get-tuple-element.28.refs_5_.refs_7_), channel_id=1, source_target_pairs={{0,32},{32,64},{64,96},{96,128},{128,160},{160,192},{192,224},{224... | collective-permute-start | bytes 1572872 | tf_op jit(solution)/shard_map/ppermute | solution.py:28
  19.8 13.1 %collective-permute-start.3 = (bf16[2,128,1024]{2,1,0:T(8,128)(2,1)S(1)}, bf16[2,128,1024]{2,1,0:T(8,128)(2,1)S(1)}, u32[]{:S(2)}, u32[]{:S(2)}) collective-permute-start(bf16[2,128,1024]{2,1,0:T(8,128)(2,1)S(1)} %collective-permute-done.1.refs_2_.refs_11_), channel_id=1, source_target_pairs={{0,224},{32,0},{64,32},{96,64},{128,96},{160,128},{192,160},{224,1... | collective-permute-start | bytes 1572872 | tf_op jit(solution)/shard_map/ppermute | solution.py:28
  23.2 13.1 %collective-permute-start.2 = (bf16[2,128,1024]{2,1,0:T(8,128)(2,1)S(1)}, bf16[2,128,1024]{2,1,0:T(8,128)(2,1)S(1)}, u32[]{:S(2)}, u32[]{:S(2)}) collective-permute-start(bf16[2,128,1024]{2,1,0:T(8,128)(2,1)S(1)} %collective-permute-done.refs_1_.refs_9_), channel_id=1, source_target_pairs={{0,32},{32,64},{64,96},{96,128},{128,160},{160,192},{192,224},{224... | collective-permute-start | bytes 1572872 | tf_op jit(solution)/shard_map/ppermute | solution.py:28
  23.2 28.2 %collective-permute-start.11 = (bf16[2,128,1024]{2,1,0:T(8,128)(2,1)S(1)}, bf16[2,128,1024]{2,1,0:T(8,128)(2,1)S(1)}, u32[]{:S(2)}, u32[]{:S(2)}) collective-permute-start(bf16[2,128,1024]{2,1,0:T(8,128)(2,1)S(1)} %get-tuple-element.28.refs_5_.refs_7_), channel_id=1, source_target_pairs={{0,8},{8,0},{1,9},{9,1},{2,10},{10,2},{3,11},{11,3},{4,12},{12,4},... | collective-permute-start | bytes 1572872 | tf_op jit(solution)/shard_map/ppermute | solution.py:23
  32.9 18.7 %collective-permute-start.6 = (bf16[2,128,1024]{2,1,0:T(8,128)(2,1)S(1)}, bf16[2,128,1024]{2,1,0:T(8,128)(2,1)S(1)}, u32[]{:S(2)}, u32[]{:S(2)}) collective-permute-start(bf16[2,128,1024]{2,1,0:T(8,128)(2,1)S(1)} %collective-permute-done.3.refs_2_.refs_15_), channel_id=1, source_target_pairs={{0,224},{32,0},{64,32},{96,64},{128,96},{160,128},{192,160},{224,1... | collective-permute-start | bytes 1572872 | tf_op jit(solution)/shard_map/ppermute | solution.py:28
  36.3 30.1 %copy-start = (bf16[2,128,1024]{2,1,0:T(8,128)(2,1)}, bf16[2,128,1024]{2,1,0:T(8,128)(2,1)S(1)}, u32[]{:S(2)}) copy-start(bf16[2,128,1024]{2,1,0:T(8,128)(2,1)S(1)} %collective-permute-done.2.refs_1_.refs_13_) | copy-start | bytes 1572868
  36.3 15.7 %collective-permute-start.5 = (bf16[2,128,1024]{2,1,0:T(8,128)(2,1)S(1)}, bf16[2,128,1024]{2,1,0:T(8,128)(2,1)S(1)}, u32[]{:S(2)}, u32[]{:S(2)}) collective-permute-start(bf16[2,128,1024]{2,1,0:T(8,128)(2,1)S(1)} %collective-permute-done.2.refs_1_.refs_13_), channel_id=1, source_target_pairs={{0,32},{32,64},{64,96},{96,128},{128,160},{160,192},{192,224},{224... | collective-permute-start | bytes 1572872 | tf_op jit(solution)/shard_map/ppermute | solution.py:28
  36.3 11.5 %collective-permute-start.4 = (f32[4,1024]{1,0:T(4,128)S(1)}, f32[4,1024]{1,0:T(4,128)S(1)}, u32[]{:S(2)}, u32[]{:S(2)}) collective-permute-start(f32[4,1024]{1,0:T(4,128)S(1)} %get-tuple-element.27.refs_0_), channel_id=1, source_target_pairs={{0,128},{32,160},{64,192},{96,224},{128,0},{160,32},{192,64},{224,... | collective-permute-start | bytes 49160 | tf_op jit(solution)/shard_map/ppermute | solution.py:28
  38.1 14.5 %collective-permute-start.10 = (bf16[2,128,1024]{2,1,0:T(8,128)(2,1)S(1)}, bf16[2,128,1024]{2,1,0:T(8,128)(2,1)S(1)}, u32[]{:S(2)}, u32[]{:S(2)}) collective-permute-start(bf16[2,128,1024]{2,1,0:T(8,128)(2,1)S(1)} %get-tuple-element.28.refs_5_.refs_7_), channel_id=1, source_target_pairs={{0,16},{16,0},{1,17},{17,1},{2,18},{18,2},{3,19},{19,3},{4,20},{20... | collective-permute-start | bytes 1572872 | tf_op jit(solution)/shard_map/ppermute | solution.py:23
  47.8 5.6 %collective-permute-start.13 = (bf16[2,128,1024]{2,1,0:T(8,128)(2,1)S(1)}, bf16[2,128,1024]{2,1,0:T(8,128)(2,1)S(1)}, u32[]{:S(2)}, u32[]{:S(2)}) collective-permute-start(bf16[2,128,1024]{2,1,0:T(8,128)(2,1)S(1)} %collective-permute-done.1.refs_2_.refs_11_), channel_id=1, source_target_pairs={{0,8},{8,0},{1,9},{9,1},{2,10},{10,2},{3,11},{11,3},{4,12},{12,4},... | collective-permute-start | bytes 1572872 | tf_op jit(solution)/shard_map/ppermute | solution.py:23
  51.5 7.8 %copy-start.2 = (bf16[2,128,1024]{2,1,0:T(8,128)(2,1)}, bf16[2,128,1024]{2,1,0:T(8,128)(2,1)S(1)}, u32[]{:S(2)}) copy-start(bf16[2,128,1024]{2,1,0:T(8,128)(2,1)S(1)} %collective-permute-done.11.refs_8_) | copy-start | bytes 1572868
  51.5 4.2 %collective-permute-start.12 = (bf16[2,128,1024]{2,1,0:T(8,128)(2,1)S(1)}, bf16[2,128,1024]{2,1,0:T(8,128)(2,1)S(1)}, u32[]{:S(2)}, u32[]{:S(2)}) collective-permute-start(bf16[2,128,1024]{2,1,0:T(8,128)(2,1)S(1)} %collective-permute-done.refs_1_.refs_9_), channel_id=1, source_target_pairs={{0,8},{8,0},{1,9},{9,1},{2,10},{10,2},{3,11},{11,3},{4,12},{12,4},... | collective-permute-start | bytes 1572872 | tf_op jit(solution)/shard_map/ppermute | solution.py:23
  51.6 7.7 %collective-permute-start.15 = (bf16[2,128,1024]{2,1,0:T(8,128)(2,1)S(1)}, bf16[2,128,1024]{2,1,0:T(8,128)(2,1)S(1)}, u32[]{:S(2)}, u32[]{:S(2)}) collective-permute-start(bf16[2,128,1024]{2,1,0:T(8,128)(2,1)S(1)} %collective-permute-done.3.refs_2_.refs_15_), channel_id=1, source_target_pairs={{0,8},{8,0},{1,9},{9,1},{2,10},{10,2},{3,11},{11,3},{4,12},{12,4},... | collective-permute-start | bytes 1572872 | tf_op jit(solution)/shard_map/ppermute | solution.py:23
  52.0 14.9 %collective-permute-start.14 = (bf16[2,128,1024]{2,1,0:T(8,128)(2,1)S(1)}, bf16[2,128,1024]{2,1,0:T(8,128)(2,1)S(1)}, u32[]{:S(2)}, u32[]{:S(2)}) collective-permute-start(bf16[2,128,1024]{2,1,0:T(8,128)(2,1)S(1)} %collective-permute-done.2.refs_1_.refs_13_), channel_id=1, source_target_pairs={{0,8},{8,0},{1,9},{9,1},{2,10},{10,2},{3,11},{11,3},{4,12},{12,4},... | collective-permute-start | bytes 1572872 | tf_op jit(solution)/shard_map/ppermute | solution.py:23
  52.6 0.8 copy-start.4
  53.4 6.7 %collective-permute-start.19 = (bf16[1,128,1024]{2,1,0:T(8,128)(2,1)S(1)}, bf16[1,128,1024]{2,1,0:T(8,128)(2,1)S(1)}, u32[]{:S(2)}, u32[]{:S(2)}) collective-permute-start(bf16[1,128,1024]{2,1,0:T(8,128)(2,1)S(1)} %slice.13), channel_id=1, source_target_pairs={{0,224},{32,0},{64,32},{96,64},{128,96},{160,128},{192,160},{224,1... | collective-permute-start | bytes 786440 | tf_op jit(solution)/shard_map/ppermute | solution.py:28
  53.4 0.8 copy-start.6
  54.2 7.9 %collective-permute-start.18 = (bf16[1,128,1024]{2,1,0:T(8,128)(2,1)S(1)}, bf16[1,128,1024]{2,1,0:T(8,128)(2,1)}, u32[]{:S(2)}, u32[]{:S(2)}) collective-permute-start(bf16[1,128,1024]{2,1,0:T(8,128)(2,1)S(1)} %slice.12), channel_id=1, source_target_pairs={{0,32},{32,64},{64,96},{96,128},{128,160},{160,192},{192,224},{224... | collective-permute-start | bytes 786440 | tf_op jit(solution)/shard_map/ppermute | solution.py:28
  55.7 0.8 copy-start.8
  56.5 22.1 %collective-permute-start.17 = (bf16[2,128,1024]{2,1,0:T(8,128)(2,1)S(1)}, bf16[2,128,1024]{2,1,0:T(8,128)(2,1)}, u32[]{:S(2)}, u32[]{:S(2)}) collective-permute-start(bf16[2,128,1024]{2,1,0:T(8,128)(2,1)S(1)} %collective-permute-done.6.refs_3_.refs_19_), channel_id=1, source_target_pairs={{0,8},{8,0},{1,9},{9,1},{2,10},{10,2},{3,11},{11,3},{4,12},{12,4},... | collective-permute-start | bytes 1572872 | tf_op jit(solution)/shard_map/ppermute | solution.py:23
  59.2 0.8 copy-start.10
  60.1 18.6 %collective-permute-start.16 = (bf16[2,128,1024]{2,1,0:T(8,128)(2,1)S(1)}, bf16[2,128,1024]{2,1,0:T(8,128)(2,1)}, u32[]{:S(2)}, u32[]{:S(2)}) collective-permute-start(bf16[2,128,1024]{2,1,0:T(8,128)(2,1)S(1)} %collective-permute-done.5.refs_2_.refs_17_), channel_id=1, source_target_pairs={{0,8},{8,0},{1,9},{9,1},{2,10},{10,2},{3,11},{11,3},{4,12},{12,4},... | collective-permute-start | bytes 1572872 | tf_op jit(solution)/shard_map/ppermute | solution.py:23
  60.1 18.5 %collective-permute-start.21 = (bf16[1,128,1024]{2,1,0:T(8,128)(2,1)S(1)}, bf16[1,128,1024]{2,1,0:T(8,128)(2,1)}, u32[]{:S(2)}, u32[]{:S(2)}) collective-permute-start(bf16[1,128,1024]{2,1,0:T(8,128)(2,1)S(1)} %collective-permute-done.19.refs_22_), channel_id=1, source_target_pairs={{0,8},{8,0},{1,9},{9,1},{2,10},{10,2},{3,11},{11,3},{4,12},{12,4},... | collective-permute-start | bytes 786440 | tf_op jit(solution)/shard_map/ppermute | solution.py:23
  62.1 16.5 %collective-permute-start.20 = (bf16[1,128,1024]{2,1,0:T(8,128)(2,1)}, bf16[1,128,1024]{2,1,0:T(8,128)(2,1)}, u32[]{:S(2)}, u32[]{:S(2)}) collective-permute-start(bf16[1,128,1024]{2,1,0:T(8,128)(2,1)} %collective-permute-done.18.refs_21_), channel_id=1, source_target_pairs={{0,8},{8,0},{1,9},{9,1},{2,10},{10,2},{3,11},{11,3},{4,12},{12,4},... | collective-permute-start | bytes 786440 | tf_op jit(solution)/shard_map/ppermute | solution.py:23
  66.9 0.8 copy-start.12
  67.7 1.2 collective-permute-start.9
  68.9 4.1 %collective-permute-start.8 = (f32[4,1024]{1,0:T(4,128)S(1)}, f32[4,1024]{1,0:T(4,128)S(1)}, u32[]{:S(2)}, u32[]{:S(2)}) collective-permute-start(f32[4,1024]{1,0:T(4,128)S(1)} %moments.5.refs_1_), channel_id=1, source_target_pairs={{0,16},{8,24},{16,0},{24,8},{1,17},{9,25},{17,1},{25,9},{2,18},{10... | collective-permute-start | bytes 49160 | tf_op jit(solution)/shard_map/ppermute | solution.py:33
  73.0 5.6 %collective-permute-start.7 = (f32[4,1024]{1,0:T(4,128)S(1)}, f32[4,1024]{1,0:T(4,128)S(1)}, u32[]{:S(2)}, u32[]{:S(2)}) collective-permute-start(f32[4,1024]{1,0:T(4,128)S(1)} %moments.5.refs_1_), channel_id=1, source_target_pairs={{0,24},{8,16},{16,8},{24,0},{1,25},{9,17},{17,9},{25,1},{2,26},{10... | collective-permute-start | bytes 49160 | tf_op jit(solution)/shard_map/ppermute | solution.py:33
  78.6 1.0 copy-start.1
  79.7 1.0 copy-start.3
  80.7 1.0 copy-start.5
  81.8 1.0 copy-start.7
  82.8 1.0 copy-start.9
  83.8 1.0 copy-start.11
  84.9 1.0 copy-start.13
  95.2 7.8 %collective-permute-start.23 = (bf16[2,256,256]{2,1,0:T(8,128)(2,1)S(1)}, bf16[2,256,256]{2,1,0:T(8,128)(2,1)S(1)}, u32[]{:S(2)}, u32[]{:S(2)}) collective-permute-start(bf16[2,256,256]{2,1,0:T(8,128)(2,1)S(1)} %get-tuple-element.33), channel_id=1, source_target_pairs={{0,1},{1,0},{2,3},{3,2},{4,5},{5,4},{6,7},{7,6},{8,9},{9,8},{10,11... | collective-permute-start | bytes 786440 | tf_op jit(solution)/shard_map/ppermute | solution.py:40
  96.5 14.1 %collective-permute-start.24 = (bf16[2,256,256]{2,1,0:T(8,128)(2,1)S(1)}, bf16[2,256,256]{2,1,0:T(8,128)(2,1)S(1)}, u32[]{:S(2)}, u32[]{:S(2)}) collective-permute-start(bf16[2,256,256]{2,1,0:T(8,128)(2,1)S(1)} %get-tuple-element.34), channel_id=1, source_target_pairs={{0,2},{1,3},{2,0},{3,1},{4,6},{5,7},{6,4},{7,5},{8,10},{9,11},{10,... | collective-permute-start | bytes 786440 | tf_op jit(solution)/shard_map/ppermute | solution.py:40
  99.0 4.0 %collective-permute-start.22 = (f32[1,1024]{1,0:T(1,128)S(1)}, f32[1,1024]{1,0:T(1,128)S(1)}, u32[]{:S(2)}, u32[]{:S(2)}) collective-permute-start(f32[1,1024]{1,0:T(1,128)S(1)} %get-tuple-element.31.refs_0_), channel_id=1, source_target_pairs={{0,16},{16,0},{1,17},{17,1},{2,18},{18,2},{3,19},{19,3},{4,20},{20... | collective-permute-start | bytes 12296 | tf_op jit(solution)/shard_map/ppermute | solution.py:23
  101.0 14.0 %collective-permute-start.25 = (bf16[2,256,256]{2,1,0:T(8,128)(2,1)S(1)}, bf16[2,256,256]{2,1,0:T(8,128)(2,1)S(1)}, u32[]{:S(2)}, u32[]{:S(2)}) collective-permute-start(bf16[2,256,256]{2,1,0:T(8,128)(2,1)S(1)} %get-tuple-element.35), channel_id=1, source_target_pairs={{0,3},{1,2},{2,1},{3,0},{4,7},{5,6},{6,5},{7,4},{8,11},{9,10},{10,... | collective-permute-start | bytes 786440 | tf_op jit(solution)/shard_map/ppermute | solution.py:40
  101.2 13.8 %collective-permute-start.26 = (bf16[2,256,256]{2,1,0:T(8,128)(2,1)S(1)}, bf16[2,256,256]{2,1,0:T(8,128)(2,1)S(1)}, u32[]{:S(2)}, u32[]{:S(2)}) collective-permute-start(bf16[2,256,256]{2,1,0:T(8,128)(2,1)S(1)} %get-tuple-element.36), channel_id=1, source_target_pairs={{0,4},{1,5},{2,6},{3,7},{4,0},{5,1},{6,2},{7,3},{8,12},{9,13},{10,... | collective-permute-start | bytes 786440 | tf_op jit(solution)/shard_map/ppermute | solution.py:40
  102.9 12.1 %collective-permute-start.27 = (bf16[2,256,256]{2,1,0:T(8,128)(2,1)S(1)}, bf16[2,256,256]{2,1,0:T(8,128)(2,1)S(1)}, u32[]{:S(2)}, u32[]{:S(2)}) collective-permute-start(bf16[2,256,256]{2,1,0:T(8,128)(2,1)S(1)} %get-tuple-element.37), channel_id=1, source_target_pairs={{0,5},{1,4},{2,7},{3,6},{4,1},{5,0},{6,3},{7,2},{8,13},{9,12},{10,... | collective-permute-start | bytes 786440 | tf_op jit(solution)/shard_map/ppermute | solution.py:40
  103.0 20.0 %collective-permute-start.28 = (bf16[2,256,256]{2,1,0:T(8,128)(2,1)S(1)}, bf16[2,256,256]{2,1,0:T(8,128)(2,1)S(1)}, u32[]{:S(2)}, u32[]{:S(2)}) collective-permute-start(bf16[2,256,256]{2,1,0:T(8,128)(2,1)S(1)} %get-tuple-element.38), channel_id=1, source_target_pairs={{0,6},{1,7},{2,4},{3,5},{4,2},{5,3},{6,0},{7,1},{8,14},{9,15},{10,... | collective-permute-start | bytes 786440 | tf_op jit(solution)/shard_map/ppermute | solution.py:40
  110.7 15.7 %collective-permute-start.29 = (bf16[2,256,256]{2,1,0:T(8,128)(2,1)S(1)}, bf16[2,256,256]{2,1,0:T(8,128)(2,1)S(1)}, u32[]{:S(2)}, u32[]{:S(2)}) collective-permute-start(bf16[2,256,256]{2,1,0:T(8,128)(2,1)S(1)} %get-tuple-element.39), channel_id=1, source_target_pairs={{0,7},{1,6},{2,5},{3,4},{4,3},{5,2},{6,1},{7,0},{8,15},{9,14},{10,... | collective-permute-start | bytes 786440 | tf_op jit(solution)/shard_map/ppermute | solution.py:40
  126.8 17.9 %collective-permute-start.36 = (bf16[2,272,256]{2,1,0:T(8,128)(2,1)S(1)}, bf16[2,272,256]{2,1,0:T(8,128)(2,1)S(1)}, u32[]{:S(2)}, u32[]{:S(2)}) collective-permute-start(bf16[2,272,256]{2,1,0:T(8,128)(2,1)S(1)} %get-tuple-element.41.refs_4_), channel_id=1, source_target_pairs={{0,7},{1,6},{2,5},{3,4},{4,3},{5,2},{6,1},{7,0},{8,15},{9,14},{10,... | collective-permute-start | bytes 835592 | tf_op jit(solution)/shard_map/ppermute | solution.py:40
  128.9 15.7 %collective-permute-start.35 = (bf16[2,272,256]{2,1,0:T(8,128)(2,1)S(1)}, bf16[2,272,256]{2,1,0:T(8,128)(2,1)S(1)}, u32[]{:S(2)}, u32[]{:S(2)}) collective-permute-start(bf16[2,272,256]{2,1,0:T(8,128)(2,1)S(1)} %get-tuple-element.41.refs_4_), channel_id=1, source_target_pairs={{0,6},{1,7},{2,4},{3,5},{4,2},{5,3},{6,0},{7,1},{8,14},{9,15},{10,... | collective-permute-start | bytes 835592 | tf_op jit(solution)/shard_map/ppermute | solution.py:40
  129.3 17.1 %collective-permute-start.34 = (bf16[2,272,256]{2,1,0:T(8,128)(2,1)S(1)}, bf16[2,272,256]{2,1,0:T(8,128)(2,1)S(1)}, u32[]{:S(2)}, u32[]{:S(2)}) collective-permute-start(bf16[2,272,256]{2,1,0:T(8,128)(2,1)S(1)} %get-tuple-element.41.refs_4_), channel_id=1, source_target_pairs={{0,5},{1,4},{2,7},{3,6},{4,1},{5,0},{6,3},{7,2},{8,13},{9,12},{10,... | collective-permute-start | bytes 835592 | tf_op jit(solution)/shard_map/ppermute | solution.py:40
  131.6 23.8 %collective-permute-start.33 = (bf16[2,272,256]{2,1,0:T(8,128)(2,1)S(1)}, bf16[2,272,256]{2,1,0:T(8,128)(2,1)S(1)}, u32[]{:S(2)}, u32[]{:S(2)}) collective-permute-start(bf16[2,272,256]{2,1,0:T(8,128)(2,1)S(1)} %get-tuple-element.41.refs_4_), channel_id=1, source_target_pairs={{0,4},{1,5},{2,6},{3,7},{4,0},{5,1},{6,2},{7,3},{8,12},{9,13},{10,... | collective-permute-start | bytes 835592 | tf_op jit(solution)/shard_map/ppermute | solution.py:40
  132.2 23.3 %collective-permute-start.32 = (bf16[2,272,256]{2,1,0:T(8,128)(2,1)S(1)}, bf16[2,272,256]{2,1,0:T(8,128)(2,1)S(1)}, u32[]{:S(2)}, u32[]{:S(2)}) collective-permute-start(bf16[2,272,256]{2,1,0:T(8,128)(2,1)S(1)} %get-tuple-element.41.refs_4_), channel_id=1, source_target_pairs={{0,3},{1,2},{2,1},{3,0},{4,7},{5,6},{6,5},{7,4},{8,11},{9,10},{10,... | collective-permute-start | bytes 835592 | tf_op jit(solution)/shard_map/ppermute | solution.py:40
  144.6 10.8 %collective-permute-start.31 = (bf16[2,272,256]{2,1,0:T(8,128)(2,1)S(1)}, bf16[2,272,256]{2,1,0:T(8,128)(2,1)S(1)}, u32[]{:S(2)}, u32[]{:S(2)}) collective-permute-start(bf16[2,272,256]{2,1,0:T(8,128)(2,1)S(1)} %get-tuple-element.41.refs_4_), channel_id=1, source_target_pairs={{0,2},{1,3},{2,0},{3,1},{4,6},{5,7},{6,4},{7,5},{8,10},{9,11},{10,... | collective-permute-start | bytes 835592 | tf_op jit(solution)/shard_map/ppermute | solution.py:40
  144.6 12.0 %collective-permute-start.30 = (bf16[2,272,256]{2,1,0:T(8,128)(2,1)S(1)}, bf16[2,272,256]{2,1,0:T(8,128)(2,1)S(1)}, u32[]{:S(2)}, u32[]{:S(2)}) collective-permute-start(bf16[2,272,256]{2,1,0:T(8,128)(2,1)S(1)} %get-tuple-element.41.refs_4_), channel_id=1, source_target_pairs={{0,1},{1,0},{2,3},{3,2},{4,5},{5,4},{6,7},{7,6},{8,9},{9,8},{10,11... | collective-permute-start | bytes 835592 | tf_op jit(solution)/shard_map/ppermute | solution.py:40
  159.3 7.7 %collective-permute-start.39 = (f32[40,128]{1,0:T(8,128)S(1)}, f32[40,128]{1,0:T(8,128)S(1)}, u32[]{:S(2)}, u32[]{:S(2)}) collective-permute-start(f32[40,128]{1,0:T(8,128)S(1)} %get-tuple-element.42), channel_id=1, source_target_pairs={{0,8},{8,0},{16,24},{24,16},{1,9},{9,1},{17,25},{25,17},{2,10},{10... | collective-permute-start | bytes 61448 | tf_op jit(solution)/shard_map/ppermute | solution.py:33
  163.8 4.2 %collective-permute-start.38 = (f32[40,128]{1,0:T(8,128)S(1)}, f32[40,128]{1,0:T(8,128)S(1)}, u32[]{:S(2)}, u32[]{:S(2)}) collective-permute-start(f32[40,128]{1,0:T(8,128)S(1)} %get-tuple-element.42), channel_id=1, source_target_pairs={{0,16},{8,24},{16,0},{24,8},{1,17},{9,25},{17,1},{25,9},{2,18},{10... | collective-permute-start | bytes 61448 | tf_op jit(solution)/shard_map/ppermute | solution.py:33
  166.2 4.7 %collective-permute-start.37 = (f32[40,128]{1,0:T(8,128)S(1)}, f32[40,128]{1,0:T(8,128)S(1)}, u32[]{:S(2)}, u32[]{:S(2)}) collective-permute-start(f32[40,128]{1,0:T(8,128)S(1)} %get-tuple-element.42), channel_id=1, source_target_pairs={{0,24},{8,16},{16,8},{24,0},{1,25},{9,17},{17,9},{25,1},{2,26},{10... | collective-permute-start | bytes 61448 | tf_op jit(solution)/shard_map/ppermute | solution.py:33
  170.9 14.7 %collective-permute-start.40 = (bf16[2,128,1024]{2,1,0:T(8,128)(2,1)S(1)}, bf16[2,128,1024]{2,1,0:T(8,128)(2,1)S(1)}, u32[]{:S(2)}, u32[]{:S(2)}) collective-permute-start(bf16[2,128,1024]{2,1,0:T(8,128)(2,1)S(1)} %get-tuple-element.47), channel_id=1, source_target_pairs={{0,16},{16,0},{1,17},{17,1},{2,18},{18,2},{3,19},{19,3},{4,20},{20... | collective-permute-start | bytes 1572872 | tf_op jit(solution)/shard_map/ppermute | solution.py:23
